TPU v7x, 256 devices: a whole 4x4x8 slice. The times are simulated.
256 devices in a mesh: seq: 32 (over z, y), dp: 8 (over x, core).
Axes of the slice: x: 4, y: 4, z: 8, core: 2. Of those that a mesh axis runs over, the one named last changes fastest.
Arguments:
- q_in: bfloat16 [8, 12288, 1536], P('dp', 'seq')
- k_in: bfloat16 [8, 12288, 1536], P('dp', 'seq')
- v_in: bfloat16 [8, 12288, 1536], P('dp', 'seq'), may hold values from -6 to 6
- q_gain: float32 [128], replicated, may hold values from 0.4 to 5
- k_gain: float32 [128], replicated, may hold values from 0.4 to 5
- window: int32 [8, 32, 3], P('dp', 'seq'), may hold values from -1 to 30, as said below
- grad_out: bfloat16 [8, 12288, 1536], P('dp', 'seq'), may hold values from -6 to 6
Outputs:
- attn_out: bfloat16 [8, 12288, 1536], P('dp', 'seq')
- grad_q: bfloat16 [8, 12288, 1536], P('dp', 'seq')
- grad_k: bfloat16 [8, 12288, 1536], P('dp', 'seq')
- grad_v: bfloat16 [8, 12288, 1536], P('dp', 'seq')
- grad_q_gain: float32 [128], replicated
- grad_k_gain: float32 [128], replicated
Inputs may be any that keep to these rules, and one draw needn't show every extreme that they name: `window`: entry j of tile t's list is -1 or t - 1 (j = 0), t - 2 (j = 1), t - 2 * 2 (j = 2); it is -1 where that tile lies outside the grid, and some present neighbours are left out.
All inputs are finite; a program needn't handle non-finite values.
Results may differ from a plain program's by a relative error of at most 0.0054.
The roundings to bfloat16 on the way count: a program that leaves them out, or rounds other values in their place, can miss the bound.
Values may be sent and summed in bfloat16 or wider, within the bound.
No kernel may reach another device: no remote copies, remote signals or barrier semaphores. Data moves between devices by JAX's collectives and lax.ppermute only.
A program may use at most 128 MiB of HBM per device.

v0:
```python
import jax
import jax.numpy as jnp
from jax import lax
from jax.sharding import PartitionSpec as P

HEAD_DIM = 128
GRID_W = 2
GRID_H = 2


def shifted(block, axis, distance):
    devices = range(lax.axis_size(axis))
    route = [(i - distance, i) for i in devices if i - distance in devices]
    return lax.ppermute(block, axis, route)


def normalize(rows, gain_vec):
    flat = rows.astype(jnp.float32).reshape(rows.shape[:-1] + (-1, HEAD_DIM))
    root = lax.rsqrt(jnp.mean(flat * flat, axis=-1, keepdims=True) + 1e-06)
    unit = flat * root
    return (unit * gain_vec, unit, root)


def norm_backward(grad_norm, unit, root, gain_vec):
    scaled = grad_norm * gain_vec
    inner = jnp.mean(scaled * unit, axis=-1, keepdims=True)
    return (root * (scaled - unit * inner), jnp.sum(grad_norm * unit, axis=(0, 1)))


def fetch_window(payload, step_back):
    return shifted((payload[0], payload[1]), "seq", step_back)


def return_terms(payload, step_back):
    return shifted((payload[0], payload[1]), "seq", step_back)


def heads_last(stacked):
    moved = jnp.moveaxis(stacked, 0, -2)
    return moved.reshape(moved.shape[:-2] + (moved.shape[-2] * moved.shape[-1],))


def on_device(q_in, k_in, v_in, q_gain, k_gain, window, grad_out):
    tile_rows = q_in.shape[1]
    feat_width = q_in.shape[2]
    head_count = feat_width // HEAD_DIM
    score_scale = HEAD_DIM ** (-0.5)
    offsets = (1, GRID_W, GRID_W * GRID_H)
    q_norm, q_unit, q_root = normalize(q_in[0], q_gain)
    k_norm, k_unit, k_root = normalize(k_in[0], k_gain)
    q_send = q_norm.astype(jnp.bfloat16).reshape(tile_rows, feat_width)
    k_send = k_norm.astype(jnp.bfloat16).reshape(tile_rows, feat_width)
    values = v_in[0]
    grads = grad_out[0]
    valid_dirs = window[0, 0] >= 0
    fetched = [fetch_window((k_send, values), step) for step in offsets]
    key_rows = jnp.stack([k_send] + [pair[0] for pair in fetched])
    val_rows = jnp.stack([values] + [pair[1] for pair in fetched])
    key_valid = jnp.concatenate([jnp.ones((1,), bool), valid_dirs])
    key_mask = jnp.broadcast_to(key_valid[:, None], (4, tile_rows)).reshape(4 * tile_rows)
    block_count = 4

    def one_head(head_idx):
        col_start = head_idx * HEAD_DIM
        q_head = lax.dynamic_slice_in_dim(q_send, col_start, HEAD_DIM, 1)
        k_head = lax.dynamic_slice_in_dim(key_rows, col_start, HEAD_DIM, 2).reshape(
            4 * tile_rows, HEAD_DIM
        )
        v_head = lax.dynamic_slice_in_dim(val_rows, col_start, HEAD_DIM, 2).reshape(
            4 * tile_rows, HEAD_DIM
        )
        g_head = lax.dynamic_slice_in_dim(grads, col_start, HEAD_DIM, 1)
        scores = (
            jnp.einsum("qd,kd->qk", q_head, k_head, preferred_element_type=jnp.float32)
            * score_scale
        )
        scores = jnp.where(key_mask[None, :], scores, -jnp.inf)
        row_max = jnp.max(scores, axis=-1, keepdims=True)
        weights_raw = jnp.exp(scores - row_max)
        row_sum = jnp.sum(weights_raw, axis=-1, keepdims=True)
        probs = weights_raw / row_sum
        probs_low = probs.astype(jnp.bfloat16)
        out_low = jnp.dot(probs_low, v_head, preferred_element_type=jnp.float32).astype(
            jnp.bfloat16
        )
        row_dot = jnp.sum(
            g_head.astype(jnp.float32) * out_low.astype(jnp.float32), axis=-1, keepdims=True
        )
        grad_probs = jnp.einsum("qd,kd->qk", g_head, v_head, preferred_element_type=jnp.float32)
        grad_scores = (probs * (grad_probs - row_dot) * score_scale).astype(jnp.bfloat16)
        grad_qhead = jnp.dot(grad_scores, k_head, preferred_element_type=jnp.float32)
        used = block_count * tile_rows
        key_terms = jnp.einsum("qk,qd->kd", grad_scores, q_head, preferred_element_type=jnp.float32)
        val_terms = jnp.einsum("qk,qd->kd", probs_low, g_head, preferred_element_type=jnp.float32)
        key_terms = key_terms.astype(jnp.bfloat16).reshape(block_count, tile_rows, HEAD_DIM)
        val_terms = val_terms.astype(jnp.bfloat16).reshape(block_count, tile_rows, HEAD_DIM)
        return (
            out_low,
            grad_qhead,
            key_terms,
            val_terms,
            row_max[:, 0],
            row_sum[:, 0],
            row_dot[:, 0],
        )

    out_heads, grad_qheads, key_heads, val_heads, row_maxes, row_sums, row_dots = lax.map(
        one_head, jnp.arange(head_count)
    )
    attn = heads_last(out_heads)
    grad_qnorm = heads_last(grad_qheads).reshape(tile_rows, head_count, HEAD_DIM)
    key_blocks = heads_last(key_heads)
    val_blocks = heads_last(val_heads)
    key_sum = key_blocks[0].astype(jnp.float32)
    val_sum = val_blocks[0].astype(jnp.float32)
    for direction, step in enumerate(offsets):
        back_keys, back_vals = return_terms(
            (key_blocks[direction + 1], val_blocks[direction + 1]), -step
        )
        key_sum = key_sum + back_keys.astype(jnp.float32)
        val_sum = val_sum + back_vals.astype(jnp.float32)
    grad_knorm = key_sum.reshape(tile_rows, head_count, HEAD_DIM)
    q_back, q_gain_part = norm_backward(grad_qnorm, q_unit, q_root, q_gain)
    k_back, k_gain_part = norm_backward(grad_knorm, k_unit, k_root, k_gain)
    q_gain_sum, k_gain_sum = lax.psum((q_gain_part, k_gain_part), ("seq", "dp"))
    grad_q = q_back.reshape(tile_rows, feat_width).astype(jnp.bfloat16)
    grad_k = k_back.reshape(tile_rows, feat_width).astype(jnp.bfloat16)
    grad_v = val_sum.astype(jnp.bfloat16)
    return (attn[None], grad_q[None], grad_k[None], grad_v[None], q_gain_sum, k_gain_sum)


def solution(mesh):
    placed = (
        P("dp", "seq", None),
        P("dp", "seq", None),
        P("dp", "seq", None),
        P(),
        P(),
        P("dp", "seq", None),
        P("dp", "seq", None),
    )
    return jax.shard_map(
        on_device,
        mesh=mesh,
        in_specs=placed,
        out_specs=(
            P("dp", "seq", None),
            P("dp", "seq", None),
            P("dp", "seq", None),
            P("dp", "seq", None),
            P(),
            P(),
        ),
        check_vma=False,
    )
```

profile of v0, /device:TPU:4, one launch (start us, length us, event | category | flops | bytes accessed | tf_op | source)
XLA Modules:
  0.0 625.5 jit_solution(13348228941153973605)
XLA Ops:
  0.6 3.9 collective-permute-start.5
  4.5 6.2 collective-permute-start.4
  10.7 3.7 collective-permute-start.3
  14.4 1.7 copy.39
  16.1 1.7 multiply_reduce_fusion.4
  19.2 2.7 collective-permute-start.2
  21.9 6.2 collective-permute-start.1
  28.1 1.7 copy.38
  29.8 2.4 multiply_reduce_fusion.5
  32.1 4.5 collective-permute-start
  37.8 2.5 copy.40
  42.5 19.1 %collective-permute-done.3 = bf16[384,1536]{1,0:T(8,128)(2,1)} collective-permute-done((bf16[384,1536]{1,0:T(8,128)(2,1)}, bf16[384,1536]{1,0:T(8,128)(2,1)}, u32[]{:S(2)}, u32[]{:S(2)}) %collective-permute-start.3) | collective-permute-done | bytes 1179680 | tf_op jit(solution)/shard_map/ppermute | solution.py:14
  61.7 3.7 pad_maximum_fusion.1
  65.4 21.6 %collective-permute-done.1 = bf16[384,1536]{0,1:T(8,128)(2,1)} collective-permute-done((bf16[384,1536]{0,1:T(8,128)(2,1)}, bf16[384,1536]{0,1:T(8,128)(2,1)}, u32[]{:S(2)}, u32[]{:S(2)}) %collective-permute-start.1) | collective-permute-done | bytes 1179680 | tf_op jit(solution)/shard_map/ppermute | solution.py:14
  87.0 23.8 %collective-permute-done = bf16[384,1536]{0,1:T(8,128)(2,1)} collective-permute-done((bf16[384,1536]{0,1:T(8,128)(2,1)}, bf16[384,1536]{0,1:T(8,128)(2,1)}, u32[]{:S(2)}, u32[]{:S(2)}) %collective-permute-start) | collective-permute-done | bytes 1179680 | tf_op jit(solution)/shard_map/ppermute | solution.py:14
  110.8 4.0 pad_maximum_fusion
  114.8 196.5 %while.17 = (s32[]{:T(128)}, bf16[12,384,128]{1,2,0:T(8,128)(2,1)}, f32[12,384,128]{1,2,0:T(8,128)}, bf16[12,4,384,128]{2,3,0,1:T(8,128)(2,1)}, bf16[12,4,384,12...) while((s32[]{:T(128)}, bf16[12,384,128]{1,2,0:T(8,128)(2,1)}, ...), condition=%wide.region_6.7_spmd.clone, body=%wide.region_2.6_spmd.clone.sunk | while | flops 914275200 | bytes 35210092 | solution.py:107
  118.6 1.6 fusion.67
  135.0 1.6 fusion.67
  151.4 1.6 fusion.67
  167.8 1.6 fusion.67
  184.1 1.6 fusion.67
  216.8 1.6 fusion.67
  249.6 1.6 fusion.67
  298.7 1.6 fusion.67
  311.3 4.5 fusion.34
  321.2 4.6 fusion.35
  329.2 66.2 %collective-permute-done.11 = bf16[384,1536]{0,1:T(8,128)(2,1)} collective-permute-done((bf16[384,1536]{0,1:T(8,128)(2,1)S(1)}, bf16[384,1536]{0,1:T(8,128)(2,1)}, u32[]{:S(2)}, u32[]{:S(2)}) %collective-permute-start.11) | collective-permute-done | bytes 1179680 | tf_op jit(solution)/shard_map/ppermute | solution.py:14
  398.9 2.6 fusion.31
  403.0 92.6 %collective-permute-done.8 = bf16[384,1536]{0,1:T(8,128)(2,1)} collective-permute-done((bf16[384,1536]{0,1:T(8,128)(2,1)}, bf16[384,1536]{0,1:T(8,128)(2,1)}, u32[]{:S(2)}, u32[]{:S(2)}) %collective-permute-start.8) | collective-permute-done | bytes 1179680 | tf_op jit(solution)/shard_map/ppermute | solution.py:14
  495.7 3.1 multiply_reduce_fusion.1
  501.3 124.2 %all-reduce = (f32[128]{0:T(128)}, f32[128]{0:T(128)}) all-reduce(f32[128]{0:T(128)S(1)} %get-tuple-element.129, f32[128]{0:T(128)S(1)} %bitcast_reduce_fusion), channel_id=1, replica_groups=mesh['seq'=32,'dp'=8] {'seq','dp'}, use_global_device_ids=true, to_apply=%region_10.11 | all-reduce | flops 256 | bytes 2048 | tf_op jit(solution)/shard_map/psum | solution.py:125
  (378 shorter events, 195.6 us)
Async XLA Ops:
  0.6 31.5 %collective-permute-start.5 = (bf16[384,1536]{1,0:T(8,128)(2,1)}, bf16[384,1536]{1,0:T(8,128)(2,1)S(1)}, u32[]{:S(2)}, u32[]{:S(2)}) collective-permute-start(bf16[384,1536]{1,0:T(8,128)(2,1)} %bitcast.149), channel_id=1, source_target_pairs={{0,32},{8,40},{16,48},{24,56},{32,64},{40,72},{48,80},{56,88},{64,... | collective-permute-start | bytes 3538952 | tf_op jit(solution)/shard_map/ppermute | solution.py:14
  4.5 38.0 %collective-permute-start.4 = (bf16[384,1536]{1,0:T(8,128)(2,1)}, bf16[384,1536]{1,0:T(8,128)(2,1)}, u32[]{:S(2)}, u32[]{:S(2)}) collective-permute-start(bf16[384,1536]{1,0:T(8,128)(2,1)} %bitcast.150), channel_id=1, source_target_pairs={{0,16},{8,24},{16,32},{24,40},{32,48},{40,56},{48,64},{56,72},{64,... | collective-permute-start | bytes 3538952 | tf_op jit(solution)/shard_map/ppermute | solution.py:14
  10.7 51.0 %collective-permute-start.3 = (bf16[384,1536]{1,0:T(8,128)(2,1)}, bf16[384,1536]{1,0:T(8,128)(2,1)}, u32[]{:S(2)}, u32[]{:S(2)}) collective-permute-start(bf16[384,1536]{1,0:T(8,128)(2,1)} %bitcast.151), channel_id=1, source_target_pairs={{0,8},{8,16},{16,24},{24,32},{32,40},{40,48},{48,56},{56,64},{64,7... | collective-permute-start | bytes 3538952 | tf_op jit(solution)/shard_map/ppermute | solution.py:14
  16.1 20.6 %copy-start.3 = (bf16[1,384,1536]{1,2,0:T(8,128)(2,1)}, bf16[1,384,1536]{1,2,0:T(8,128)(2,1)S(1)}, u32[]{:S(2)}) copy-start(bf16[1,384,1536]{1,2,0:T(8,128)(2,1)S(1)} %copy.39) | copy-start | bytes 3538948
  19.2 46.1 %collective-permute-start.2 = (bf16[384,1536]{0,1:T(8,128)(2,1)}, bf16[384,1536]{0,1:T(8,128)(2,1)}, u32[]{:S(2)}, u32[]{:S(2)}) collective-permute-start(bf16[384,1536]{0,1:T(8,128)(2,1)} %multiply_convert_fusion.1), channel_id=1, source_target_pairs={{0,32},{8,40},{16,48},{24,56},{32,64},{40,72},{48,80},{56,88},{64,... | collective-permute-start | bytes 3538952 | tf_op jit(solution)/shard_map/ppermute | solution.py:14
  21.9 65.1 %collective-permute-start.1 = (bf16[384,1536]{0,1:T(8,128)(2,1)}, bf16[384,1536]{0,1:T(8,128)(2,1)}, u32[]{:S(2)}, u32[]{:S(2)}) collective-permute-start(bf16[384,1536]{0,1:T(8,128)(2,1)} %multiply_convert_fusion.1), channel_id=1, source_target_pairs={{0,16},{8,24},{16,32},{24,40},{32,48},{40,56},{48,64},{56,72},{64,... | collective-permute-start | bytes 3538952 | tf_op jit(solution)/shard_map/ppermute | solution.py:14
  29.8 6.9 %copy-start.17 = (f32[128]{0:T(128)S(1)}, f32[128]{0:T(128)}, u32[]{:S(2)}) copy-start(f32[128]{0:T(128)} %param.12) | copy-start | bytes 1540
  32.1 78.7 %collective-permute-start = (bf16[384,1536]{0,1:T(8,128)(2,1)}, bf16[384,1536]{0,1:T(8,128)(2,1)}, u32[]{:S(2)}, u32[]{:S(2)}) collective-permute-start(bf16[384,1536]{0,1:T(8,128)(2,1)} %multiply_convert_fusion.1), channel_id=1, source_target_pairs={{0,8},{8,16},{16,24},{24,32},{32,40},{40,48},{48,56},{56,64},{64,7... | collective-permute-start | bytes 3538952 | tf_op jit(solution)/shard_map/ppermute | solution.py:14
  37.8 23.9 %copy-start.9 = (bf16[1,384,1536]{2,1,0:T(8,128)(2,1)S(1)}, bf16[1,384,1536]{2,1,0:T(8,128)(2,1)}, u32[]{:S(2)}) copy-start(bf16[1,384,1536]{2,1,0:T(8,128)(2,1)} %param.11) | copy-start | bytes 3538948
  40.2 21.4 %copy-start.11 = (bf16[384,1536]{1,0:T(8,128)(2,1)S(1)}, bf16[384,1536]{1,0:T(8,128)(2,1)}, u32[]{:S(2)}) copy-start(bf16[384,1536]{1,0:T(8,128)(2,1)} %copy-done.10) | copy-start | bytes 3538948
  117.2 6.4 %copy-start.2 = (bf16[4,384,128]{2,1,0:T(8,128)(2,1)}, bf16[4,384,128]{2,1,0:T(8,128)(2,1)S(1)}, u32[]{:S(2)}) copy-start(bf16[4,384,128]{2,1,0:T(8,128)(2,1)S(1)} %constant_dynamic-slice_fusion.4) | copy-start | bytes 1179652 | tf_op jit(solution)/shard_map/while
  133.5 6.4 %copy-start.2 = (bf16[4,384,128]{2,1,0:T(8,128)(2,1)}, bf16[4,384,128]{2,1,0:T(8,128)(2,1)S(1)}, u32[]{:S(2)}) copy-start(bf16[4,384,128]{2,1,0:T(8,128)(2,1)S(1)} %constant_dynamic-slice_fusion.4) | copy-start | bytes 1179652 | tf_op jit(solution)/shard_map/while
  149.9 6.4 %copy-start.2 = (bf16[4,384,128]{2,1,0:T(8,128)(2,1)}, bf16[4,384,128]{2,1,0:T(8,128)(2,1)S(1)}, u32[]{:S(2)}) copy-start(bf16[4,384,128]{2,1,0:T(8,128)(2,1)S(1)} %constant_dynamic-slice_fusion.4) | copy-start | bytes 1179652 | tf_op jit(solution)/shard_map/while
  166.3 6.4 %copy-start.2 = (bf16[4,384,128]{2,1,0:T(8,128)(2,1)}, bf16[4,384,128]{2,1,0:T(8,128)(2,1)S(1)}, u32[]{:S(2)}) copy-start(bf16[4,384,128]{2,1,0:T(8,128)(2,1)S(1)} %constant_dynamic-slice_fusion.4) | copy-start | bytes 1179652 | tf_op jit(solution)/shard_map/while
  182.6 6.4 %copy-start.2 = (bf16[4,384,128]{2,1,0:T(8,128)(2,1)}, bf16[4,384,128]{2,1,0:T(8,128)(2,1)S(1)}, u32[]{:S(2)}) copy-start(bf16[4,384,128]{2,1,0:T(8,128)(2,1)S(1)} %constant_dynamic-slice_fusion.4) | copy-start | bytes 1179652 | tf_op jit(solution)/shard_map/while
  199.0 6.4 %copy-start.2 = (bf16[4,384,128]{2,1,0:T(8,128)(2,1)}, bf16[4,384,128]{2,1,0:T(8,128)(2,1)S(1)}, u32[]{:S(2)}) copy-start(bf16[4,384,128]{2,1,0:T(8,128)(2,1)S(1)} %constant_dynamic-slice_fusion.4) | copy-start | bytes 1179652 | tf_op jit(solution)/shard_map/while
  215.4 6.4 %copy-start.2 = (bf16[4,384,128]{2,1,0:T(8,128)(2,1)}, bf16[4,384,128]{2,1,0:T(8,128)(2,1)S(1)}, u32[]{:S(2)}) copy-start(bf16[4,384,128]{2,1,0:T(8,128)(2,1)S(1)} %constant_dynamic-slice_fusion.4) | copy-start | bytes 1179652 | tf_op jit(solution)/shard_map/while
  231.8 6.4 %copy-start.2 = (bf16[4,384,128]{2,1,0:T(8,128)(2,1)}, bf16[4,384,128]{2,1,0:T(8,128)(2,1)S(1)}, u32[]{:S(2)}) copy-start(bf16[4,384,128]{2,1,0:T(8,128)(2,1)S(1)} %constant_dynamic-slice_fusion.4) | copy-start | bytes 1179652 | tf_op jit(solution)/shard_map/while
  248.1 6.4 %copy-start.2 = (bf16[4,384,128]{2,1,0:T(8,128)(2,1)}, bf16[4,384,128]{2,1,0:T(8,128)(2,1)S(1)}, u32[]{:S(2)}) copy-start(bf16[4,384,128]{2,1,0:T(8,128)(2,1)S(1)} %constant_dynamic-slice_fusion.4) | copy-start | bytes 1179652 | tf_op jit(solution)/shard_map/while
  264.5 6.4 %copy-start.2 = (bf16[4,384,128]{2,1,0:T(8,128)(2,1)}, bf16[4,384,128]{2,1,0:T(8,128)(2,1)S(1)}, u32[]{:S(2)}) copy-start(bf16[4,384,128]{2,1,0:T(8,128)(2,1)S(1)} %constant_dynamic-slice_fusion.4) | copy-start | bytes 1179652 | tf_op jit(solution)/shard_map/while
  297.3 6.4 %copy-start.2 = (bf16[4,384,128]{2,1,0:T(8,128)(2,1)}, bf16[4,384,128]{2,1,0:T(8,128)(2,1)S(1)}, u32[]{:S(2)}) copy-start(bf16[4,384,128]{2,1,0:T(8,128)(2,1)S(1)} %constant_dynamic-slice_fusion.4) | copy-start | bytes 1179652 | tf_op jit(solution)/shard_map/while
  315.8 79.6 %collective-permute-start.11 = (bf16[384,1536]{0,1:T(8,128)(2,1)S(1)}, bf16[384,1536]{0,1:T(8,128)(2,1)}, u32[]{:S(2)}, u32[]{:S(2)}) collective-permute-start(bf16[384,1536]{0,1:T(8,128)(2,1)S(1)} %bitcast.153), channel_id=1, source_target_pairs={{32,0},{40,8},{48,16},{56,24},{64,32},{72,40},{80,48},{88,56},{96,... | collective-permute-start | bytes 3538952 | tf_op jit(solution)/shard_map/ppermute | solution.py:14
  318.5 80.4 %collective-permute-start.10 = (bf16[384,1536]{0,1:T(8,128)(2,1)}, bf16[384,1536]{0,1:T(8,128)(2,1)}, u32[]{:S(2)}, u32[]{:S(2)}) collective-permute-start(bf16[384,1536]{0,1:T(8,128)(2,1)} %bitcast.33), channel_id=1, source_target_pairs={{16,0},{24,8},{32,16},{40,24},{48,32},{56,40},{64,48},{72,56},{80,... | collective-permute-start | bytes 3538952 | tf_op jit(solution)/shard_map/ppermute | solution.py:14
  319.8 79.1 %collective-permute-start.9 = (bf16[384,1536]{0,1:T(8,128)(2,1)}, bf16[384,1536]{0,1:T(8,128)(2,1)}, u32[]{:S(2)}, u32[]{:S(2)}) collective-permute-start(bf16[384,1536]{0,1:T(8,128)(2,1)} %bitcast.32), channel_id=1, source_target_pairs={{8,0},{16,8},{24,16},{32,24},{40,32},{48,40},{56,48},{64,56},{72,6... | collective-permute-start | bytes 3538952 | tf_op jit(solution)/shard_map/ppermute | solution.py:14
  321.1 7.2 %copy-start.6 = (f32[384,12,128]{0,2,1:T(8,128)S(1)}, f32[384,12,128]{0,2,1:T(8,128)}, u32[]{:S(2)}) copy-start(f32[384,12,128]{0,2,1:T(8,128)} %get-tuple-element.160) | copy-start | bytes 7077892
  321.1 7.2 %copy-start.8 = (f32[12,384,128]{1,2,0:T(8,128)S(1)}, f32[12,384,128]{1,2,0:T(8,128)}, u32[]{:S(2)}) copy-start(f32[12,384,128]{1,2,0:T(8,128)} %get-tuple-element.67) | copy-start | bytes 7077892
  321.1 7.2 %copy-start.16 = (f32[384,12]{0,1:T(8,128)S(1)}, f32[384,12]{0,1:T(8,128)}, u32[]{:S(2)}) copy-start(f32[384,12]{0,1:T(8,128)} %copy-done.15) | copy-start | bytes 55300
  321.2 7.2 %copy-start.18 = (f32[128]{0:T(128)S(1)}, f32[128]{0:T(128)}, u32[]{:S(2)}) copy-start(f32[128]{0:T(128)} %param.12) | copy-start | bytes 1540
  325.8 169.8 %collective-permute-start.8 = (bf16[384,1536]{0,1:T(8,128)(2,1)}, bf16[384,1536]{0,1:T(8,128)(2,1)}, u32[]{:S(2)}, u32[]{:S(2)}) collective-permute-start(bf16[384,1536]{0,1:T(8,128)(2,1)} %bitcast.26), channel_id=1, source_target_pairs={{32,0},{40,8},{48,16},{56,24},{64,32},{72,40},{80,48},{88,56},{96,... | collective-permute-start | bytes 3538952 | tf_op jit(solution)/shard_map/ppermute | solution.py:14
  327.1 168.6 %collective-permute-start.7 = (bf16[384,1536]{0,1:T(8,128)(2,1)}, bf16[384,1536]{0,1:T(8,128)(2,1)}, u32[]{:S(2)}, u32[]{:S(2)}) collective-permute-start(bf16[384,1536]{0,1:T(8,128)(2,1)} %bitcast.25), channel_id=1, source_target_pairs={{16,0},{24,8},{32,16},{40,24},{48,32},{56,40},{64,48},{72,56},{80,... | collective-permute-start | bytes 3538952 | tf_op jit(solution)/shard_map/ppermute | solution.py:14
  395.4 100.2 %collective-permute-start.6 = (bf16[384,1536]{0,1:T(8,128)(2,1)}, bf16[384,1536]{0,1:T(8,128)(2,1)}, u32[]{:S(2)}, u32[]{:S(2)}) collective-permute-start(bf16[384,1536]{0,1:T(8,128)(2,1)} %bitcast.24), channel_id=1, source_target_pairs={{8,0},{16,8},{24,16},{32,24},{40,32},{48,40},{56,48},{64,56},{72,6... | collective-permute-start | bytes 3538952 | tf_op jit(solution)/shard_map/ppermute | solution.py:14
  401.5 94.1 %copy-start.4 = (bf16[1,384,1536]{1,2,0:T(8,128)(2,1)S(1)}, bf16[1,384,1536]{1,2,0:T(8,128)(2,1)}, u32[]{:S(2)}) copy-start(bf16[1,384,1536]{1,2,0:T(8,128)(2,1)} %copy-done.3) | copy-start | bytes 3538948
  (46 other events, 110.5 us)
where the time goes:
time: 631 us; the launch traced here: 626 us
  waiting for transfers between devices  223 us (35%)
  blocking collectives  124 us (20%)
  matrix products  101 us (16%)
  local copies, waits for them, and re-layouts  84.5 us (13%)
  other arithmetic  47.6 us (8%)
  starting transfers between devices  35 us (6%)
  loops' own time  8.99 us (1%)
    ppermute x12, waiting for transfers between devices, shifted(): return lax.ppermute(block, axis, route)  223 us
    psum x1, blocking collectives, on_device(): q_gain_sum, k_gain_sum = lax.psum((q_gain_part, k_gain_part), ('seq', 'dp'))  124 us
    ppermute x12, starting transfers between devices, shifted(): return lax.ppermute(block, axis, route)  35 us
    dynamic_update_slice x36, local copies, waits for them, and re-layouts, on_device(): lax.map(one_head, jnp.arange(head_count))  26 us
    dot_general x12, matrix products, one_head(): jnp.einsum('qd,kd->qk', q_head, k_head, preferred_element_type=jnp.float32)  19.3 us
    dot_general x12, matrix products, one_head(): jnp.einsum('qd,kd->qk', g_head, v_head, preferred_element_type=jnp.float32)  19 us
    dot_general x12, matrix products, one_head(): jnp.einsum('qk,qd->kd', grad_scores, q_head, preferred_element_type=jnp.f...  17.7 us
    dot_general x12, matrix products, one_head(): jnp.einsum('qk,qd->kd', probs_low, g_head, preferred_element_type=jnp.flo...  17 us
  transfers between devices with their start and end apart: 12, of which 5 were waited for; matrix products, arithmetic and copies ran while one was open for 5% of the time, Pallas kernels for 0%

commit v1 on v0

v1 whole, which is shorter than its diff:
```python
import functools
import math

import jax
import jax.numpy as jnp
from jax import lax
from jax.experimental import pallas as pl
from jax.experimental.pallas import tpu as pltpu
from jax.sharding import PartitionSpec as P

HEAD_DIM = 128
ROW = 4
SPLITS = (4, 4, 4)
F32 = jnp.float32
BF16 = jnp.bfloat16

KEYS_OUT = ((0, 1), (1, 0), (2, 3))
KEYS_ON = ((1, 2), (0, 3))
TERMS_OUT = ((3, 0), (2, 1))
TERMS_ON = ((0, 1), (1, 0), (3, 2))


def dot(a, b):
    return lax.dot_general(a, b, (((1,), (0,)), ((), ())), preferred_element_type=F32)


def unit_rows(block):
    flat = block.astype(F32)
    root = lax.rsqrt(jnp.mean(flat * flat, axis=1, keepdims=True) + 1e-6)
    return flat * root, root


def attn_kernel(win, q_ref, k_ref, v_ref, g_ref, kv1, kv2, kv4, qg_ref, kg_ref, *refs):
    refs = refs[2:] if len(refs) == 17 else refs
    (out_ref, gq_ref, own_ref, t1_ref, t2_ref, t4_ref, qsum_ref, ksum_ref) = refs[:8]
    (s_ref, p_ref, kb_ref, kt_ref, m_ref, l_ref, acc_ref) = refs[8:]
    step = pl.program_id(0)
    scale = HEAD_DIM ** (-0.5)
    to_two = scale * math.log2(math.e)

    @pl.when(step == 0)
    def _():
        qsum_ref[...] = jnp.zeros_like(qsum_ref)
        ksum_ref[...] = jnp.zeros_like(ksum_ref)

    q_gain = qg_ref[...]
    k_gain = kg_ref[...]
    qt = q_ref[...].T.astype(F32)
    q_root = lax.rsqrt(jnp.mean(qt * qt, axis=0, keepdims=True) + 1e-6)
    q_unit = qt * q_root
    qt_b = (q_unit * q_gain).astype(BF16)
    q_b = qt_b.T
    g_b = g_ref[...]
    gt_b = g_b.T

    def keys(j):
        return k_ref[...] if j == 0 else (kv1, kv2, kv4)[j - 1][0]

    def vals(j):
        return v_ref[...] if j == 0 else (kv1, kv2, kv4)[j - 1][1]

    terms = (own_ref, t1_ref, t2_ref, t4_ref)

    def each(body, otherwise=None):
        body(0)
        for j in range(1, 4):
            pl.when(win[j - 1] >= 0)(functools.partial(body, j))
            if otherwise is not None:
                pl.when(win[j - 1] < 0)(functools.partial(otherwise, j))

    def scores(j):
        unit, _ = unit_rows(keys(j))
        k_b = (unit * k_gain).astype(BF16)
        kb_ref[j] = k_b
        kt_ref[j] = k_b.T
        s = dot(k_b, qt_b)
        s_ref[j] = s
        top = jnp.max(s, axis=0, keepdims=True)
        m_ref[...] = top if j == 0 else jnp.maximum(m_ref[...], top)

    each(scores)
    m_ref[...] = m_ref[...] * to_two

    def powers(j):
        e = jnp.exp2(s_ref[j] * to_two - m_ref[...])
        s_ref[j] = e
        total = jnp.sum(e, axis=0, keepdims=True)
        l_ref[...] = total if j == 0 else l_ref[...] + total

    each(powers)
    l_ref[...] = 1.0 / l_ref[...]

    def forward(j):
        p = (s_ref[j] * l_ref[...]).astype(BF16)
        p_ref[j] = p
        o = dot(vals(j).T, p)
        acc_ref[...] = o if j == 0 else acc_ref[...] + o

    each(forward)
    out_low = acc_ref[...].astype(BF16)
    out_ref[...] = out_low.T
    row_dot = jnp.sum(gt_b.astype(F32) * out_low.astype(F32), axis=0, keepdims=True)
    m_ref[...] = row_dot

    def backward(j):
        dp = dot(vals(j), gt_b)
        ds = ((s_ref[j] * l_ref[...]) * (dp - m_ref[...]) * scale).astype(BF16)
        dq = dot(kt_ref[j], ds)
        acc_ref[...] = dq if j == 0 else acc_ref[...] + dq
        dk = dot(ds, q_b).astype(BF16)
        terms[j][0] = dk
        terms[j][1] = dot(p_ref[j], g_b).astype(BF16)
        unit, _ = unit_rows(keys(j))
        ksum_ref[...] += jnp.sum((dk.astype(F32) * unit).reshape(-1, 8, HEAD_DIM), axis=0)

    def nothing(j):
        terms[j][...] = jnp.zeros_like(terms[j])

    each(backward, nothing)
    dq = acc_ref[...]
    qsum_ref[...] += dq * q_unit
    scaled = dq * q_gain
    inner = jnp.mean(scaled * q_unit, axis=0, keepdims=True)
    gq_ref[...] = (q_root * (scaled - q_unit * inner)).astype(BF16).T


def attn_part(first, heads, win, q, k, v, g, pairs, q_gain, k_gain, filled):
    rows, width = q.shape
    part = heads * HEAD_DIM
    whole = pl.BlockSpec((rows, HEAD_DIM), lambda h: (0, first + h))
    two = pl.BlockSpec((2, rows, HEAD_DIM), lambda h: (0, 0, h))
    smem = pl.BlockSpec(memory_space=pltpu.SMEM)
    hbm = pl.BlockSpec(memory_space=pl.ANY)

    def const(shape):
        return pl.BlockSpec(shape, lambda h: (0, 0))

    full = jax.ShapeDtypeStruct((rows, width), BF16)
    pair = jax.ShapeDtypeStruct((2, rows, part), BF16)
    filled = () if filled is None else filled
    return pl.pallas_call(
        attn_kernel,
        grid=(heads,),
        in_specs=[smem, whole, whole, whole, whole, two, two, two, const((HEAD_DIM, 1)), const((1, HEAD_DIM))]
        + [hbm] * len(filled),
        out_specs=[whole, whole, two, two, two, two, const((HEAD_DIM, rows)), const((8, HEAD_DIM))],
        out_shape=[
            full,
            full,
            pair,
            pair,
            pair,
            pair,
            jax.ShapeDtypeStruct((HEAD_DIM, rows), F32),
            jax.ShapeDtypeStruct((8, HEAD_DIM), F32),
        ],
        scratch_shapes=[
            pltpu.VMEM((4, rows, rows), F32),
            pltpu.VMEM((4, rows, rows), BF16),
            pltpu.VMEM((4, rows, HEAD_DIM), BF16),
            pltpu.VMEM((4, HEAD_DIM, rows), BF16),
            pltpu.VMEM((1, rows), F32),
            pltpu.VMEM((1, rows), F32),
            pltpu.VMEM((HEAD_DIM, rows), F32),
        ],
        input_output_aliases={10 + i: i for i in range(len(filled))},
        compiler_params=pltpu.CompilerParams(
            dimension_semantics=("arbitrary",), vmem_limit_bytes=24 * 2**20
        ),
        cost_estimate=pl.CostEstimate(
            flops=heads * 12 * 4 * rows * rows * HEAD_DIM * 3,
            bytes_accessed=heads * rows * HEAD_DIM * 2 * 20,
            transcendentals=heads * 4 * rows * rows,
        ),
        name="attention_part",
    )(win, q, k, v, g, *pairs, q_gain.reshape(HEAD_DIM, 1), k_gain.reshape(1, HEAD_DIM), *filled)


def close_kernel(k_ref, own, got_y, got_z, kg_ref, *refs):
    gk_ref, gv_ref = refs[-2:]
    dk = own[0].astype(F32) + got_y[0].astype(F32) + got_z[0].astype(F32)
    dv = own[1].astype(F32) + got_y[1].astype(F32) + got_z[1].astype(F32)
    gv_ref[...] = dv.astype(BF16)
    unit, root = unit_rows(k_ref[...])
    scaled = dk * kg_ref[...]
    inner = jnp.mean(scaled * unit, axis=1, keepdims=True)
    gk_ref[...] = (root * (scaled - unit * inner)).astype(BF16)


def close_part(first, heads, k, own, got_y, got_z, k_gain, filled):
    rows, width = k.shape
    whole = pl.BlockSpec((rows, HEAD_DIM), lambda h: (0, first + h))
    two = pl.BlockSpec((2, rows, HEAD_DIM), lambda h: (0, 0, h))
    hbm = pl.BlockSpec(memory_space=pl.ANY)
    full = jax.ShapeDtypeStruct((rows, width), BF16)
    filled = () if filled is None else filled
    return pl.pallas_call(
        close_kernel,
        grid=(heads,),
        in_specs=[whole, two, two, two, pl.BlockSpec((1, HEAD_DIM), lambda h: (0, 0))] + [hbm] * len(filled),
        out_specs=[whole, whole],
        out_shape=[full, full],
        input_output_aliases={5 + i: i for i in range(len(filled))},
        compiler_params=pltpu.CompilerParams(dimension_semantics=("arbitrary",), vmem_limit_bytes=16 * 2**20),
        cost_estimate=pl.CostEstimate(
            flops=heads * rows * HEAD_DIM * 20,
            bytes_accessed=heads * rows * HEAD_DIM * 2 * 9,
            transcendentals=heads * rows,
        ),
        name="close_part",
    )(k, own, got_y, got_z, k_gain.reshape(1, HEAD_DIM), *filled)


def on_device(q_in, k_in, v_in, q_gain, k_gain, window, grad_out):
    q, k, v, g = q_in[0], k_in[0], v_in[0], grad_out[0]
    win = window[0, 0]
    tiles = lax.axis_size("seq")
    starts = range(0, tiles, ROW)

    def in_row(block, hops):
        return lax.ppermute(block, "seq", [(s + a, s + b) for s in starts for a, b in hops])

    def frames(block, step):
        return lax.ppermute(
            block, "seq", [(t, t + step) for t in range(tiles) if 0 <= t + step < tiles]
        )

    firsts = [sum(SPLITS[:i]) for i in range(len(SPLITS))]
    fetched = []
    for first, heads in zip(firsts, SPLITS):
        cols = slice(first * HEAD_DIM, (first + heads) * HEAD_DIM)
        mine = jnp.stack([k[:, cols], v[:, cols]])
        near = in_row(mine, KEYS_OUT)
        back = frames(mine, ROW)
        far = in_row(near, KEYS_ON)
        fetched.append((near, far, back))
    filled, sums, held = None, [], []
    for first, heads, pairs in zip(firsts, SPLITS, fetched):
        out = attn_part(first, heads, win, q, k, v, g, pairs, q_gain, k_gain, filled)
        filled = tuple(out[:2])
        own, near, far, back = out[2:6]
        sums.append((jnp.sum(out[6], axis=1), jnp.sum(out[7], axis=0)))
        via = in_row(far, TERMS_OUT)
        got_z = frames(back, -ROW)
        onward = (near.astype(F32) + via.astype(F32)).astype(BF16)
        got_y = in_row(onward, TERMS_ON)
        held.append((own, got_y, got_z))
    gains = jnp.stack([sum(s[0] for s in sums), sum(s[1] for s in sums)])
    gains = lax.psum(gains, ("seq", "dp"))
    closed = None
    for first, heads, got in zip(firsts, SPLITS, held):
        closed = tuple(close_part(first, heads, k, *got, k_gain, closed))
    return (filled[0][None], filled[1][None], closed[0][None], closed[1][None], gains[0], gains[1])


def solution(mesh):
    rows = P("dp", "seq", None)
    return jax.shard_map(
        on_device,
        mesh=mesh,
        in_specs=(rows, rows, rows, P(), P(), rows, rows),
        out_specs=(rows, rows, rows, rows, P(), P()),
        check_vma=False,
    )
```

time: 631 us -> 298 us (0.47)
  waiting for transfers between devices: 223 us -> 71.2 us
  matrix products: 101 us -> 0 us
  local copies, waits for them, and re-layouts: 84.5 us -> 12 us
  other arithmetic: 47.6 us -> 6.58 us
  Pallas kernels: 0 us -> 39.5 us
  starting transfers between devices: 35 us -> 50.5 us
  blocking collectives: 124 us -> 113 us
  loops' own time: 8.99 us -> 0 us
    ppermute x12 -> x18, waiting for transfers between devices: 223 us -> 71.2 us  [the longest x12 71.2 us: in_row(): lax.ppermute(block, 'seq', [(s + a, s + b) for s in starts for a, b in ho...]
    dot_general x72 -> x0, matrix products: 101 us -> none  [the longest x12 19.3 us: one_head(): jnp.einsum('qd,kd->qk', q_head, k_head, preferred_element_type=jnp.float32)]
    pallas_call x0 -> x6, Pallas kernels: none -> 39.5 us  [the longest x3 27.9 us: attn_part(): pl.pallas_call(attn_kernel, grid=(heads,), in_specs=[smem, whole, whole,...]
    dynamic_slice x48 -> x0, local copies, waits for them, and re-layouts: 36.2 us -> none  [the longest x24 17 us: one_head(): lax.dynamic_slice_in_dim(key_rows, col_start, HEAD_DIM, 2)]
    dynamic_update_slice x36 -> x0, local copies, waits for them, and re-layouts: 26 us -> none  [on_device(): lax.map(one_head, jnp.arange(head_count))]
    reduce_sum x30 -> x6, other arithmetic: 25.4 us -> 0.37 us  [on_device(): sums.append((jnp.sum(out[6], axis=1), jnp.sum(out[7], axis=0)))]
    ppermute x12 -> x18, starting transfers between devices: 35 us -> 50.5 us  [the longest x12 33.3 us: in_row(): lax.ppermute(block, 'seq', [(s + a, s + b) for s in starts for a, b in ho...]
    psum x1, blocking collectives: 124 us -> 113 us  [on_device(): gains = lax.psum(gains, ('seq', 'dp'))]
  transfers between devices with their start and end apart: 12 -> 18, of which waited for: 5 -> 6; matrix products, arithmetic and copies ran while one was open for 5% -> 2% of each run, Pallas kernels for 0% -> 12%
where the time goes in v1:
time: 298 us; the launch traced here: 294 us
  blocking collectives  113 us (38%)
  waiting for transfers between devices  71.2 us (24%)
  starting transfers between devices  50.5 us (17%)
  Pallas kernels  39.5 us (13%)
  local copies, waits for them, and re-layouts  12 us (4%)
  other arithmetic  6.58 us (2%)
    psum x1, blocking collectives, on_device(): gains = lax.psum(gains, ('seq', 'dp'))  113 us
    ppermute x12, waiting for transfers between devices, in_row(): lax.ppermute(block, 'seq', [(s + a, s + b) for s in starts for a, b in ho...  71.2 us
    ppermute x12, starting transfers between devices, in_row(): lax.ppermute(block, 'seq', [(s + a, s + b) for s in starts for a, b in ho...  33.3 us
    pallas_call x3, Pallas kernels, attn_part(): pl.pallas_call(attn_kernel, grid=(heads,), in_specs=[smem, whole, whole,...  27.9 us
    ppermute x6, starting transfers between devices, frames(): lax.ppermute(block, 'seq', [(t, t + step) for t in range(tiles) if 0 <= t...  17.2 us
    pallas_call x3, Pallas kernels, close_part(): pl.pallas_call(close_kernel, grid=(heads,), in_specs=[whole, two, two, tw...  11.6 us
    unnamed x42, local copies, waits for them, and re-layouts  9.47 us
  transfers between devices with their start and end apart: 18, of which 6 were waited for; matrix products, arithmetic and copies ran while one was open for 2% of the time, Pallas kernels for 12%

profile of v1, /device:TPU:4, one launch (start us, length us, event | category | flops | bytes accessed | tf_op | source)
XLA Modules:
  0.0 293.9 jit_solution(16422308733524641028)
XLA Ops:
  0.6 1.9 slice_bitcast_fusion
  3.5 3.5 %collective-permute-start.6 = (bf16[2,384,512]{2,1,0:T(8,128)(2,1)}, bf16[2,384,512]{2,1,0:T(8,128)(2,1)S(1)}, u32[]{:S(2)}, u32[]{:S(2)}) collective-permute-start(bf16[2,384,512]{2,1,0:T(8,128)(2,1)} %pad_maximum_fusion.2), channel_id=1, source_target_pairs={{0,8},{8,0},{16,24},{32,40},{40,32},{48,56},{64,72},{72,64},{80,88... | collective-permute-start | bytes 2359304 | tf_op jit(solution)/shard_map/ppermute | solution.py:221
  7.9 2.5 collective-permute-start
  11.4 3.5 %collective-permute-start.3 = (bf16[2,384,512]{2,1,0:T(8,128)(2,1)}, bf16[2,384,512]{2,1,0:T(8,128)(2,1)}, u32[]{:S(2)}, u32[]{:S(2)}) collective-permute-start(bf16[2,384,512]{2,1,0:T(8,128)(2,1)} %pad_maximum_fusion.1), channel_id=1, source_target_pairs={{0,8},{8,0},{16,24},{32,40},{40,32},{48,56},{64,72},{72,64},{80,88... | collective-permute-start | bytes 2359304 | tf_op jit(solution)/shard_map/ppermute | solution.py:221
  14.9 4.7 %collective-permute-start.8 = (bf16[2,384,512]{2,1,0:T(8,128)(2,1)}, bf16[2,384,512]{2,1,0:T(8,128)(2,1)}, u32[]{:S(2)}, u32[]{:S(2)}) collective-permute-start(bf16[2,384,512]{2,1,0:T(8,128)(2,1)} %pad_maximum_fusion.2), channel_id=1, source_target_pairs={{0,32},{8,40},{16,48},{24,56},{32,64},{40,72},{48,80},{56,88},{64,... | collective-permute-start | bytes 2359304 | tf_op jit(solution)/shard_map/ppermute | solution.py:224
  19.6 6.4 %collective-permute-done.6.kv1 = bf16[2,384,512]{2,1,0:T(8,128)(2,1)S(1)} collective-permute-done((bf16[2,384,512]{2,1,0:T(8,128)(2,1)}, bf16[2,384,512]{2,1,0:T(8,128)(2,1)S(1)}, u32[]{:S(2)}, u32[]{:S(2)}) %collective-permute-start.6) | collective-permute-done | bytes 786464 | tf_op jit(solution)/shard_map/ppermute | solution.py:221
  26.0 5.8 %collective-permute-start.7 = (bf16[2,384,512]{2,1,0:T(8,128)(2,1)S(1)}, bf16[2,384,512]{2,1,0:T(8,128)(2,1)}, u32[]{:S(2)}, u32[]{:S(2)}) collective-permute-start(bf16[2,384,512]{2,1,0:T(8,128)(2,1)S(1)} %collective-permute-done.6.kv1), channel_id=1, source_target_pairs={{8,16},{0,24},{40,48},{32,56},{72,80},{64,88},{104,112},{96,120},{... | collective-permute-start | bytes 2359304 | tf_op jit(solution)/shard_map/ppermute | solution.py:221
  32.7 4.7 %collective-permute-start.2 = (bf16[2,384,512]{2,1,0:T(8,128)(2,1)}, bf16[2,384,512]{2,1,0:T(8,128)(2,1)}, u32[]{:S(2)}, u32[]{:S(2)}) collective-permute-start(bf16[2,384,512]{2,1,0:T(8,128)(2,1)} %pad_maximum_fusion), channel_id=1, source_target_pairs={{0,32},{8,40},{16,48},{24,56},{32,64},{40,72},{48,80},{56,88},{64,... | collective-permute-start | bytes 2359304 | tf_op jit(solution)/shard_map/ppermute | solution.py:224
  37.5 5.5 %collective-permute-done.kv1 = bf16[2,384,512]{2,1,0:T(8,128)(2,1)} collective-permute-done((bf16[2,384,512]{2,1,0:T(8,128)(2,1)}, bf16[2,384,512]{2,1,0:T(8,128)(2,1)}, u32[]{:S(2)}, u32[]{:S(2)}) %collective-permute-start) | collective-permute-done | bytes 786464 | tf_op jit(solution)/shard_map/ppermute | solution.py:221
  43.0 3.9 %collective-permute-start.5 = (bf16[2,384,512]{2,1,0:T(8,128)(2,1)}, bf16[2,384,512]{2,1,0:T(8,128)(2,1)S(1)}, u32[]{:S(2)}, u32[]{:S(2)}) collective-permute-start(bf16[2,384,512]{2,1,0:T(8,128)(2,1)} %pad_maximum_fusion.1), channel_id=1, source_target_pairs={{0,32},{8,40},{16,48},{24,56},{32,64},{40,72},{48,80},{56,88},{64,... | collective-permute-start | bytes 2359304 | tf_op jit(solution)/shard_map/ppermute | solution.py:224
  46.8 11.8 %collective-permute-done.3.kv1 = bf16[2,384,512]{2,1,0:T(8,128)(2,1)} collective-permute-done((bf16[2,384,512]{2,1,0:T(8,128)(2,1)}, bf16[2,384,512]{2,1,0:T(8,128)(2,1)}, u32[]{:S(2)}, u32[]{:S(2)}) %collective-permute-start.3) | collective-permute-done | bytes 786464 | tf_op jit(solution)/shard_map/ppermute | solution.py:221
  58.7 5.0 %collective-permute-start.1 = (bf16[2,384,512]{2,1,0:T(8,128)(2,1)}, bf16[2,384,512]{2,1,0:T(8,128)(2,1)S(1)}, u32[]{:S(2)}, u32[]{:S(2)}) collective-permute-start(bf16[2,384,512]{2,1,0:T(8,128)(2,1)} %collective-permute-done.kv1), channel_id=1, source_target_pairs={{8,16},{0,24},{40,48},{32,56},{72,80},{64,88},{104,112},{96,120},{... | collective-permute-start | bytes 2359304 | tf_op jit(solution)/shard_map/ppermute | solution.py:221
  63.6 1.3 collective-permute-start.4
  68.7 9.3 %attention_part.3 = (bf16[384,1536]{1,0:T(8,128)(2,1)}, bf16[384,1536]{1,0:T(8,128)(2,1)}, bf16[2,384,512]{2,1,0:T(8,128)(2,1)S(1)}, bf16[2,384,512]{2,1,0:T(8,1...) custom-call(s32[3]{0:T(128)S(1)} %bitcast.54, ...), custom_call_target="tpu_custom_call" | custom-call | flops 10871635968 | bytes 7864320 | tf_op jit(solution)/shard_map/attention_part/pallas_call | solution.py:141
  78.9 1.3 collective-permute-start.15
  80.2 16.5 %collective-permute-done.4.kv2 = bf16[2,384,512]{2,1,0:T(8,128)(2,1)S(1)} collective-permute-done((bf16[2,384,512]{2,1,0:T(8,128)(2,1)}, bf16[2,384,512]{2,1,0:T(8,128)(2,1)S(1)}, u32[]{:S(2)}, u32[]{:S(2)}) %collective-permute-start.4) | collective-permute-done | bytes 786464 | tf_op jit(solution)/shard_map/ppermute | solution.py:221
  97.5 9.2 %attention_part.4 = (bf16[384,1536]{1,0:T(8,128)(2,1)}, bf16[384,1536]{1,0:T(8,128)(2,1)}, bf16[2,384,512]{2,1,0:T(8,128)(2,1)S(1)}, bf16[2,384,512]{2,1,0:T(8,1...) custom-call(s32[3]{0:T(128)S(1)} %bitcast.55, ...), custom_call_target="tpu_custom_call", output_to_operand_aliasing={{0}: (10, {}), {1}: (11, {})} | custom-call | flops 10871635968 | bytes 7864320 | tf_op jit(solution)/shard_map/attention_part/pallas_call | solution.py:141
  106.7 1.5 collective-permute-start.12
  108.2 9.3 %attention_part.5 = (bf16[384,1536]{1,0:T(8,128)(2,1)}, bf16[384,1536]{1,0:T(8,128)(2,1)}, bf16[2,384,512]{2,1,0:T(8,128)(2,1)S(1)}, bf16[2,384,512]{2,1,0:T(8,1...) custom-call(s32[3]{0:T(128)S(1)} %bitcast.56, ...), custom_call_target="tpu_custom_call", output_to_operand_aliasing={{0}: (10, {}), {1}: (11, {})} | custom-call | flops 10871635968 | bytes 7864320 | tf_op jit(solution)/shard_map/attention_part/pallas_call | solution.py:141
  117.6 1.3 collective-permute-start.9
  118.9 1.3 collective-permute-start.17
  120.2 1.3 collective-permute-start.14
  121.5 1.3 collective-permute-start.11
  123.9 13.3 %collective-permute-done.12 = bf16[2,384,512]{2,1,0:T(8,128)(2,1)S(1)} collective-permute-done((bf16[2,384,512]{2,1,0:T(8,128)(2,1)S(1)}, bf16[2,384,512]{2,1,0:T(8,128)(2,1)S(1)}, u32[]{:S(2)}, u32[]{:S(2)}) %collective-permute-start.12) | collective-permute-done | bytes 786464 | tf_op jit(solution)/shard_map/ppermute | solution.py:221
  137.2 1.9 collective-permute-start.16
  140.2 17.7 %collective-permute-done.9 = bf16[2,384,512]{2,1,0:T(8,128)(2,1)S(1)} collective-permute-done((bf16[2,384,512]{2,1,0:T(8,128)(2,1)S(1)}, bf16[2,384,512]{2,1,0:T(8,128)(2,1)S(1)}, u32[]{:S(2)}, u32[]{:S(2)}) %collective-permute-start.9) | collective-permute-done | bytes 786464 | tf_op jit(solution)/shard_map/ppermute | solution.py:221
  157.9 1.9 collective-permute-start.13
  161.9 3.9 %collective-permute-start.10 = (bf16[2,384,512]{2,1,0:T(8,128)(2,1)}, bf16[2,384,512]{2,1,0:T(8,128)(2,1)}, u32[]{:S(2)}, u32[]{:S(2)}) collective-permute-start(bf16[2,384,512]{2,1,0:T(8,128)(2,1)} %add_convert_fusion.2), channel_id=1, source_target_pairs={{0,8},{8,0},{24,16},{32,40},{40,32},{56,48},{64,72},{72,64},{88,80... | collective-permute-start | bytes 2359304 | tf_op jit(solution)/shard_map/ppermute | solution.py:221
  166.2 113.2 %psum.7 = f32[2,128]{1,0:T(2,128)S(1)} all-reduce(f32[2,128]{1,0:T(2,128)S(1)} %pad_maximum_fusion.3), channel_id=1, replica_groups=mesh['seq'=32,'dp'=8] {'seq','dp'}, use_global_device_ids=true, to_apply=%region_6.0 | all-reduce | flops 256 | bytes 2048 | tf_op jit(solution)/shard_map/psum | solution.py:249
  282.2 3.8 %close_part.3 = (bf16[384,1536]{1,0:T(8,128)(2,1)}, bf16[384,1536]{1,0:T(8,128)(2,1)}) custom-call(bf16[384,1536]{1,0:T(8,128)(2,1)S(1)} %bitcast.35, bf16[2,384,512]{2,1,0:T(8,128)(2,1)S(1)} %copy-done.5, bf16[2,384,512]{2,1,0:T(8,128)(2,1)} %collective-permute-done.16.got_y, bf16[2,384,512]{2,1,0:T(8,128)(2,1)S(1)} %copy-done.7, f32[1,128]{1,0:T(1,128)S(1)} %bitcast.45), custom_call_target="tpu_custom_call" | custom-call | flops 3932160 | bytes 3538944 | tf_op jit(solution)/shard_map/close_part/pallas_call | solution.py:197
  286.0 4.1 %close_part.4 = (bf16[384,1536]{1,0:T(8,128)(2,1)}, bf16[384,1536]{1,0:T(8,128)(2,1)}) custom-call(bf16[384,1536]{1,0:T(8,128)(2,1)S(1)} %bitcast.36, bf16[2,384,512]{2,1,0:T(8,128)(2,1)S(1)} %get-tuple-element.46.own, bf16[2,384,512]{2,1,0:T(8,128)(2,1)} %collective-permute-done.13.got_y, ...), custom_call_target="tpu_custom_call", output_to_operand_aliasing={{0}: (5, {}), {1}: (6, {})} | custom-call | flops 3932160 | bytes 3538944 | tf_op jit(solution)/shard_map/close_part/pallas_call | solution.py:197
  290.1 3.8 %close_part.5 = (bf16[384,1536]{1,0:T(8,128)(2,1)}, bf16[384,1536]{1,0:T(8,128)(2,1)}) custom-call(bf16[384,1536]{1,0:T(8,128)(2,1)S(1)} %bitcast.37, bf16[2,384,512]{2,1,0:T(8,128)(2,1)S(1)} %copy-done.3, bf16[2,384,512]{2,1,0:T(8,128)(2,1)} %collective-permute-done.10.got_y, ...), custom_call_target="tpu_custom_call", output_to_operand_aliasing={{0}: (5, {}), {1}: (6, {})} | custom-call | flops 3932160 | bytes 3538944 | tf_op jit(solution)/shard_map/close_part/pallas_call | solution.py:197
  (71 shorter events, 16.7 us)
Async XLA Ops:
  3.5 22.5 %collective-permute-start.6 = (bf16[2,384,512]{2,1,0:T(8,128)(2,1)}, bf16[2,384,512]{2,1,0:T(8,128)(2,1)S(1)}, u32[]{:S(2)}, u32[]{:S(2)}) collective-permute-start(bf16[2,384,512]{2,1,0:T(8,128)(2,1)} %pad_maximum_fusion.2), channel_id=1, source_target_pairs={{0,8},{8,0},{16,24},{32,40},{40,32},{48,56},{64,72},{72,64},{80,88... | collective-permute-start | bytes 2359304 | tf_op jit(solution)/shard_map/ppermute | solution.py:221
  7.0 58.0 %copy-start.1 = (bf16[1,384,1536]{2,1,0:T(8,128)(2,1)S(1)}, bf16[1,384,1536]{2,1,0:T(8,128)(2,1)}, u32[]{:S(2)}) copy-start(bf16[1,384,1536]{2,1,0:T(8,128)(2,1)} %param.9) | copy-start | bytes 3538948
  7.9 29.5 %copy-start.20 = (f32[128]{0:T(128)S(1)}, f32[128]{0:T(128)}, u32[]{:S(2)}) copy-start(f32[128]{0:T(128)} %param.10) | copy-start | bytes 1540
  7.9 57.1 %copy-start = (bf16[1,384,1536]{2,1,0:T(8,128)(2,1)S(1)}, bf16[1,384,1536]{2,1,0:T(8,128)(2,1)}, u32[]{:S(2)}) copy-start(bf16[1,384,1536]{2,1,0:T(8,128)(2,1)} %param.8) | copy-start | bytes 3538948
  7.9 57.1 %copy-start.12 = (f32[128]{0:T(128)S(1)}, f32[128]{0:T(128)}, u32[]{:S(2)}) copy-start(f32[128]{0:T(128)} %param.11) | copy-start | bytes 1540
  7.9 57.1 %copy-start.18 = (s32[1,1,3]{2,1,0:T(1,128)S(1)}, s32[1,1,3]{2,1,0:T(1,128)}, u32[]{:S(2)}) copy-start(s32[1,1,3]{2,1,0:T(1,128)} %param.12) | copy-start | bytes 40
  7.9 35.0 %collective-permute-start = (bf16[2,384,512]{2,1,0:T(8,128)(2,1)}, bf16[2,384,512]{2,1,0:T(8,128)(2,1)}, u32[]{:S(2)}, u32[]{:S(2)}) collective-permute-start(bf16[2,384,512]{2,1,0:T(8,128)(2,1)} %pad_maximum_fusion), channel_id=1, source_target_pairs={{0,8},{8,0},{16,24},{32,40},{40,32},{48,56},{64,72},{72,64},{80,88... | collective-permute-start | bytes 2359304 | tf_op jit(solution)/shard_map/ppermute | solution.py:221
  11.4 47.3 %collective-permute-start.3 = (bf16[2,384,512]{2,1,0:T(8,128)(2,1)}, bf16[2,384,512]{2,1,0:T(8,128)(2,1)}, u32[]{:S(2)}, u32[]{:S(2)}) collective-permute-start(bf16[2,384,512]{2,1,0:T(8,128)(2,1)} %pad_maximum_fusion.1), channel_id=1, source_target_pairs={{0,8},{8,0},{16,24},{32,40},{40,32},{48,56},{64,72},{72,64},{80,88... | collective-permute-start | bytes 2359304 | tf_op jit(solution)/shard_map/ppermute | solution.py:221
  14.9 48.8 %collective-permute-start.8 = (bf16[2,384,512]{2,1,0:T(8,128)(2,1)}, bf16[2,384,512]{2,1,0:T(8,128)(2,1)}, u32[]{:S(2)}, u32[]{:S(2)}) collective-permute-start(bf16[2,384,512]{2,1,0:T(8,128)(2,1)} %pad_maximum_fusion.2), channel_id=1, source_target_pairs={{0,32},{8,40},{16,48},{24,56},{32,64},{40,72},{48,80},{56,88},{64,... | collective-permute-start | bytes 2359304 | tf_op jit(solution)/shard_map/ppermute | solution.py:224
  26.0 39.0 %collective-permute-start.7 = (bf16[2,384,512]{2,1,0:T(8,128)(2,1)S(1)}, bf16[2,384,512]{2,1,0:T(8,128)(2,1)}, u32[]{:S(2)}, u32[]{:S(2)}) collective-permute-start(bf16[2,384,512]{2,1,0:T(8,128)(2,1)S(1)} %collective-permute-done.6.kv1), channel_id=1, source_target_pairs={{8,16},{0,24},{40,48},{32,56},{72,80},{64,88},{104,112},{96,120},{... | collective-permute-start | bytes 2359304 | tf_op jit(solution)/shard_map/ppermute | solution.py:221
  32.7 75.5 %collective-permute-start.2 = (bf16[2,384,512]{2,1,0:T(8,128)(2,1)}, bf16[2,384,512]{2,1,0:T(8,128)(2,1)}, u32[]{:S(2)}, u32[]{:S(2)}) collective-permute-start(bf16[2,384,512]{2,1,0:T(8,128)(2,1)} %pad_maximum_fusion), channel_id=1, source_target_pairs={{0,32},{8,40},{16,48},{24,56},{32,64},{40,72},{48,80},{56,88},{64,... | collective-permute-start | bytes 2359304 | tf_op jit(solution)/shard_map/ppermute | solution.py:224
  37.5 40.5 %copy-start.10 = (f32[128,1]{1,0:T(8,128)}, f32[128,1]{1,0:T(8,128)S(1)}, u32[]{:S(2)}) copy-start(f32[128,1]{1,0:T(8,128)S(1)} %copy.23.qg_ref) | copy-start | bytes 1540
  43.0 37.2 %collective-permute-start.5 = (bf16[2,384,512]{2,1,0:T(8,128)(2,1)}, bf16[2,384,512]{2,1,0:T(8,128)(2,1)S(1)}, u32[]{:S(2)}, u32[]{:S(2)}) collective-permute-start(bf16[2,384,512]{2,1,0:T(8,128)(2,1)} %pad_maximum_fusion.1), channel_id=1, source_target_pairs={{0,32},{8,40},{16,48},{24,56},{32,64},{40,72},{48,80},{56,88},{64,... | collective-permute-start | bytes 2359304 | tf_op jit(solution)/shard_map/ppermute | solution.py:224
  58.7 49.6 %collective-permute-start.1 = (bf16[2,384,512]{2,1,0:T(8,128)(2,1)}, bf16[2,384,512]{2,1,0:T(8,128)(2,1)S(1)}, u32[]{:S(2)}, u32[]{:S(2)}) collective-permute-start(bf16[2,384,512]{2,1,0:T(8,128)(2,1)} %collective-permute-done.kv1), channel_id=1, source_target_pairs={{8,16},{0,24},{40,48},{32,56},{72,80},{64,88},{104,112},{96,120},{... | collective-permute-start | bytes 2359304 | tf_op jit(solution)/shard_map/ppermute | solution.py:221
  63.6 33.0 %collective-permute-start.4 = (bf16[2,384,512]{2,1,0:T(8,128)(2,1)}, bf16[2,384,512]{2,1,0:T(8,128)(2,1)S(1)}, u32[]{:S(2)}, u32[]{:S(2)}) collective-permute-start(bf16[2,384,512]{2,1,0:T(8,128)(2,1)} %collective-permute-done.3.kv1), channel_id=1, source_target_pairs={{8,16},{0,24},{40,48},{32,56},{72,80},{64,88},{104,112},{96,120},{... | collective-permute-start | bytes 2359304 | tf_op jit(solution)/shard_map/ppermute | solution.py:221
  65.0 1.3 copy-start.13
  66.3 1.3 copy-start.14
  68.7 27.9 %copy-start.15 = (bf16[1,384,1536]{2,1,0:T(8,128)(2,1)S(1)}, bf16[1,384,1536]{2,1,0:T(8,128)(2,1)}, u32[]{:S(2)}) copy-start(bf16[1,384,1536]{2,1,0:T(8,128)(2,1)} %param.13) | copy-start | bytes 3538948
  78.9 42.6 %collective-permute-start.15 = (bf16[2,384,512]{2,1,0:T(8,128)(2,1)S(1)}, bf16[2,384,512]{2,1,0:T(8,128)(2,1)S(1)}, u32[]{:S(2)}, u32[]{:S(2)}) collective-permute-start(bf16[2,384,512]{2,1,0:T(8,128)(2,1)S(1)} %get-tuple-element.52), channel_id=1, source_target_pairs={{24,0},{16,8},{56,32},{48,40},{88,64},{80,72},{120,96},{112,104},{... | collective-permute-start | bytes 2359304 | tf_op jit(solution)/shard_map/ppermute | solution.py:221
  97.5 10.7 %copy-start.19 = (s32[1,1,3]{2,1,0:T(1,128)S(1)}, s32[1,1,3]{2,1,0:T(1,128)}, u32[]{:S(2)}) copy-start(s32[1,1,3]{2,1,0:T(1,128)} %param.12) | copy-start | bytes 40
  106.7 30.4 %collective-permute-start.12 = (bf16[2,384,512]{2,1,0:T(8,128)(2,1)S(1)}, bf16[2,384,512]{2,1,0:T(8,128)(2,1)S(1)}, u32[]{:S(2)}, u32[]{:S(2)}) collective-permute-start(bf16[2,384,512]{2,1,0:T(8,128)(2,1)S(1)} %get-tuple-element.48), channel_id=1, source_target_pairs={{24,0},{16,8},{56,32},{48,40},{88,64},{80,72},{120,96},{112,104},{... | collective-permute-start | bytes 2359304 | tf_op jit(solution)/shard_map/ppermute | solution.py:221
  117.6 6.3 %copy-start.2 = (bf16[2,384,512]{2,1,0:T(8,128)(2,1)}, bf16[2,384,512]{2,1,0:T(8,128)(2,1)S(1)}, u32[]{:S(2)}) copy-start(bf16[2,384,512]{2,1,0:T(8,128)(2,1)S(1)} %get-tuple-element.42.own) | copy-start | bytes 2359300
  117.6 6.3 %copy-start.8 = (f32[128,384]{1,0:T(8,128)}, f32[128,384]{1,0:T(8,128)S(1)}, u32[]{:S(2)}) copy-start(f32[128,384]{1,0:T(8,128)S(1)} %get-tuple-element.62) | copy-start | bytes 589828
  117.6 40.3 %collective-permute-start.9 = (bf16[2,384,512]{2,1,0:T(8,128)(2,1)S(1)}, bf16[2,384,512]{2,1,0:T(8,128)(2,1)S(1)}, u32[]{:S(2)}, u32[]{:S(2)}) collective-permute-start(bf16[2,384,512]{2,1,0:T(8,128)(2,1)S(1)} %get-tuple-element.44), channel_id=1, source_target_pairs={{24,0},{16,8},{56,32},{48,40},{88,64},{80,72},{120,96},{112,104},{... | collective-permute-start | bytes 2359304 | tf_op jit(solution)/shard_map/ppermute | solution.py:221
  118.9 42.1 %collective-permute-start.17 = (bf16[2,384,512]{2,1,0:T(8,128)(2,1)S(1)}, bf16[2,384,512]{2,1,0:T(8,128)(2,1)S(1)}, u32[]{:S(2)}, u32[]{:S(2)}) collective-permute-start(bf16[2,384,512]{2,1,0:T(8,128)(2,1)S(1)} %get-tuple-element.53), channel_id=1, source_target_pairs={{32,0},{40,8},{48,16},{56,24},{64,32},{72,40},{80,48},{88,56},{96,... | collective-permute-start | bytes 2359304 | tf_op jit(solution)/shard_map/ppermute | solution.py:224
  120.2 165.8 %collective-permute-start.14 = (bf16[2,384,512]{2,1,0:T(8,128)(2,1)}, bf16[2,384,512]{2,1,0:T(8,128)(2,1)}, u32[]{:S(2)}, u32[]{:S(2)}) collective-permute-start(bf16[2,384,512]{2,1,0:T(8,128)(2,1)} %get-tuple-element.49), channel_id=1, source_target_pairs={{32,0},{40,8},{48,16},{56,24},{64,32},{72,40},{80,48},{88,56},{96,... | collective-permute-start | bytes 2359304 | tf_op jit(solution)/shard_map/ppermute | solution.py:224
  121.5 168.6 %collective-permute-start.11 = (bf16[2,384,512]{2,1,0:T(8,128)(2,1)}, bf16[2,384,512]{2,1,0:T(8,128)(2,1)S(1)}, u32[]{:S(2)}, u32[]{:S(2)}) collective-permute-start(bf16[2,384,512]{2,1,0:T(8,128)(2,1)} %get-tuple-element.45), channel_id=1, source_target_pairs={{32,0},{40,8},{48,16},{56,24},{64,32},{72,40},{80,48},{88,56},{96,... | collective-permute-start | bytes 2359304 | tf_op jit(solution)/shard_map/ppermute | solution.py:224
  137.2 142.8 %collective-permute-start.16 = (bf16[2,384,512]{2,1,0:T(8,128)(2,1)}, bf16[2,384,512]{2,1,0:T(8,128)(2,1)}, u32[]{:S(2)}, u32[]{:S(2)}) collective-permute-start(bf16[2,384,512]{2,1,0:T(8,128)(2,1)} %add_convert_fusion), channel_id=1, source_target_pairs={{0,8},{8,0},{24,16},{32,40},{40,32},{56,48},{64,72},{72,64},{88,80... | collective-permute-start | bytes 2359304 | tf_op jit(solution)/shard_map/ppermute | solution.py:221
  157.9 128.1 %collective-permute-start.13 = (bf16[2,384,512]{2,1,0:T(8,128)(2,1)}, bf16[2,384,512]{2,1,0:T(8,128)(2,1)}, u32[]{:S(2)}, u32[]{:S(2)}) collective-permute-start(bf16[2,384,512]{2,1,0:T(8,128)(2,1)} %add_convert_fusion.1), channel_id=1, source_target_pairs={{0,8},{8,0},{24,16},{32,40},{40,32},{56,48},{64,72},{72,64},{88,80... | collective-permute-start | bytes 2359304 | tf_op jit(solution)/shard_map/ppermute | solution.py:221
  159.8 6.2 %copy-start.9 = (f32[128,384]{1,0:T(8,128)S(1)}, f32[128,384]{1,0:T(8,128)}, u32[]{:S(2)}) copy-start(f32[128,384]{1,0:T(8,128)} %copy-done.8) | copy-start | bytes 589828
  161.9 128.2 %collective-permute-start.10 = (bf16[2,384,512]{2,1,0:T(8,128)(2,1)}, bf16[2,384,512]{2,1,0:T(8,128)(2,1)}, u32[]{:S(2)}, u32[]{:S(2)}) collective-permute-start(bf16[2,384,512]{2,1,0:T(8,128)(2,1)} %add_convert_fusion.2), channel_id=1, source_target_pairs={{0,8},{8,0},{24,16},{32,40},{40,32},{56,48},{64,72},{72,64},{88,80... | collective-permute-start | bytes 2359304 | tf_op jit(solution)/shard_map/ppermute | solution.py:221
  286.0 4.1 %copy-start.3 = (bf16[2,384,512]{2,1,0:T(8,128)(2,1)S(1)}, bf16[2,384,512]{2,1,0:T(8,128)(2,1)}, u32[]{:S(2)}) copy-start(bf16[2,384,512]{2,1,0:T(8,128)(2,1)} %copy-done.2) | copy-start | bytes 2359300
  (7 other events, 6.9 us)

commit v2 on v1

v2 whole, which is shorter than its diff:
```python
import functools
import math

import jax
import jax.numpy as jnp
from jax import lax
from jax.experimental import pallas as pl
from jax.experimental.pallas import tpu as pltpu
from jax.sharding import PartitionSpec as P

HEAD_DIM = 128
ROW = 4
SPLITS = (4, 4, 4)
Z_KEYS = ((0,), (1, 2))
Z_TERMS = ((0, 1), (2,))
RELAY_KEYS = (True, True, True)
RELAY_TERMS = (True, True, False)
ORDERED = True
CLOSE_BEFORE = {}
CLOSE_AFTER = (0, 1)
CLOSE_LAST = (2,)
RADIX = {"dp": 2, "seq": 4}
TAIL = ((0, ("on",)), (3, ("y", "z", "c")))
ATTN_COST = 4_000_000_000
CLOSE_COST = 1_000_000_000
F32 = jnp.float32
BF16 = jnp.bfloat16
MIB = 2**20

KEYS_OUT = ((0, 1), (1, 0), (2, 3))
KEYS_ON = ((1, 2), (0, 3))
TERMS_OUT = ((3, 0), (2, 1))
TERMS_ON = ((0, 1), (1, 0), (3, 2))
STEP_ONE = ((0, 1), (2, 3))
STEP_TWO = ((0, 2), (1, 3))


def dot(a, b):
    return lax.dot_general(a, b, (((1,), (0,)), ((), ())), preferred_element_type=F32)


def unit_rows(block):
    flat = block.astype(F32)
    root = lax.rsqrt(jnp.mean(flat * flat, axis=1, keepdims=True) + 1e-6)
    return flat * root, root


def attn_kernel(per_step, begun, win, q_ref, k_ref, v_ref, g_ref, kv1, kv2, kv4, qg_ref, kg_ref, *refs):
    (out_ref, gq_ref, own_ref, t1_ref, t2_ref, t4_ref, qsum_ref, ksum_ref) = refs[-8:]
    scale = HEAD_DIM ** (-0.5)
    to_two = scale * math.log2(math.e)

    @pl.when(pl.program_id(0) == 0)
    def _():
        qsum_ref[...] = refs[0][...] if begun else jnp.zeros_like(qsum_ref)
        ksum_ref[...] = refs[1][...] if begun else jnp.zeros_like(ksum_ref)

    q_gain = qg_ref[...]
    k_gain = kg_ref[...]
    held = [True] + [win[j] >= 0 for j in range(3)]
    terms = (own_ref, t1_ref, t2_ref, t4_ref)
    for at in range(per_step):
        cols = slice(at * HEAD_DIM, (at + 1) * HEAD_DIM)
        qt = q_ref[:, cols].T.astype(F32)
        q_root = lax.rsqrt(jnp.mean(qt * qt, axis=0, keepdims=True) + 1e-6)
        q_unit = qt * q_root
        qt_b = (q_unit * q_gain).astype(BF16)
        q_b = qt_b.T
        g_b = g_ref[:, cols]
        gt_b = g_b.T
        keys = [k_ref[:, cols]] + [ref[0, :, cols] for ref in (kv1, kv2, kv4)]
        vals = [v_ref[:, cols]] + [ref[1, :, cols] for ref in (kv1, kv2, kv4)]

        k_norm, scores, tops = [], [], []
        for j in range(4):
            k_norm.append((unit_rows(keys[j])[0] * k_gain).astype(BF16))
            scores.append(dot(k_norm[j], qt_b))
            top = jnp.max(scores[j], axis=0, keepdims=True)
            tops.append(top if j == 0 else jnp.where(held[j], top, -jnp.inf))
        row_max = functools.reduce(jnp.maximum, tops) * to_two
        raw, sums, dps = [], [], []
        for j in range(4):
            dps.append(dot(vals[j], gt_b))
            factor = to_two if j == 0 else jnp.where(held[j], to_two, 0.0)
            less = row_max if j == 0 else jnp.where(held[j], row_max, 1e30)
            raw.append(jnp.exp2(scores[j] * factor - less))
            sums.append(jnp.sum(raw[j], axis=0, keepdims=True))
        inverse = 1.0 / functools.reduce(jnp.add, sums)
        out = None
        for j in range(4):
            probs_low = (raw[j] * inverse).astype(BF16)
            terms[j][at, 1] = dot(probs_low, g_b).astype(BF16)
            o = dot(vals[j].T, probs_low)
            out = o if j == 0 else out + o
        out_low = out.astype(BF16)
        out_ref[:, cols] = out_low.T
        row_dot = jnp.sum(gt_b.astype(F32) * out_low.astype(F32), axis=0, keepdims=True)
        scaled_inverse = inverse * scale
        dq = None
        k_part = None
        for j in range(4):
            ds = (raw[j] * ((dps[j] - row_dot) * scaled_inverse)).astype(BF16)
            d = dot(k_norm[j].T, ds)
            dq = d if j == 0 else dq + d
            dk = dot(ds, q_b).astype(BF16)
            terms[j][at, 0] = dk
            part = jnp.sum((dk.astype(F32) * unit_rows(keys[j])[0]).reshape(-1, 8, HEAD_DIM), axis=0)
            k_part = part if j == 0 else k_part + part
        ksum_ref[...] += k_part
        qsum_ref[...] += dq * q_unit
        scaled = dq * q_gain
        inner = jnp.mean(scaled * q_unit, axis=0, keepdims=True)
        gq_ref[:, cols] = (q_root * (scaled - q_unit * inner)).astype(BF16).T


def attn_part(first, heads, win, q, k, v, g, pairs, z_at, q_gain, k_gain, filled, t4_shape, t4_at, t4_filled, totals):
    rows, width = q.shape
    per_step = next(n for n in (2, 1) if not any(x % n for x in (first, heads, z_at, t4_at)))
    wide = per_step * HEAD_DIM
    whole = pl.BlockSpec((rows, wide), lambda h: (0, first // per_step + h))
    smem = pl.BlockSpec(memory_space=pltpu.SMEM)
    hbm = pl.BlockSpec(memory_space=pl.ANY)

    def two_at(start):
        return pl.BlockSpec((per_step, 2, rows, HEAD_DIM), lambda h: (start // per_step + h, 0, 0, 0))

    def keys_at(start):
        return pl.BlockSpec((2, rows, wide), lambda h: (0, 0, start // per_step + h))

    def const(shape):
        return pl.BlockSpec(shape, lambda h: (0, 0))

    full = jax.ShapeDtypeStruct((rows, width), BF16)
    pair = jax.ShapeDtypeStruct((heads, 2, rows, HEAD_DIM), BF16)
    sums = [(HEAD_DIM, rows), (8, HEAD_DIM)]
    begun = totals is not None
    more = list(totals) if begun else []
    more_specs = [const(x) for x in sums] if begun else []
    kept = {6: 10, 7: 11} if begun else {}
    for out, array in ((0, filled and filled[0]), (1, filled and filled[1]), (5, t4_filled)):
        if array is not None:
            kept[out] = 10 + len(more)
            more.append(array)
            more_specs.append(hbm)
    return pl.pallas_call(
        functools.partial(attn_kernel, per_step, begun),
        grid=(heads // per_step,),
        in_specs=[smem, whole, whole, whole, whole, keys_at(0), keys_at(0), keys_at(z_at)]
        + [const((HEAD_DIM, 1)), const((1, HEAD_DIM))]
        + more_specs,
        out_specs=[whole, whole, two_at(0), two_at(0), two_at(0), two_at(t4_at)] + [const(x) for x in sums],
        out_shape=[
            full,
            full,
            pair,
            pair,
            pair,
            jax.ShapeDtypeStruct((t4_shape, 2, rows, HEAD_DIM), BF16),
            *[jax.ShapeDtypeStruct(x, F32) for x in sums],
        ],
        input_output_aliases={where: out for out, where in kept.items()},
        compiler_params=pltpu.CompilerParams(
            dimension_semantics=("arbitrary",), vmem_limit_bytes=58 * MIB
        ),
        cost_estimate=pl.CostEstimate(
            flops=heads * ATTN_COST,
            bytes_accessed=heads * ATTN_COST // 1000,
            transcendentals=0,
        ),
        name="attention_part",
    )(win, q, k, v, g, *pairs, q_gain.reshape(HEAD_DIM, 1), k_gain.reshape(1, HEAD_DIM), *more)


def close_kernel(count, k_ref, *refs):
    got, kg_ref, (gk_ref, gv_ref) = refs[:count], refs[count], refs[-2:]
    dk, dv = (functools.reduce(jnp.add, [r[0, i].astype(F32) for r in got]) for i in range(2))
    gv_ref[...] = dv.astype(BF16)
    unit, root = unit_rows(k_ref[...])
    scaled = dk * kg_ref[...]
    inner = jnp.mean(scaled * unit, axis=1, keepdims=True)
    gk_ref[...] = (root * (scaled - unit * inner)).astype(BF16)


def close_part(first, heads, k, got, z_at, k_gain, filled):
    rows, width = k.shape
    whole = pl.BlockSpec((rows, HEAD_DIM), lambda h: (0, first + h))
    two = pl.BlockSpec((1, 2, rows, HEAD_DIM), lambda h: (h, 0, 0, 0))
    two_z = pl.BlockSpec((1, 2, rows, HEAD_DIM), lambda h: (z_at + h, 0, 0, 0))
    hbm = pl.BlockSpec(memory_space=pl.ANY)
    full = jax.ShapeDtypeStruct((rows, width), BF16)
    filled = () if filled is None else filled
    count = len(got)
    return pl.pallas_call(
        functools.partial(close_kernel, count),
        grid=(heads,),
        in_specs=[whole] + [two] * (count - 1) + [two_z] + [pl.BlockSpec((1, HEAD_DIM), lambda h: (0, 0))] + [hbm] * len(filled),
        out_specs=[whole, whole],
        out_shape=[full, full],
        input_output_aliases={2 + count + i: i for i in range(len(filled))},
        compiler_params=pltpu.CompilerParams(dimension_semantics=("arbitrary",), vmem_limit_bytes=58 * MIB),
        cost_estimate=pl.CostEstimate(
            flops=heads * CLOSE_COST,
            bytes_accessed=heads * CLOSE_COST // 1000,
            transcendentals=0,
        ),
        name="close_part",
    )(k, *got, k_gain.reshape(1, HEAD_DIM), *filled)


def total_over_mesh(block, waits):
    def spread(x, axis, size, stride, group):
        def peer(i, d):
            at = i // stride % group
            return i + ((at ^ d) - at) * stride

        got = [x] + [lax.ppermute(x, axis, [(i, peer(i, d)) for i in range(size)]) for d in range(1, group)]
        while len(got) > 1:
            got = [a + b for a, b in zip(got[::2], got[1::2])]
        return got[0]

    def whole_axis(x, axis, size):
        stride = 1
        while stride < size:
            group = 4 if RADIX[axis] == 4 and size // stride % 4 == 0 else 2
            x = spread(after(x, *waits.pop(0)), axis, size, stride, group)
            stride *= group
        return x

    block = whole_axis(block, "dp", lax.axis_size("dp"))
    return whole_axis(block, "seq", lax.axis_size("seq"))


def after(block, *others):
    return lax.optimization_barrier((block,) + others)[0] if ORDERED and others else block


def on_device(q_in, k_in, v_in, q_gain, k_gain, window, grad_out):
    q, k, v, g = q_in[0], k_in[0], v_in[0], grad_out[0]
    rows = q.shape[0]
    win = window[0, 0]
    tiles = lax.axis_size("seq")
    starts = range(0, tiles, ROW)

    def in_row(block, hops):
        return lax.ppermute(block, "seq", [(s + a, s + b) for s in starts for a, b in hops])

    def frames(block, step):
        return lax.ppermute(
            block, "seq", [(t, t + step) for t in range(tiles) if 0 <= t + step < tiles]
        )

    def back_of(hops):
        return tuple((b, a) for a, b in hops)

    firsts = [sum(SPLITS[:i]) for i in range(len(SPLITS))]
    parts = range(len(SPLITS))
    last = len(SPLITS) - 1
    near, far, back, outs, onward, sent, got_z = {}, {}, {}, {}, {}, {}, {}

    def place(groups, i):
        group = next(g for g in groups if i in g)
        sizes = [SPLITS[j] for j in group]
        return group, sum(sizes), sum(sizes[: group.index(i)])

    def pack(first, heads):
        cols = slice(first * HEAD_DIM, (first + heads) * HEAD_DIM)
        return jnp.stack([x[:, cols] for x in (k, v)])

    for i in parts:
        mine = pack(firsts[i], SPLITS[i])
        along = mine if i == 0 else after(mine, near[i - 1])
        group, heads, _ = place(Z_KEYS, i)
        if i == group[0]:
            ours = mine if heads == SPLITS[i] else pack(firsts[i], heads)
            if i > 0:
                ours = after(ours, *list(back.values())[-1:], near[max(group[0] - 1, 0)])
            back[group] = frames(ours, ROW)
        if RELAY_KEYS[i]:
            near[i] = in_row(along, KEYS_OUT)
            far[i] = in_row(near[i], KEYS_ON)
        else:
            near[i] = in_row(along, STEP_ONE)
            far[i] = in_row(along, STEP_TWO)

    vias = {}

    def relay(i, *tokens):
        own, to_near = outs[i][2:4]
        if i in vias:
            via = after(vias[i], *tokens)
            onward[i] = (to_near.astype(F32) + via.astype(F32)).astype(BF16)
            sent[i] = (own, in_row(onward[i], TERMS_ON))

    def send(i):
        own, to_near, to_far, to_back = outs[i][2:6]
        if RELAY_TERMS[i]:
            vias[i] = in_row(to_far, TERMS_OUT)
        else:
            got_far = in_row(to_far, back_of(STEP_TWO))
            sent[i] = (own, in_row(to_near, back_of(STEP_ONE)), got_far)
        group = place(Z_TERMS, i)[0]
        if i == group[-1]:
            got_z[group] = frames(to_back, -ROW)

    closed = None

    def close(i):
        nonlocal closed
        group, _, at = place(Z_TERMS, i)
        closed = tuple(close_part(firsts[i], SPLITS[i], k, sent[i] + (got_z[group],), at, k_gain, closed))

    filled, t4 = None, None
    for i in parts:
        tokens = [near[i + 1]] if i + 1 in near else []
        if i >= 2:
            relay(i - 2, outs[i - 1][7])
        if i - 2 in onward:
            tokens.append(onward[i - 2])
        for j in CLOSE_BEFORE.get(i, ()):
            close(j)
            tokens.append(closed[0])
        z_group, _, z_at = place(Z_KEYS, i)
        group, t4_heads, t4_at = place(Z_TERMS, i)
        outs[i] = attn_part(
            firsts[i], SPLITS[i], after(win, *tokens), q, k, v, g, (near[i], far[i], back[z_group]), z_at,
            q_gain, k_gain, filled, t4_heads, t4_at, t4 if t4_at else None, outs[i - 1][6:8] if i else None,
        )
        filled, t4 = tuple(outs[i][:2]), outs[i][5]
        send(i)
    relay(last - 1, *([outs[last][7]] if last > 0 else []))
    relay(last)
    gains = jnp.stack([jnp.sum(outs[last][6], axis=1), jnp.sum(outs[last][7], axis=0)])
    for i in CLOSE_AFTER:
        close(i)
    waits = [()] * 8
    known = {"on": onward.get(last - 1), "z": got_z[Z_TERMS[-1]], "y": sent[last][1:], "c": closed and closed[0], "tn": sent[max(last - 2, 0)][1]}
    for stage, names in TAIL:
        waits[stage] = tuple(jax.tree.leaves([known[n] for n in names]))
    for i in CLOSE_LAST:
        close(i)
    gains = total_over_mesh(gains, waits)
    return (filled[0][None], filled[1][None], closed[0][None], closed[1][None], gains[0], gains[1])


def solution(mesh):
    rows = P("dp", "seq", None)
    return jax.shard_map(
        on_device,
        mesh=mesh,
        in_specs=(rows, rows, rows, P(), P(), rows, rows),
        out_specs=(rows, rows, rows, rows, P(), P()),
        check_vma=False,
    )
```

time: 298 us -> 194 us (0.65); the launches traced: 294 us -> 193 us
  blocking collectives: 113 us -> 0 us
  starting transfers between devices: 50.5 us -> 82.2 us
  waiting for transfers between devices: 71.2 us -> 44.2 us
  Pallas kernels: 39.5 us -> 57 us
  local copies, waits for them, and re-layouts: 12 us -> 6.24 us
  other arithmetic: 6.58 us -> 2.69 us
    psum x1 -> x0, blocking collectives: 113 us -> none  [on_device(): gains = lax.psum(gains, ('seq', 'dp'))]
    ppermute x12, waiting for transfers between devices: 71.2 us -> 26.6 us  [in_row(): lax.ppermute(block, 'seq', [(s + a, s + b) for s in starts for a, b in ho...]
    ppermute x0 -> x10, starting transfers between devices: none -> 35.9 us  [spread(): lax.ppermute(x, axis, [(i, peer(i, d)) for i in range(size)])]
    pallas_call x6, Pallas kernels: 39.5 us -> 57 us  [the longest x3 44.3 us: attn_part(): pl.pallas_call(functools.partial(attn_kernel, per_step, begun), grid=(hea...]
    ppermute x0 -> x10, waiting for transfers between devices: none -> 12.5 us  [spread(): lax.ppermute(x, axis, [(i, peer(i, d)) for i in range(size)])]
    unnamed x42 -> x26, local copies, waits for them, and re-layouts: 9.47 us -> 2.96 us
    ppermute x6 -> x4, waiting for transfers between devices: 0.02 us -> 5.1 us  [frames(): lax.ppermute(block, 'seq', [(t, t + step) for t in range(tiles) if 0 <= t...]
    ppermute x6 -> x4, starting transfers between devices: 17.2 us -> 12.6 us  [frames(): lax.ppermute(block, 'seq', [(t, t + step) for t in range(tiles) if 0 <= t...]
  transfers between devices with their start and end apart: 18 -> 26, of which waited for: 6 -> 11; matrix products, arithmetic and copies ran while one was open for 2% -> 1% of each run, Pallas kernels for 12% -> 29%
where the time goes in v2:
time: 194 us; the launch traced here: 193 us
  starting transfers between devices  82.2 us (42%)
  Pallas kernels  57 us (29%)
  waiting for transfers between devices  44.2 us (23%)
  local copies, waits for them, and re-layouts  6.24 us (3%)
  other arithmetic  2.69 us (1%)
    pallas_call x3, Pallas kernels, attn_part(): pl.pallas_call(functools.partial(attn_kernel, per_step, begun), grid=(hea...  44.3 us
    ppermute x10, starting transfers between devices, spread(): lax.ppermute(x, axis, [(i, peer(i, d)) for i in range(size)])  35.9 us
    ppermute x12, starting transfers between devices, in_row(): lax.ppermute(block, 'seq', [(s + a, s + b) for s in starts for a, b in ho...  33.7 us
    ppermute x12, waiting for transfers between devices, in_row(): lax.ppermute(block, 'seq', [(s + a, s + b) for s in starts for a, b in ho...  26.6 us
    pallas_call x3, Pallas kernels, close_part(): pl.pallas_call(functools.partial(close_kernel, count), grid=(heads,), in_...  12.6 us
    ppermute x4, starting transfers between devices, frames(): lax.ppermute(block, 'seq', [(t, t + step) for t in range(tiles) if 0 <= t...  12.6 us
    ppermute x10, waiting for transfers between devices, spread(): lax.ppermute(x, axis, [(i, peer(i, d)) for i in range(size)])  12.5 us
    ppermute x4, waiting for transfers between devices, frames(): lax.ppermute(block, 'seq', [(t, t + step) for t in range(tiles) if 0 <= t...  5.1 us
  transfers between devices with their start and end apart: 26, of which 11 were waited for; matrix products, arithmetic and copies ran while one was open for 1% of the time, Pallas kernels for 29%

profile of v2, /device:TPU:4, one launch (start us, length us, event | category | flops | bytes accessed | tf_op | source)
XLA Modules:
  0.0 193.2 jit_solution(13375242946260543618)
XLA Ops:
  0.6 1.8 slice_bitcast_fusion.2
  3.4 3.6 %collective-permute-start = (bf16[2,384,512]{2,1,0:T(8,128)(2,1)}, bf16[2,384,512]{2,1,0:T(8,128)(2,1)}, u32[]{:S(2)}, u32[]{:S(2)}) collective-permute-start(bf16[2,384,512]{2,1,0:T(8,128)(2,1)} %pad_maximum_fusion.2), channel_id=1, source_target_pairs={{0,8},{8,0},{16,24},{32,40},{40,32},{48,56},{64,72},{72,64},{80,88... | collective-permute-start | bytes 2359304 | tf_op jit(solution)/shard_map/ppermute | solution.py:245
  7.1 4.8 %collective-permute-start.3 = (bf16[2,384,512]{2,1,0:T(8,128)(2,1)}, bf16[2,384,512]{2,1,0:T(8,128)(2,1)}, u32[]{:S(2)}, u32[]{:S(2)}) collective-permute-start(bf16[2,384,512]{2,1,0:T(8,128)(2,1)} %pad_maximum_fusion.2), channel_id=1, source_target_pairs={{0,32},{8,40},{16,48},{24,56},{32,64},{40,72},{48,80},{56,88},{64,... | collective-permute-start | bytes 2359304 | tf_op jit(solution)/shard_map/ppermute | solution.py:248
  12.8 12.3 %collective-permute-done.kv1 = bf16[2,384,512]{2,1,0:T(8,128)(2,1)} collective-permute-done((bf16[2,384,512]{2,1,0:T(8,128)(2,1)}, bf16[2,384,512]{2,1,0:T(8,128)(2,1)}, u32[]{:S(2)}, u32[]{:S(2)}) %collective-permute-start) | collective-permute-done | bytes 786464 | tf_op jit(solution)/shard_map/ppermute | solution.py:245
  25.1 3.5 %collective-permute-start.1 = (bf16[2,384,512]{2,1,0:T(8,128)(2,1)}, bf16[2,384,512]{2,1,0:T(8,128)(2,1)}, u32[]{:S(2)}, u32[]{:S(2)}) collective-permute-start(bf16[2,384,512]{2,1,0:T(8,128)(2,1)} %pad_maximum_fusion.1), channel_id=1, source_target_pairs={{0,8},{8,0},{16,24},{32,40},{40,32},{48,56},{64,72},{72,64},{80,88... | collective-permute-start | bytes 2359304 | tf_op jit(solution)/shard_map/ppermute | solution.py:245
  28.5 3.7 %collective-permute-start.2 = (bf16[2,384,512]{2,1,0:T(8,128)(2,1)}, bf16[2,384,512]{2,1,0:T(8,128)(2,1)}, u32[]{:S(2)}, u32[]{:S(2)}) collective-permute-start(bf16[2,384,512]{2,1,0:T(8,128)(2,1)} %collective-permute-done.kv1), channel_id=1, source_target_pairs={{8,16},{0,24},{40,48},{32,56},{72,80},{64,88},{104,112},{96,120},{... | collective-permute-start | bytes 2359304 | tf_op jit(solution)/shard_map/ppermute | solution.py:245
  33.3 5.0 %collective-permute-start.7 = (bf16[2,384,1024]{2,1,0:T(8,128)(2,1)S(1)}, bf16[2,384,1024]{2,1,0:T(8,128)(2,1)}, u32[]{:S(2)}, u32[]{:S(2)}) collective-permute-start(bf16[2,384,1024]{2,1,0:T(8,128)(2,1)S(1)} %pad_maximum_fusion), channel_id=1, source_target_pairs={{0,32},{8,40},{16,48},{24,56},{32,64},{40,72},{48,80},{56,88},{64,... | collective-permute-start | bytes 4718600 | tf_op jit(solution)/shard_map/ppermute | solution.py:248
  38.4 7.3 %collective-permute-done.1.kv1 = bf16[2,384,512]{2,1,0:T(8,128)(2,1)} collective-permute-done((bf16[2,384,512]{2,1,0:T(8,128)(2,1)}, bf16[2,384,512]{2,1,0:T(8,128)(2,1)}, u32[]{:S(2)}, u32[]{:S(2)}) %collective-permute-start.1) | collective-permute-done | bytes 786464 | tf_op jit(solution)/shard_map/ppermute | solution.py:245
  45.7 3.5 %collective-permute-start.5 = (bf16[2,384,512]{2,1,0:T(8,128)(2,1)S(1)}, bf16[2,384,512]{2,1,0:T(8,128)(2,1)}, u32[]{:S(2)}, u32[]{:S(2)}) collective-permute-start(bf16[2,384,512]{2,1,0:T(8,128)(2,1)S(1)} %pad_maximum_fusion.3), channel_id=1, source_target_pairs={{0,8},{8,0},{16,24},{32,40},{40,32},{48,56},{64,72},{72,64},{80,88... | collective-permute-start | bytes 2359304 | tf_op jit(solution)/shard_map/ppermute | solution.py:245
  49.1 2.8 %collective-permute-start.6 = (bf16[2,384,512]{2,1,0:T(8,128)(2,1)}, bf16[2,384,512]{2,1,0:T(8,128)(2,1)S(1)}, u32[]{:S(2)}, u32[]{:S(2)}) collective-permute-start(bf16[2,384,512]{2,1,0:T(8,128)(2,1)} %collective-permute-done.1.kv1), channel_id=1, source_target_pairs={{8,16},{0,24},{40,48},{32,56},{72,80},{64,88},{104,112},{96,120},{... | collective-permute-start | bytes 2359304 | tf_op jit(solution)/shard_map/ppermute | solution.py:245
  51.9 14.7 %attention_part.3 = (bf16[384,1536]{1,0:T(8,128)(2,1)}, bf16[384,1536]{1,0:T(8,128)(2,1)}, bf16[4,2,384,128]{3,2,1,0:T(8,128)(2,1)}, bf16[4,2,384,128]{3,2,1,0:T...) custom-call(s32[3]{0:T(128)} %bitcast.55, ...), custom_call_target="tpu_custom_call" | custom-call | flops 16000000000 | bytes 16000000 | tf_op jit(solution)/shard_map/attention_part/pallas_call | solution.py:145
  67.9 6.0 %collective-permute-start.8 = (bf16[2,384,512]{2,1,0:T(8,128)(2,1)}, bf16[2,384,512]{2,1,0:T(8,128)(2,1)S(1)}, u32[]{:S(2)}, u32[]{:S(2)}) collective-permute-start(bf16[2,384,512]{2,1,0:T(8,128)(2,1)} %collective-permute-done.5.kv1), channel_id=1, source_target_pairs={{8,16},{0,24},{40,48},{32,56},{72,80},{64,88},{104,112},{96,120},{... | collective-permute-start | bytes 2359304 | tf_op jit(solution)/shard_map/ppermute | solution.py:245
  74.8 14.8 %attention_part.4 = (bf16[384,1536]{1,0:T(8,128)(2,1)}, bf16[384,1536]{1,0:T(8,128)(2,1)}, bf16[4,2,384,128]{3,2,1,0:T(8,128)(2,1)}, bf16[4,2,384,128]{3,2,1,0:T...) custom-call(s32[3]{0:T(128)} %bitcast.56, ...), custom_call_target="tpu_custom_call", output_to_operand_aliasing={{6}: (10, {}), {7}: (11, {}), {0}: (12, {}), {1}: (13, {}),... | custom-call | flops 16000000000 | bytes 16000000 | tf_op jit(solution)/shard_map/attention_part/pallas_call | solution.py:145
  89.9 3.6 %collective-permute-start.15 = (bf16[4,2,384,128]{3,2,1,0:T(8,128)(2,1)S(1)}, bf16[4,2,384,128]{3,2,1,0:T(8,128)(2,1)}, u32[]{:S(2)}, u32[]{:S(2)}) collective-permute-start(bf16[4,2,384,128]{3,2,1,0:T(8,128)(2,1)S(1)} %add_convert_fusion.1), channel_id=1, source_target_pairs={{0,8},{8,0},{24,16},{32,40},{40,32},{56,48},{64,72},{72,64},{88,80... | collective-permute-start | bytes 2359304 | tf_op jit(solution)/shard_map/ppermute | solution.py:245
  94.8 1.5 collective-permute-start.14
  97.3 14.9 %attention_part.5 = (bf16[384,1536]{1,0:T(8,128)(2,1)}, bf16[384,1536]{1,0:T(8,128)(2,1)}, bf16[4,2,384,128]{3,2,1,0:T(8,128)(2,1)}, bf16[4,2,384,128]{3,2,1,0:T...) custom-call(s32[3]{0:T(128)} %bitcast.57, ...), custom_call_target="tpu_custom_call", output_to_operand_aliasing={{6}: (10, {}), {7}: (11, {}), {0}: (12, {}), {1}: (13, {})} | custom-call | flops 16000000000 | bytes 16000000 | tf_op jit(solution)/shard_map/attention_part/pallas_call | solution.py:145
  113.2 1.9 collective-permute-start.13
  117.7 2.4 %collective-permute-done.17 = f32[2,128]{1,0:T(2,128)S(1)} collective-permute-done((f32[2,128]{1,0:T(2,128)S(1)}, f32[2,128]{1,0:T(2,128)S(1)}, u32[]{:S(2)}, u32[]{:S(2)}) %collective-permute-start.17) | collective-permute-done | bytes 1056 | tf_op jit(solution)/shard_map/ppermute | solution.py:216
  123.2 2.0 %collective-permute-done.18 = f32[2,128]{1,0:T(2,128)S(1)} collective-permute-done((f32[2,128]{1,0:T(2,128)S(1)}, f32[2,128]{1,0:T(2,128)S(1)}, u32[]{:S(2)}, u32[]{:S(2)}) %collective-permute-start.18) | collective-permute-done | bytes 1056 | tf_op jit(solution)/shard_map/ppermute | solution.py:216
  126.4 5.1 %collective-permute-done.14.refs_2_ = bf16[8,2,384,128]{3,2,1,0:T(8,128)(2,1)S(1)} collective-permute-done((bf16[8,2,384,128]{3,2,1,0:T(8,128)(2,1)}, bf16[8,2,384,128]{3,2,1,0:T(8,128)(2,1)S(1)}, u32[]{:S(2)}, u32[]{:S(2)}) %collective-permute-start.14) | collective-permute-done | bytes 1572896 | tf_op jit(solution)/shard_map/ppermute | solution.py:248
  132.7 4.1 %close_part.3 = (bf16[384,1536]{1,0:T(8,128)(2,1)}, bf16[384,1536]{1,0:T(8,128)(2,1)}) custom-call(bf16[384,1536]{1,0:T(8,128)(2,1)} %bitcast.42, bf16[4,2,384,128]{3,2,1,0:T(8,128)(2,1)} %get-tuple-element.76.refs_0_, bf16[4,2,384,128]{3,2,1,0:T(8,128)(2,1)} %collective-permute-done.15.refs_1_, bf16[8,2,384,128]{3,2,1,0:T(8,128)(2,1)} %copy-done.7, ...), custom_call_target="tpu_custom_call" | custom-call | flops 4000000000 | bytes 4000000 | tf_op jit(solution)/shard_map/close_part/pallas_call | solution.py:193
  136.8 4.1 %close_part.4 = (bf16[384,1536]{1,0:T(8,128)(2,1)}, bf16[384,1536]{1,0:T(8,128)(2,1)}) custom-call(bf16[384,1536]{1,0:T(8,128)(2,1)} %bitcast.43, bf16[4,2,384,128]{3,2,1,0:T(8,128)(2,1)} %get-tuple-element.70.refs_0_, bf16[4,2,384,128]{3,2,1,0:T(8,128)(2,1)} %collective-permute-done.13.refs_1_, ...), custom_call_target="tpu_custom_call", output_to_operand_aliasing={{0}: (5, {}), {1}: (6, {})} | custom-call | flops 4000000000 | bytes 4000000 | tf_op jit(solution)/shard_map/close_part/pallas_call | solution.py:193
  141.0 6.2 %collective-permute-done.9.refs_1_ = bf16[4,2,384,128]{3,2,1,0:T(8,128)(2,1)S(1)} collective-permute-done((bf16[4,2,384,128]{3,2,1,0:T(8,128)(2,1)}, bf16[4,2,384,128]{3,2,1,0:T(8,128)(2,1)S(1)}, u32[]{:S(2)}, u32[]{:S(2)}) %collective-permute-start.9) | collective-permute-done | bytes 786464 | tf_op jit(solution)/shard_map/ppermute | solution.py:245
  147.2 7.5 %collective-permute-start.20 = (f32[2,128]{1,0:T(2,128)S(1)}, f32[2,128]{1,0:T(2,128)S(1)}, u32[]{:S(2)}, u32[]{:S(2)}) collective-permute-start(f32[2,128]{1,0:T(2,128)S(1)} %add.40), channel_id=1, source_target_pairs={{0,16},{8,24},{16,0},{24,8},{32,48},{40,56},{48,32},{56,40},{64,80... | collective-permute-start | bytes 3080 | tf_op jit(solution)/shard_map/ppermute | solution.py:216
  154.8 14.5 %collective-permute-start.21 = (f32[2,128]{1,0:T(2,128)S(1)}, f32[2,128]{1,0:T(2,128)S(1)}, u32[]{:S(2)}, u32[]{:S(2)}) collective-permute-start(f32[2,128]{1,0:T(2,128)S(1)} %add.40), channel_id=1, source_target_pairs={{0,24},{8,16},{16,8},{24,0},{32,56},{40,48},{48,40},{56,32},{64,88... | collective-permute-start | bytes 3080 | tf_op jit(solution)/shard_map/ppermute | solution.py:216
  169.3 1.5 collective-permute-done.21
  170.8 2.0 %collective-permute-done.19 = f32[2,128]{1,0:T(2,128)S(1)} collective-permute-done((f32[2,128]{1,0:T(2,128)S(1)}, f32[2,128]{1,0:T(2,128)S(1)}, u32[]{:S(2)}, u32[]{:S(2)}) %collective-permute-start.19) | collective-permute-done | bytes 1056 | tf_op jit(solution)/shard_map/ppermute | solution.py:216
  172.9 3.9 %collective-permute-start.23 = (f32[2,128]{1,0:T(2,128)S(1)}, f32[2,128]{1,0:T(2,128)S(1)}, u32[]{:S(2)}, u32[]{:S(2)}) collective-permute-start(f32[2,128]{1,0:T(2,128)S(1)} %add_add_fusion.1), channel_id=1, source_target_pairs={{0,64},{8,72},{16,80},{24,88},{32,96},{40,104},{48,112},{56,120},{... | collective-permute-start | bytes 3080 | tf_op jit(solution)/shard_map/ppermute | solution.py:216
  176.8 1.4 collective-permute-start.24
  178.7 3.4 %collective-permute-done.24 = f32[2,128]{1,0:T(2,128)S(1)} collective-permute-done((f32[2,128]{1,0:T(2,128)S(1)}, f32[2,128]{1,0:T(2,128)S(1)}, u32[]{:S(2)}, u32[]{:S(2)}) %collective-permute-start.24) | collective-permute-done | bytes 1056 | tf_op jit(solution)/shard_map/ppermute | solution.py:216
  182.2 6.2 %collective-permute-start.25 = (f32[2,128]{1,0:T(2,128)S(1)}, f32[2,128]{1,0:T(2,128)S(1)}, u32[]{:S(2)}, u32[]{:S(2)}) collective-permute-start(f32[2,128]{1,0:T(2,128)S(1)} %add_add_fusion), channel_id=1, source_target_pairs={{0,128},{8,136},{16,144},{24,152},{32,160},{40,168},{48,176},{56,1... | collective-permute-start | bytes 3080 | tf_op jit(solution)/shard_map/ppermute | solution.py:216
  188.4 4.3 %close_part.5 = (bf16[384,1536]{1,0:T(8,128)(2,1)}, bf16[384,1536]{1,0:T(8,128)(2,1)}) custom-call(bf16[384,1536]{1,0:T(8,128)(2,1)} %bitcast.44, bf16[4,2,384,128]{3,2,1,0:T(8,128)(2,1)} %get-tuple-element.66.refs_0_, bf16[4,2,384,128]{3,2,1,0:T(8,128)(2,1)} %copy-done.8, ...), custom_call_target="tpu_custom_call", output_to_operand_aliasing={{0}: (6, {}), {1}: (7, {})} | custom-call | flops 4000000000 | bytes 4000000 | tf_op jit(solution)/shard_map/close_part/pallas_call | solution.py:193
  (71 shorter events, 17.8 us)
Async XLA Ops:
  2.5 30.5 %copy-start.1 = (bf16[1,384,1536]{2,1,0:T(8,128)(2,1)S(1)}, bf16[1,384,1536]{2,1,0:T(8,128)(2,1)}, u32[]{:S(2)}) copy-start(bf16[1,384,1536]{2,1,0:T(8,128)(2,1)} %param.8) | copy-start | bytes 3538948
  3.4 28.8 %copy-start.6 = (f32[128]{0:T(128)S(1)}, f32[128]{0:T(128)}, u32[]{:S(2)}) copy-start(f32[128]{0:T(128)} %param.10) | copy-start | bytes 1540
  3.4 29.5 %copy-start = (bf16[1,384,1536]{2,1,0:T(8,128)(2,1)S(1)}, bf16[1,384,1536]{2,1,0:T(8,128)(2,1)}, u32[]{:S(2)}) copy-start(bf16[1,384,1536]{2,1,0:T(8,128)(2,1)} %param.9) | copy-start | bytes 3538948
  3.4 21.6 %collective-permute-start = (bf16[2,384,512]{2,1,0:T(8,128)(2,1)}, bf16[2,384,512]{2,1,0:T(8,128)(2,1)}, u32[]{:S(2)}, u32[]{:S(2)}) collective-permute-start(bf16[2,384,512]{2,1,0:T(8,128)(2,1)} %pad_maximum_fusion.2), channel_id=1, source_target_pairs={{0,8},{8,0},{16,24},{32,40},{40,32},{48,56},{64,72},{72,64},{80,88... | collective-permute-start | bytes 2359304 | tf_op jit(solution)/shard_map/ppermute | solution.py:245
  7.1 26.3 %collective-permute-start.3 = (bf16[2,384,512]{2,1,0:T(8,128)(2,1)}, bf16[2,384,512]{2,1,0:T(8,128)(2,1)}, u32[]{:S(2)}, u32[]{:S(2)}) collective-permute-start(bf16[2,384,512]{2,1,0:T(8,128)(2,1)} %pad_maximum_fusion.2), channel_id=1, source_target_pairs={{0,32},{8,40},{16,48},{24,56},{32,64},{40,72},{48,80},{56,88},{64,... | collective-permute-start | bytes 2359304 | tf_op jit(solution)/shard_map/ppermute | solution.py:248
  25.1 20.6 %collective-permute-start.1 = (bf16[2,384,512]{2,1,0:T(8,128)(2,1)}, bf16[2,384,512]{2,1,0:T(8,128)(2,1)}, u32[]{:S(2)}, u32[]{:S(2)}) collective-permute-start(bf16[2,384,512]{2,1,0:T(8,128)(2,1)} %pad_maximum_fusion.1), channel_id=1, source_target_pairs={{0,8},{8,0},{16,24},{32,40},{40,32},{48,56},{64,72},{72,64},{80,88... | collective-permute-start | bytes 2359304 | tf_op jit(solution)/shard_map/ppermute | solution.py:245
  28.5 23.4 %collective-permute-start.2 = (bf16[2,384,512]{2,1,0:T(8,128)(2,1)}, bf16[2,384,512]{2,1,0:T(8,128)(2,1)}, u32[]{:S(2)}, u32[]{:S(2)}) collective-permute-start(bf16[2,384,512]{2,1,0:T(8,128)(2,1)} %collective-permute-done.kv1), channel_id=1, source_target_pairs={{8,16},{0,24},{40,48},{32,56},{72,80},{64,88},{104,112},{96,120},{... | collective-permute-start | bytes 2359304 | tf_op jit(solution)/shard_map/ppermute | solution.py:245
  33.3 40.6 %collective-permute-start.7 = (bf16[2,384,1024]{2,1,0:T(8,128)(2,1)S(1)}, bf16[2,384,1024]{2,1,0:T(8,128)(2,1)}, u32[]{:S(2)}, u32[]{:S(2)}) collective-permute-start(bf16[2,384,1024]{2,1,0:T(8,128)(2,1)S(1)} %pad_maximum_fusion), channel_id=1, source_target_pairs={{0,32},{8,40},{16,48},{24,56},{32,64},{40,72},{48,80},{56,88},{64,... | collective-permute-start | bytes 4718600 | tf_op jit(solution)/shard_map/ppermute | solution.py:248
  45.7 22.2 %collective-permute-start.5 = (bf16[2,384,512]{2,1,0:T(8,128)(2,1)S(1)}, bf16[2,384,512]{2,1,0:T(8,128)(2,1)}, u32[]{:S(2)}, u32[]{:S(2)}) collective-permute-start(bf16[2,384,512]{2,1,0:T(8,128)(2,1)S(1)} %pad_maximum_fusion.3), channel_id=1, source_target_pairs={{0,8},{8,0},{16,24},{32,40},{40,32},{48,56},{64,72},{72,64},{80,88... | collective-permute-start | bytes 2359304 | tf_op jit(solution)/shard_map/ppermute | solution.py:245
  49.1 24.8 %collective-permute-start.6 = (bf16[2,384,512]{2,1,0:T(8,128)(2,1)}, bf16[2,384,512]{2,1,0:T(8,128)(2,1)S(1)}, u32[]{:S(2)}, u32[]{:S(2)}) collective-permute-start(bf16[2,384,512]{2,1,0:T(8,128)(2,1)} %collective-permute-done.1.kv1), channel_id=1, source_target_pairs={{8,16},{0,24},{40,48},{32,56},{72,80},{64,88},{104,112},{96,120},{... | collective-permute-start | bytes 2359304 | tf_op jit(solution)/shard_map/ppermute | solution.py:245
  66.6 23.1 %collective-permute-start.4 = (bf16[4,2,384,128]{3,2,1,0:T(8,128)(2,1)}, bf16[4,2,384,128]{3,2,1,0:T(8,128)(2,1)S(1)}, u32[]{:S(2)}, u32[]{:S(2)}) collective-permute-start(bf16[4,2,384,128]{3,2,1,0:T(8,128)(2,1)} %get-tuple-element.49), channel_id=1, source_target_pairs={{24,0},{16,8},{56,32},{48,40},{88,64},{80,72},{120,96},{112,104},{... | collective-permute-start | bytes 2359304 | tf_op jit(solution)/shard_map/ppermute | solution.py:245
  67.9 28.4 %collective-permute-start.8 = (bf16[2,384,512]{2,1,0:T(8,128)(2,1)}, bf16[2,384,512]{2,1,0:T(8,128)(2,1)S(1)}, u32[]{:S(2)}, u32[]{:S(2)}) collective-permute-start(bf16[2,384,512]{2,1,0:T(8,128)(2,1)} %collective-permute-done.5.kv1), channel_id=1, source_target_pairs={{8,16},{0,24},{40,48},{32,56},{72,80},{64,88},{104,112},{96,120},{... | collective-permute-start | bytes 2359304 | tf_op jit(solution)/shard_map/ppermute | solution.py:245
  89.9 31.9 %collective-permute-start.15 = (bf16[4,2,384,128]{3,2,1,0:T(8,128)(2,1)S(1)}, bf16[4,2,384,128]{3,2,1,0:T(8,128)(2,1)}, u32[]{:S(2)}, u32[]{:S(2)}) collective-permute-start(bf16[4,2,384,128]{3,2,1,0:T(8,128)(2,1)S(1)} %add_convert_fusion.1), channel_id=1, source_target_pairs={{0,8},{8,0},{24,16},{32,40},{40,32},{56,48},{64,72},{72,64},{88,80... | collective-permute-start | bytes 2359304 | tf_op jit(solution)/shard_map/ppermute | solution.py:245
  93.5 19.4 %collective-permute-start.12 = (bf16[4,2,384,128]{3,2,1,0:T(8,128)(2,1)}, bf16[4,2,384,128]{3,2,1,0:T(8,128)(2,1)S(1)}, u32[]{:S(2)}, u32[]{:S(2)}) collective-permute-start(bf16[4,2,384,128]{3,2,1,0:T(8,128)(2,1)} %get-tuple-element.72), channel_id=1, source_target_pairs={{24,0},{16,8},{56,32},{48,40},{88,64},{80,72},{120,96},{112,104},{... | collective-permute-start | bytes 2359304 | tf_op jit(solution)/shard_map/ppermute | solution.py:245
  94.8 36.7 %collective-permute-start.14 = (bf16[8,2,384,128]{3,2,1,0:T(8,128)(2,1)}, bf16[8,2,384,128]{3,2,1,0:T(8,128)(2,1)S(1)}, u32[]{:S(2)}, u32[]{:S(2)}) collective-permute-start(bf16[8,2,384,128]{3,2,1,0:T(8,128)(2,1)} %get-tuple-element.75), channel_id=1, source_target_pairs={{32,0},{40,8},{48,16},{56,24},{64,32},{72,40},{80,48},{88,56},{96,... | collective-permute-start | bytes 4718600 | tf_op jit(solution)/shard_map/ppermute | solution.py:248
  113.2 23.7 %collective-permute-start.13 = (bf16[4,2,384,128]{3,2,1,0:T(8,128)(2,1)S(1)}, bf16[4,2,384,128]{3,2,1,0:T(8,128)(2,1)}, u32[]{:S(2)}, u32[]{:S(2)}) collective-permute-start(bf16[4,2,384,128]{3,2,1,0:T(8,128)(2,1)S(1)} %add_convert_fusion), channel_id=1, source_target_pairs={{0,8},{8,0},{24,16},{32,40},{40,32},{56,48},{64,72},{72,64},{88,80... | collective-permute-start | bytes 2359304 | tf_op jit(solution)/shard_map/ppermute | solution.py:245
  115.2 1.2 collective-permute-start.16
  116.5 3.6 %collective-permute-start.17 = (f32[2,128]{1,0:T(2,128)S(1)}, f32[2,128]{1,0:T(2,128)S(1)}, u32[]{:S(2)}, u32[]{:S(2)}) collective-permute-start(f32[2,128]{1,0:T(2,128)S(1)} %add.38), channel_id=1, source_target_pairs={{0,2},{1,3},{2,0},{3,1},{4,6},{5,7},{6,4},{7,5},{8,10},{9,11},{10,... | collective-permute-start | bytes 3080 | tf_op jit(solution)/shard_map/ppermute | solution.py:216
  120.1 5.1 %collective-permute-start.18 = (f32[2,128]{1,0:T(2,128)S(1)}, f32[2,128]{1,0:T(2,128)S(1)}, u32[]{:S(2)}, u32[]{:S(2)}) collective-permute-start(f32[2,128]{1,0:T(2,128)S(1)} %add.39), channel_id=1, source_target_pairs={{0,4},{1,5},{2,6},{3,7},{4,0},{5,1},{6,2},{7,3},{8,12},{9,13},{10,... | collective-permute-start | bytes 3080 | tf_op jit(solution)/shard_map/ppermute | solution.py:216
  120.6 26.6 %collective-permute-start.9 = (bf16[4,2,384,128]{3,2,1,0:T(8,128)(2,1)}, bf16[4,2,384,128]{3,2,1,0:T(8,128)(2,1)S(1)}, u32[]{:S(2)}, u32[]{:S(2)}) collective-permute-start(bf16[4,2,384,128]{3,2,1,0:T(8,128)(2,1)} %get-tuple-element.67), channel_id=1, source_target_pairs={{8,0},{24,16},{40,32},{56,48},{72,64},{88,80},{104,96},{120,112},{... | collective-permute-start | bytes 2359304 | tf_op jit(solution)/shard_map/ppermute | solution.py:245
  121.9 25.4 %collective-permute-start.10 = (bf16[4,2,384,128]{3,2,1,0:T(8,128)(2,1)}, bf16[4,2,384,128]{3,2,1,0:T(8,128)(2,1)S(1)}, u32[]{:S(2)}, u32[]{:S(2)}) collective-permute-start(bf16[4,2,384,128]{3,2,1,0:T(8,128)(2,1)} %get-tuple-element.68), channel_id=1, source_target_pairs={{16,0},{24,8},{48,32},{56,40},{80,64},{88,72},{112,96},{120,104},{... | collective-permute-start | bytes 2359304 | tf_op jit(solution)/shard_map/ppermute | solution.py:245
  125.1 22.1 %collective-permute-start.11 = (bf16[4,2,384,128]{3,2,1,0:T(8,128)(2,1)}, bf16[4,2,384,128]{3,2,1,0:T(8,128)(2,1)S(1)}, u32[]{:S(2)}, u32[]{:S(2)}) collective-permute-start(bf16[4,2,384,128]{3,2,1,0:T(8,128)(2,1)} %get-tuple-element.69), channel_id=1, source_target_pairs={{32,0},{40,8},{48,16},{56,24},{64,32},{72,40},{80,48},{88,56},{96,... | collective-permute-start | bytes 2359304 | tf_op jit(solution)/shard_map/ppermute | solution.py:248
  147.2 41.2 %copy-start.8 = (bf16[4,2,384,128]{3,2,1,0:T(8,128)(2,1)}, bf16[4,2,384,128]{3,2,1,0:T(8,128)(2,1)S(1)}, u32[]{:S(2)}) copy-start(bf16[4,2,384,128]{3,2,1,0:T(8,128)(2,1)S(1)} %collective-permute-done.9.refs_1_) | copy-start | bytes 2359300
  147.2 41.2 %copy-start.9 = (bf16[4,2,384,128]{3,2,1,0:T(8,128)(2,1)}, bf16[4,2,384,128]{3,2,1,0:T(8,128)(2,1)S(1)}, u32[]{:S(2)}) copy-start(bf16[4,2,384,128]{3,2,1,0:T(8,128)(2,1)S(1)} %collective-permute-done.10.refs_2_) | copy-start | bytes 2359300
  147.2 41.2 %copy-start.10 = (bf16[4,2,384,128]{3,2,1,0:T(8,128)(2,1)}, bf16[4,2,384,128]{3,2,1,0:T(8,128)(2,1)S(1)}, u32[]{:S(2)}) copy-start(bf16[4,2,384,128]{3,2,1,0:T(8,128)(2,1)S(1)} %collective-permute-done.11.refs_3_) | copy-start | bytes 2359300
  147.2 22.1 %collective-permute-start.20 = (f32[2,128]{1,0:T(2,128)S(1)}, f32[2,128]{1,0:T(2,128)S(1)}, u32[]{:S(2)}, u32[]{:S(2)}) collective-permute-start(f32[2,128]{1,0:T(2,128)S(1)} %add.40), channel_id=1, source_target_pairs={{0,16},{8,24},{16,0},{24,8},{32,48},{40,56},{48,32},{56,40},{64,80... | collective-permute-start | bytes 3080 | tf_op jit(solution)/shard_map/ppermute | solution.py:216
  154.8 16.1 %collective-permute-start.21 = (f32[2,128]{1,0:T(2,128)S(1)}, f32[2,128]{1,0:T(2,128)S(1)}, u32[]{:S(2)}, u32[]{:S(2)}) collective-permute-start(f32[2,128]{1,0:T(2,128)S(1)} %add.40), channel_id=1, source_target_pairs={{0,24},{8,16},{16,8},{24,0},{32,56},{40,48},{48,40},{56,32},{64,88... | collective-permute-start | bytes 3080 | tf_op jit(solution)/shard_map/ppermute | solution.py:216
  169.3 3.6 %collective-permute-start.19 = (f32[2,128]{1,0:T(2,128)S(1)}, f32[2,128]{1,0:T(2,128)S(1)}, u32[]{:S(2)}, u32[]{:S(2)}) collective-permute-start(f32[2,128]{1,0:T(2,128)S(1)} %add.40), channel_id=1, source_target_pairs={{0,8},{8,0},{16,24},{24,16},{32,40},{40,32},{48,56},{56,48},{64,72... | collective-permute-start | bytes 3080 | tf_op jit(solution)/shard_map/ppermute | solution.py:216
  172.9 5.8 %collective-permute-start.23 = (f32[2,128]{1,0:T(2,128)S(1)}, f32[2,128]{1,0:T(2,128)S(1)}, u32[]{:S(2)}, u32[]{:S(2)}) collective-permute-start(f32[2,128]{1,0:T(2,128)S(1)} %add_add_fusion.1), channel_id=1, source_target_pairs={{0,64},{8,72},{16,80},{24,88},{32,96},{40,104},{48,112},{56,120},{... | collective-permute-start | bytes 3080 | tf_op jit(solution)/shard_map/ppermute | solution.py:216
  176.8 5.4 %collective-permute-start.24 = (f32[2,128]{1,0:T(2,128)S(1)}, f32[2,128]{1,0:T(2,128)S(1)}, u32[]{:S(2)}, u32[]{:S(2)}) collective-permute-start(f32[2,128]{1,0:T(2,128)S(1)} %add_add_fusion.1), channel_id=1, source_target_pairs={{0,96},{8,104},{16,112},{24,120},{32,64},{40,72},{48,80},{56,88},{... | collective-permute-start | bytes 3080 | tf_op jit(solution)/shard_map/ppermute | solution.py:216
  178.2 3.9 %collective-permute-start.22 = (f32[2,128]{1,0:T(2,128)S(1)}, f32[2,128]{1,0:T(2,128)S(1)}, u32[]{:S(2)}, u32[]{:S(2)}) collective-permute-start(f32[2,128]{1,0:T(2,128)S(1)} %add_add_fusion.1), channel_id=1, source_target_pairs={{0,32},{8,40},{16,48},{24,56},{32,0},{40,8},{48,16},{56,24},{64,96... | collective-permute-start | bytes 3080 | tf_op jit(solution)/shard_map/ppermute | solution.py:216
  182.2 10.6 %collective-permute-start.25 = (f32[2,128]{1,0:T(2,128)S(1)}, f32[2,128]{1,0:T(2,128)S(1)}, u32[]{:S(2)}, u32[]{:S(2)}) collective-permute-start(f32[2,128]{1,0:T(2,128)S(1)} %add_add_fusion), channel_id=1, source_target_pairs={{0,128},{8,136},{16,144},{24,152},{32,160},{40,168},{48,176},{56,1... | collective-permute-start | bytes 3080 | tf_op jit(solution)/shard_map/ppermute | solution.py:216
  (7 other events, 37.8 us)

commit v3 on v2

--- a/solution.py
+++ b/solution.py
@@ -14,13 +14,13 @@
 Z_KEYS = ((0,), (1, 2))
 Z_TERMS = ((0, 1), (2,))
 RELAY_KEYS = (True, True, True)
-RELAY_TERMS = (True, True, False)
+RELAY_TERMS = (True, True, True)
 ORDERED = True
 CLOSE_BEFORE = {}
 CLOSE_AFTER = (0, 1)
 CLOSE_LAST = (2,)
-RADIX = {"dp": 2, "seq": 4}
-TAIL = ((0, ("on",)), (3, ("y", "z", "c")))
+STAGES = (("dp", 1, 2), ("dp", 2, 2), ("dp", 4, 2), ("seq", 4, 4), ("seq", 16, 2), ("seq", 1, 4))
+TAIL = ((0, ("on",)), (3, ("z", "on2")), (5, ("y", "c")))
 ATTN_COST = 4_000_000_000
 CLOSE_COST = 1_000_000_000
 F32 = jnp.float32
@@ -218,16 +218,9 @@
             got = [a + b for a, b in zip(got[::2], got[1::2])]
         return got[0]
 
-    def whole_axis(x, axis, size):
-        stride = 1
-        while stride < size:
-            group = 4 if RADIX[axis] == 4 and size // stride % 4 == 0 else 2
-            x = spread(after(x, *waits.pop(0)), axis, size, stride, group)
-            stride *= group
-        return x
-
-    block = whole_axis(block, "dp", lax.axis_size("dp"))
-    return whole_axis(block, "seq", lax.axis_size("seq"))
+    for (axis, stride, group), others in zip(STAGES, waits):
+        block = spread(after(block, *others), axis, lax.axis_size(axis), stride, group)
+    return block
 
 
 def after(block, *others):
@@ -333,7 +326,7 @@
     for i in CLOSE_AFTER:
         close(i)
     waits = [()] * 8
-    known = {"on": onward.get(last - 1), "z": got_z[Z_TERMS[-1]], "y": sent[last][1:], "c": closed and closed[0], "tn": sent[max(last - 2, 0)][1]}
+    known = {"on": onward.get(last - 1), "on2": onward.get(last), "z": got_z[Z_TERMS[-1]], "y": sent[last][1:], "c": closed and closed[0], "tn": sent[max(last - 2, 0)][1]}
     for stage, names in TAIL:
         waits[stage] = tuple(jax.tree.leaves([known[n] for n in names]))
     for i in CLOSE_LAST:

time: 194 us -> 177 us (0.912)
  starting transfers between devices: 82.2 us -> 63.6 us
    ppermute x10, starting transfers between devices: 35.9 us -> 15.9 us  [spread(): lax.ppermute(x, axis, [(i, peer(i, d)) for i in range(size)])]
    ppermute x4, waiting for transfers between devices: 5.1 us -> 14.9 us  [frames(): lax.ppermute(block, 'seq', [(t, t + step) for t in range(tiles) if 0 <= t...]
    ppermute x12, waiting for transfers between devices: 26.6 us -> 20.9 us  [in_row(): lax.ppermute(block, 'seq', [(s + a, s + b) for s in starts for a, b in ho...]
    ppermute x10, waiting for transfers between devices: 12.5 us -> 8.08 us  [spread(): lax.ppermute(x, axis, [(i, peer(i, d)) for i in range(size)])]
  transfers between devices with their start and end apart: 26 -> 26, of which waited for: 11 -> 7; matrix products, arithmetic and copies ran while one was open for 1% -> 3% of each run, Pallas kernels for 29% -> 32%
where the time goes in v3:
time: 177 us; the launch traced here: 176 us
  starting transfers between devices  63.6 us (36%)
  Pallas kernels  56.7 us (32%)
  waiting for transfers between devices  43.9 us (25%)
  local copies, waits for them, and re-layouts  5.96 us (3%)
  other arithmetic  4.51 us (3%)
    pallas_call x3, Pallas kernels, attn_part(): pl.pallas_call(functools.partial(attn_kernel, per_step, begun), grid=(hea...  44.4 us
    ppermute x12, starting transfers between devices, in_row(): lax.ppermute(block, 'seq', [(s + a, s + b) for s in starts for a, b in ho...  35.2 us
    ppermute x12, waiting for transfers between devices, in_row(): lax.ppermute(block, 'seq', [(s + a, s + b) for s in starts for a, b in ho...  20.9 us
    ppermute x10, starting transfers between devices, spread(): lax.ppermute(x, axis, [(i, peer(i, d)) for i in range(size)])  15.9 us
    ppermute x4, waiting for transfers between devices, frames(): lax.ppermute(block, 'seq', [(t, t + step) for t in range(tiles) if 0 <= t...  14.9 us
    ppermute x4, starting transfers between devices, frames(): lax.ppermute(block, 'seq', [(t, t + step) for t in range(tiles) if 0 <= t...  12.5 us
    pallas_call x3, Pallas kernels, close_part(): pl.pallas_call(functools.partial(close_kernel, count), grid=(heads,), in_...  12.4 us
    ppermute x10, waiting for transfers between devices, spread(): lax.ppermute(x, axis, [(i, peer(i, d)) for i in range(size)])  8.08 us
  transfers between devices with their start and end apart: 26, of which 7 were waited for; matrix products, arithmetic and copies ran while one was open for 3% of the time, Pallas kernels for 32%

profile of v3, /device:TPU:4, one launch (start us, length us, event | category | flops | bytes accessed | tf_op | source)
XLA Modules:
  0.0 175.8 jit_solution(490828815130705735)
XLA Ops:
  0.6 1.8 %slice_bitcast_fusion.2 = (bf16[1,384,512]{2,1,0:T(8,128)(2,1)S(1)}, bf16[1,384,512]{2,1,0:T(8,128)(2,1)S(1)}, bf16[1,384,512]{2,1,0:T(8,128)(2,1)S(1)}, bf16[1,...) fusion(bf16[384,1536]{1,0:T(8,128)(2,1)} %bitcast.33, ...), kind=kLoop, calls=%fused_computation.9 | loop fusion | bytes 4718592 | tf_op jit(solution)/shard_map/stack | solution.py:260
  3.4 3.6 %collective-permute-start = (bf16[2,384,512]{2,1,0:T(8,128)(2,1)}, bf16[2,384,512]{2,1,0:T(8,128)(2,1)}, u32[]{:S(2)}, u32[]{:S(2)}) collective-permute-start(bf16[2,384,512]{2,1,0:T(8,128)(2,1)} %pad_maximum_fusion.2), channel_id=1, source_target_pairs={{0,8},{8,0},{16,24},{32,40},{40,32},{48,56},{64,72},{72,64},{80,88... | collective-permute-start | bytes 2359304 | tf_op jit(solution)/shard_map/ppermute | solution.py:238
  7.1 4.7 %collective-permute-start.3 = (bf16[2,384,512]{2,1,0:T(8,128)(2,1)}, bf16[2,384,512]{2,1,0:T(8,128)(2,1)}, u32[]{:S(2)}, u32[]{:S(2)}) collective-permute-start(bf16[2,384,512]{2,1,0:T(8,128)(2,1)} %pad_maximum_fusion.2), channel_id=1, source_target_pairs={{0,32},{8,40},{16,48},{24,56},{32,64},{40,72},{48,80},{56,88},{64,... | collective-permute-start | bytes 2359304 | tf_op jit(solution)/shard_map/ppermute | solution.py:241
  12.7 12.3 %collective-permute-done.kv1 = bf16[2,384,512]{2,1,0:T(8,128)(2,1)} collective-permute-done((bf16[2,384,512]{2,1,0:T(8,128)(2,1)}, bf16[2,384,512]{2,1,0:T(8,128)(2,1)}, u32[]{:S(2)}, u32[]{:S(2)}) %collective-permute-start) | collective-permute-done | bytes 786464 | tf_op jit(solution)/shard_map/ppermute | solution.py:238
  25.1 3.5 %collective-permute-start.1 = (bf16[2,384,512]{2,1,0:T(8,128)(2,1)}, bf16[2,384,512]{2,1,0:T(8,128)(2,1)}, u32[]{:S(2)}, u32[]{:S(2)}) collective-permute-start(bf16[2,384,512]{2,1,0:T(8,128)(2,1)} %pad_maximum_fusion.1), channel_id=1, source_target_pairs={{0,8},{8,0},{16,24},{32,40},{40,32},{48,56},{64,72},{72,64},{80,88... | collective-permute-start | bytes 2359304 | tf_op jit(solution)/shard_map/ppermute | solution.py:238
  28.5 3.7 %collective-permute-start.2 = (bf16[2,384,512]{2,1,0:T(8,128)(2,1)}, bf16[2,384,512]{2,1,0:T(8,128)(2,1)}, u32[]{:S(2)}, u32[]{:S(2)}) collective-permute-start(bf16[2,384,512]{2,1,0:T(8,128)(2,1)} %collective-permute-done.kv1), channel_id=1, source_target_pairs={{8,16},{0,24},{40,48},{32,56},{72,80},{64,88},{104,112},{96,120},{... | collective-permute-start | bytes 2359304 | tf_op jit(solution)/shard_map/ppermute | solution.py:238
  33.3 5.0 %collective-permute-start.7 = (bf16[2,384,1024]{2,1,0:T(8,128)(2,1)S(1)}, bf16[2,384,1024]{2,1,0:T(8,128)(2,1)}, u32[]{:S(2)}, u32[]{:S(2)}) collective-permute-start(bf16[2,384,1024]{2,1,0:T(8,128)(2,1)S(1)} %pad_maximum_fusion), channel_id=1, source_target_pairs={{0,32},{8,40},{16,48},{24,56},{32,64},{40,72},{48,80},{56,88},{64,... | collective-permute-start | bytes 4718600 | tf_op jit(solution)/shard_map/ppermute | solution.py:241
  38.4 7.3 %collective-permute-done.1.kv1 = bf16[2,384,512]{2,1,0:T(8,128)(2,1)} collective-permute-done((bf16[2,384,512]{2,1,0:T(8,128)(2,1)}, bf16[2,384,512]{2,1,0:T(8,128)(2,1)}, u32[]{:S(2)}, u32[]{:S(2)}) %collective-permute-start.1) | collective-permute-done | bytes 786464 | tf_op jit(solution)/shard_map/ppermute | solution.py:238
  45.7 3.5 %collective-permute-start.5 = (bf16[2,384,512]{2,1,0:T(8,128)(2,1)S(1)}, bf16[2,384,512]{2,1,0:T(8,128)(2,1)S(1)}, u32[]{:S(2)}, u32[]{:S(2)}) collective-permute-start(bf16[2,384,512]{2,1,0:T(8,128)(2,1)S(1)} %pad_maximum_fusion.3), channel_id=1, source_target_pairs={{0,8},{8,0},{16,24},{32,40},{40,32},{48,56},{64,72},{72,64},{80,88... | collective-permute-start | bytes 2359304 | tf_op jit(solution)/shard_map/ppermute | solution.py:238
  49.1 2.8 %collective-permute-start.6 = (bf16[2,384,512]{2,1,0:T(8,128)(2,1)}, bf16[2,384,512]{2,1,0:T(8,128)(2,1)S(1)}, u32[]{:S(2)}, u32[]{:S(2)}) collective-permute-start(bf16[2,384,512]{2,1,0:T(8,128)(2,1)} %collective-permute-done.1.kv1), channel_id=1, source_target_pairs={{8,16},{0,24},{40,48},{32,56},{72,80},{64,88},{104,112},{96,120},{... | collective-permute-start | bytes 2359304 | tf_op jit(solution)/shard_map/ppermute | solution.py:238
  51.9 14.7 %attention_part.3 = (bf16[384,1536]{1,0:T(8,128)(2,1)}, bf16[384,1536]{1,0:T(8,128)(2,1)}, bf16[4,2,384,128]{3,2,1,0:T(8,128)(2,1)}, bf16[4,2,384,128]{3,2,1,0:T...) custom-call(s32[3]{0:T(128)} %bitcast.55, ...), custom_call_target="tpu_custom_call" | custom-call | flops 16000000000 | bytes 16000000 | tf_op jit(solution)/shard_map/attention_part/pallas_call | solution.py:145
  66.6 1.3 collective-permute-start.4
  67.9 6.0 %collective-permute-start.8 = (bf16[2,384,512]{2,1,0:T(8,128)(2,1)S(1)}, bf16[2,384,512]{2,1,0:T(8,128)(2,1)S(1)}, u32[]{:S(2)}, u32[]{:S(2)}) collective-permute-start(bf16[2,384,512]{2,1,0:T(8,128)(2,1)S(1)} %collective-permute-done.5.kv1), channel_id=1, source_target_pairs={{8,16},{0,24},{40,48},{32,56},{72,80},{64,88},{104,112},{96,120},{... | collective-permute-start | bytes 2359304 | tf_op jit(solution)/shard_map/ppermute | solution.py:238
  74.9 14.8 %attention_part.4 = (bf16[384,1536]{1,0:T(8,128)(2,1)}, bf16[384,1536]{1,0:T(8,128)(2,1)}, bf16[4,2,384,128]{3,2,1,0:T(8,128)(2,1)}, bf16[4,2,384,128]{3,2,1,0:T...) custom-call(s32[3]{0:T(128)} %bitcast.56, ...), custom_call_target="tpu_custom_call", output_to_operand_aliasing={{6}: (10, {}), {7}: (11, {}), {0}: (12, {}), {1}: (13, {}),... | custom-call | flops 16000000000 | bytes 16000000 | tf_op jit(solution)/shard_map/attention_part/pallas_call | solution.py:145
  89.9 1.3 collective-permute-start.12
  91.2 1.5 collective-permute-start.14
  93.7 14.9 %attention_part.5 = (bf16[384,1536]{1,0:T(8,128)(2,1)}, bf16[384,1536]{1,0:T(8,128)(2,1)}, bf16[4,2,384,128]{3,2,1,0:T(8,128)(2,1)}, bf16[4,2,384,128]{3,2,1,0:T...) custom-call(s32[3]{0:T(128)} %bitcast.57, ...), custom_call_target="tpu_custom_call", output_to_operand_aliasing={{6}: (10, {}), {7}: (11, {}), {0}: (12, {}), {1}: (13, {})} | custom-call | flops 16000000000 | bytes 16000000 | tf_op jit(solution)/shard_map/attention_part/pallas_call | solution.py:145
  108.5 1.3 collective-permute-start.9
  111.1 2.8 %collective-permute-start.15 = (bf16[4,2,384,128]{3,2,1,0:T(8,128)(2,1)S(1)}, bf16[4,2,384,128]{3,2,1,0:T(8,128)(2,1)}, u32[]{:S(2)}, u32[]{:S(2)}) collective-permute-start(bf16[4,2,384,128]{3,2,1,0:T(8,128)(2,1)S(1)} %add_convert_fusion.2), channel_id=1, source_target_pairs={{0,8},{8,0},{24,16},{32,40},{40,32},{56,48},{64,72},{72,64},{88,80... | collective-permute-start | bytes 2359304 | tf_op jit(solution)/shard_map/ppermute | solution.py:238
  118.3 2.4 %collective-permute-done.17 = f32[2,128]{1,0:T(2,128)S(1)} collective-permute-done((f32[2,128]{1,0:T(2,128)S(1)}, f32[2,128]{1,0:T(2,128)S(1)}, u32[]{:S(2)}, u32[]{:S(2)}) %collective-permute-start.17) | collective-permute-done | bytes 1056 | tf_op jit(solution)/shard_map/ppermute | solution.py:216
  121.2 4.6 %collective-permute-done.18 = f32[2,128]{1,0:T(2,128)S(1)} collective-permute-done((f32[2,128]{1,0:T(2,128)S(1)}, f32[2,128]{1,0:T(2,128)S(1)}, u32[]{:S(2)}, u32[]{:S(2)}) %collective-permute-start.18) | collective-permute-done | bytes 1056 | tf_op jit(solution)/shard_map/ppermute | solution.py:216
  125.8 3.1 %collective-permute-start.13 = (bf16[4,2,384,128]{3,2,1,0:T(8,128)(2,1)S(1)}, bf16[4,2,384,128]{3,2,1,0:T(8,128)(2,1)S(1)}, u32[]{:S(2)}, u32[]{:S(2)}) collective-permute-start(bf16[4,2,384,128]{3,2,1,0:T(8,128)(2,1)S(1)} %add_convert_fusion), channel_id=1, source_target_pairs={{0,8},{8,0},{24,16},{32,40},{40,32},{56,48},{64,72},{72,64},{88,80... | collective-permute-start | bytes 2359304 | tf_op jit(solution)/shard_map/ppermute | solution.py:238
  129.1 14.9 %collective-permute-done.11.refs_2_ = bf16[4,2,384,128]{3,2,1,0:T(8,128)(2,1)} collective-permute-done((bf16[4,2,384,128]{3,2,1,0:T(8,128)(2,1)}, bf16[4,2,384,128]{3,2,1,0:T(8,128)(2,1)}, u32[]{:S(2)}, u32[]{:S(2)}) %collective-permute-start.11) | collective-permute-done | bytes 786464 | tf_op jit(solution)/shard_map/ppermute | solution.py:241
  144.0 3.3 %collective-permute-start.20 = (f32[2,128]{1,0:T(2,128)S(1)}, f32[2,128]{1,0:T(2,128)S(1)}, u32[]{:S(2)}, u32[]{:S(2)}) collective-permute-start(f32[2,128]{1,0:T(2,128)S(1)} %add.44), channel_id=1, source_target_pairs={{0,64},{8,72},{16,80},{24,88},{32,96},{40,104},{48,112},{56,120},{... | collective-permute-start | bytes 3080 | tf_op jit(solution)/shard_map/ppermute | solution.py:216
  147.3 2.6 %collective-permute-start.21 = (f32[2,128]{1,0:T(2,128)S(1)}, f32[2,128]{1,0:T(2,128)S(1)}, u32[]{:S(2)}, u32[]{:S(2)}) collective-permute-start(f32[2,128]{1,0:T(2,128)S(1)} %add.44), channel_id=1, source_target_pairs={{0,96},{8,104},{16,112},{24,120},{32,64},{40,72},{48,80},{56,88},{... | collective-permute-start | bytes 3080 | tf_op jit(solution)/shard_map/ppermute | solution.py:216
  150.4 2.5 %collective-permute-start.10 = (bf16[4,2,384,128]{3,2,1,0:T(8,128)(2,1)S(1)}, bf16[4,2,384,128]{3,2,1,0:T(8,128)(2,1)S(1)}, u32[]{:S(2)}, u32[]{:S(2)}) collective-permute-start(bf16[4,2,384,128]{3,2,1,0:T(8,128)(2,1)S(1)} %add_convert_fusion.1), channel_id=1, source_target_pairs={{0,8},{8,0},{24,16},{32,40},{40,32},{56,48},{64,72},{72,64},{88,80... | collective-permute-start | bytes 2359304 | tf_op jit(solution)/shard_map/ppermute | solution.py:238
  152.9 4.1 %close_part.3 = (bf16[384,1536]{1,0:T(8,128)(2,1)}, bf16[384,1536]{1,0:T(8,128)(2,1)}) custom-call(bf16[384,1536]{1,0:T(8,128)(2,1)} %bitcast.42, bf16[4,2,384,128]{3,2,1,0:T(8,128)(2,1)} %get-tuple-element.77.refs_0_, bf16[4,2,384,128]{3,2,1,0:T(8,128)(2,1)} %collective-permute-done.15.refs_1_, bf16[8,2,384,128]{3,2,1,0:T(8,128)(2,1)} %collective-permute-done.14.refs_2_, ...), custom_call_target="tpu_custom_call" | custom-call | flops 4000000000 | bytes 4000000 | tf_op jit(solution)/shard_map/close_part/pallas_call | solution.py:193
  157.1 4.2 %collective-permute-start.22 = (f32[2,128]{1,0:T(2,128)S(1)}, f32[2,128]{1,0:T(2,128)S(1)}, u32[]{:S(2)}, u32[]{:S(2)}) collective-permute-start(f32[2,128]{1,0:T(2,128)S(1)} %add_add_fusion.1), channel_id=1, source_target_pairs={{0,128},{8,136},{16,144},{24,152},{32,160},{40,168},{48,176},{56,1... | collective-permute-start | bytes 3080 | tf_op jit(solution)/shard_map/ppermute | solution.py:216
  162.2 4.1 %close_part.4 = (bf16[384,1536]{1,0:T(8,128)(2,1)}, bf16[384,1536]{1,0:T(8,128)(2,1)}) custom-call(bf16[384,1536]{1,0:T(8,128)(2,1)} %bitcast.43, bf16[4,2,384,128]{3,2,1,0:T(8,128)(2,1)} %get-tuple-element.71.refs_0_, bf16[4,2,384,128]{3,2,1,0:T(8,128)(2,1)} %copy-done.7, ...), custom_call_target="tpu_custom_call", output_to_operand_aliasing={{0}: (5, {}), {1}: (6, {})} | custom-call | flops 4000000000 | bytes 4000000 | tf_op jit(solution)/shard_map/close_part/pallas_call | solution.py:193
  166.3 1.3 collective-permute-done.10.refs_1_
  167.7 2.5 %collective-permute-start.24 = (f32[2,128]{1,0:T(2,128)S(1)}, f32[2,128]{1,0:T(2,128)S(1)}, u32[]{:S(2)}, u32[]{:S(2)}) collective-permute-start(f32[2,128]{1,0:T(2,128)S(1)} %add.48), channel_id=1, source_target_pairs={{0,16},{8,24},{16,0},{24,8},{32,48},{40,56},{48,32},{56,40},{64,80... | collective-permute-start | bytes 3080 | tf_op jit(solution)/shard_map/ppermute | solution.py:216
  171.1 4.1 %close_part.5 = (bf16[384,1536]{1,0:T(8,128)(2,1)}, bf16[384,1536]{1,0:T(8,128)(2,1)}) custom-call(bf16[384,1536]{1,0:T(8,128)(2,1)} %bitcast.44, bf16[4,2,384,128]{3,2,1,0:T(8,128)(2,1)} %get-tuple-element.67.refs_0_, bf16[4,2,384,128]{3,2,1,0:T(8,128)(2,1)} %copy-done.8, ...), custom_call_target="tpu_custom_call", output_to_operand_aliasing={{0}: (5, {}), {1}: (6, {})} | custom-call | flops 4000000000 | bytes 4000000 | tf_op jit(solution)/shard_map/close_part/pallas_call | solution.py:193
  (68 shorter events, 14.5 us)
Async XLA Ops:
  2.5 30.5 %copy-start.1 = (bf16[1,384,1536]{2,1,0:T(8,128)(2,1)S(1)}, bf16[1,384,1536]{2,1,0:T(8,128)(2,1)}, u32[]{:S(2)}) copy-start(bf16[1,384,1536]{2,1,0:T(8,128)(2,1)} %param.8) | copy-start | bytes 3538948
  3.4 28.8 %copy-start.5 = (f32[128]{0:T(128)S(1)}, f32[128]{0:T(128)}, u32[]{:S(2)}) copy-start(f32[128]{0:T(128)} %param.10) | copy-start | bytes 1540
  3.4 29.5 %copy-start = (bf16[1,384,1536]{2,1,0:T(8,128)(2,1)S(1)}, bf16[1,384,1536]{2,1,0:T(8,128)(2,1)}, u32[]{:S(2)}) copy-start(bf16[1,384,1536]{2,1,0:T(8,128)(2,1)} %param.9) | copy-start | bytes 3538948
  3.4 21.6 %collective-permute-start = (bf16[2,384,512]{2,1,0:T(8,128)(2,1)}, bf16[2,384,512]{2,1,0:T(8,128)(2,1)}, u32[]{:S(2)}, u32[]{:S(2)}) collective-permute-start(bf16[2,384,512]{2,1,0:T(8,128)(2,1)} %pad_maximum_fusion.2), channel_id=1, source_target_pairs={{0,8},{8,0},{16,24},{32,40},{40,32},{48,56},{64,72},{72,64},{80,88... | collective-permute-start | bytes 2359304 | tf_op jit(solution)/shard_map/ppermute | solution.py:238
  7.1 26.2 %collective-permute-start.3 = (bf16[2,384,512]{2,1,0:T(8,128)(2,1)}, bf16[2,384,512]{2,1,0:T(8,128)(2,1)}, u32[]{:S(2)}, u32[]{:S(2)}) collective-permute-start(bf16[2,384,512]{2,1,0:T(8,128)(2,1)} %pad_maximum_fusion.2), channel_id=1, source_target_pairs={{0,32},{8,40},{16,48},{24,56},{32,64},{40,72},{48,80},{56,88},{64,... | collective-permute-start | bytes 2359304 | tf_op jit(solution)/shard_map/ppermute | solution.py:241
  25.1 20.6 %collective-permute-start.1 = (bf16[2,384,512]{2,1,0:T(8,128)(2,1)}, bf16[2,384,512]{2,1,0:T(8,128)(2,1)}, u32[]{:S(2)}, u32[]{:S(2)}) collective-permute-start(bf16[2,384,512]{2,1,0:T(8,128)(2,1)} %pad_maximum_fusion.1), channel_id=1, source_target_pairs={{0,8},{8,0},{16,24},{32,40},{40,32},{48,56},{64,72},{72,64},{80,88... | collective-permute-start | bytes 2359304 | tf_op jit(solution)/shard_map/ppermute | solution.py:238
  28.5 23.4 %collective-permute-start.2 = (bf16[2,384,512]{2,1,0:T(8,128)(2,1)}, bf16[2,384,512]{2,1,0:T(8,128)(2,1)}, u32[]{:S(2)}, u32[]{:S(2)}) collective-permute-start(bf16[2,384,512]{2,1,0:T(8,128)(2,1)} %collective-permute-done.kv1), channel_id=1, source_target_pairs={{8,16},{0,24},{40,48},{32,56},{72,80},{64,88},{104,112},{96,120},{... | collective-permute-start | bytes 2359304 | tf_op jit(solution)/shard_map/ppermute | solution.py:238
  33.3 40.7 %collective-permute-start.7 = (bf16[2,384,1024]{2,1,0:T(8,128)(2,1)S(1)}, bf16[2,384,1024]{2,1,0:T(8,128)(2,1)}, u32[]{:S(2)}, u32[]{:S(2)}) collective-permute-start(bf16[2,384,1024]{2,1,0:T(8,128)(2,1)S(1)} %pad_maximum_fusion), channel_id=1, source_target_pairs={{0,32},{8,40},{16,48},{24,56},{32,64},{40,72},{48,80},{56,88},{64,... | collective-permute-start | bytes 4718600 | tf_op jit(solution)/shard_map/ppermute | solution.py:241
  45.7 22.2 %collective-permute-start.5 = (bf16[2,384,512]{2,1,0:T(8,128)(2,1)S(1)}, bf16[2,384,512]{2,1,0:T(8,128)(2,1)S(1)}, u32[]{:S(2)}, u32[]{:S(2)}) collective-permute-start(bf16[2,384,512]{2,1,0:T(8,128)(2,1)S(1)} %pad_maximum_fusion.3), channel_id=1, source_target_pairs={{0,8},{8,0},{16,24},{32,40},{40,32},{48,56},{64,72},{72,64},{80,88... | collective-permute-start | bytes 2359304 | tf_op jit(solution)/shard_map/ppermute | solution.py:238
  49.1 24.8 %collective-permute-start.6 = (bf16[2,384,512]{2,1,0:T(8,128)(2,1)}, bf16[2,384,512]{2,1,0:T(8,128)(2,1)S(1)}, u32[]{:S(2)}, u32[]{:S(2)}) collective-permute-start(bf16[2,384,512]{2,1,0:T(8,128)(2,1)} %collective-permute-done.1.kv1), channel_id=1, source_target_pairs={{8,16},{0,24},{40,48},{32,56},{72,80},{64,88},{104,112},{96,120},{... | collective-permute-start | bytes 2359304 | tf_op jit(solution)/shard_map/ppermute | solution.py:238
  66.6 23.1 %collective-permute-start.4 = (bf16[4,2,384,128]{3,2,1,0:T(8,128)(2,1)}, bf16[4,2,384,128]{3,2,1,0:T(8,128)(2,1)S(1)}, u32[]{:S(2)}, u32[]{:S(2)}) collective-permute-start(bf16[4,2,384,128]{3,2,1,0:T(8,128)(2,1)} %get-tuple-element.50), channel_id=1, source_target_pairs={{24,0},{16,8},{56,32},{48,40},{88,64},{80,72},{120,96},{112,104},{... | collective-permute-start | bytes 2359304 | tf_op jit(solution)/shard_map/ppermute | solution.py:238
  67.9 21.8 %copy-start.6 = (bf16[2,384,512]{2,1,0:T(8,128)(2,1)}, bf16[2,384,512]{2,1,0:T(8,128)(2,1)S(1)}, u32[]{:S(2)}) copy-start(bf16[2,384,512]{2,1,0:T(8,128)(2,1)S(1)} %collective-permute-done.5.kv1) | copy-start | bytes 2359300
  67.9 24.9 %collective-permute-start.8 = (bf16[2,384,512]{2,1,0:T(8,128)(2,1)S(1)}, bf16[2,384,512]{2,1,0:T(8,128)(2,1)S(1)}, u32[]{:S(2)}, u32[]{:S(2)}) collective-permute-start(bf16[2,384,512]{2,1,0:T(8,128)(2,1)S(1)} %collective-permute-done.5.kv1), channel_id=1, source_target_pairs={{8,16},{0,24},{40,48},{32,56},{72,80},{64,88},{104,112},{96,120},{... | collective-permute-start | bytes 2359304 | tf_op jit(solution)/shard_map/ppermute | solution.py:238
  74.9 14.9 %copy-start.4 = (bf16[4,2,384,128]{3,2,1,0:T(8,128)(2,1)S(1)}, bf16[4,2,384,128]{3,2,1,0:T(8,128)(2,1)}, u32[]{:S(2)}) copy-start(bf16[4,2,384,128]{3,2,1,0:T(8,128)(2,1)} %get-tuple-element.49) | copy-start | bytes 2359300
  89.9 25.7 %collective-permute-start.12 = (bf16[4,2,384,128]{3,2,1,0:T(8,128)(2,1)}, bf16[4,2,384,128]{3,2,1,0:T(8,128)(2,1)S(1)}, u32[]{:S(2)}, u32[]{:S(2)}) collective-permute-start(bf16[4,2,384,128]{3,2,1,0:T(8,128)(2,1)} %get-tuple-element.73), channel_id=1, source_target_pairs={{24,0},{16,8},{56,32},{48,40},{88,64},{80,72},{120,96},{112,104},{... | collective-permute-start | bytes 2359304 | tf_op jit(solution)/shard_map/ppermute | solution.py:238
  91.2 59.2 %collective-permute-start.14 = (bf16[8,2,384,128]{3,2,1,0:T(8,128)(2,1)}, bf16[8,2,384,128]{3,2,1,0:T(8,128)(2,1)}, u32[]{:S(2)}, u32[]{:S(2)}) collective-permute-start(bf16[8,2,384,128]{3,2,1,0:T(8,128)(2,1)} %get-tuple-element.76), channel_id=1, source_target_pairs={{32,0},{40,8},{48,16},{56,24},{64,32},{72,40},{80,48},{88,56},{96,... | collective-permute-start | bytes 4718600 | tf_op jit(solution)/shard_map/ppermute | solution.py:241
  93.7 22.0 %copy-start.3 = (bf16[4,2,384,128]{3,2,1,0:T(8,128)(2,1)S(1)}, bf16[4,2,384,128]{3,2,1,0:T(8,128)(2,1)}, u32[]{:S(2)}) copy-start(bf16[4,2,384,128]{3,2,1,0:T(8,128)(2,1)} %get-tuple-element.72) | copy-start | bytes 2359300
  108.5 20.3 %collective-permute-start.9 = (bf16[4,2,384,128]{3,2,1,0:T(8,128)(2,1)}, bf16[4,2,384,128]{3,2,1,0:T(8,128)(2,1)S(1)}, u32[]{:S(2)}, u32[]{:S(2)}) collective-permute-start(bf16[4,2,384,128]{3,2,1,0:T(8,128)(2,1)} %get-tuple-element.69), channel_id=1, source_target_pairs={{24,0},{16,8},{56,32},{48,40},{88,64},{80,72},{120,96},{112,104},{... | collective-permute-start | bytes 2359304 | tf_op jit(solution)/shard_map/ppermute | solution.py:238
  109.8 34.2 %collective-permute-start.11 = (bf16[4,2,384,128]{3,2,1,0:T(8,128)(2,1)}, bf16[4,2,384,128]{3,2,1,0:T(8,128)(2,1)}, u32[]{:S(2)}, u32[]{:S(2)}) collective-permute-start(bf16[4,2,384,128]{3,2,1,0:T(8,128)(2,1)} %get-tuple-element.70), channel_id=1, source_target_pairs={{32,0},{40,8},{48,16},{56,24},{64,32},{72,40},{80,48},{88,56},{96,... | collective-permute-start | bytes 2359304 | tf_op jit(solution)/shard_map/ppermute | solution.py:241
  111.1 38.7 %collective-permute-start.15 = (bf16[4,2,384,128]{3,2,1,0:T(8,128)(2,1)S(1)}, bf16[4,2,384,128]{3,2,1,0:T(8,128)(2,1)}, u32[]{:S(2)}, u32[]{:S(2)}) collective-permute-start(bf16[4,2,384,128]{3,2,1,0:T(8,128)(2,1)S(1)} %add_convert_fusion.2), channel_id=1, source_target_pairs={{0,8},{8,0},{24,16},{32,40},{40,32},{56,48},{64,72},{72,64},{88,80... | collective-permute-start | bytes 2359304 | tf_op jit(solution)/shard_map/ppermute | solution.py:238
  115.9 1.2 collective-permute-start.16
  117.1 3.6 %collective-permute-start.17 = (f32[2,128]{1,0:T(2,128)S(1)}, f32[2,128]{1,0:T(2,128)S(1)}, u32[]{:S(2)}, u32[]{:S(2)}) collective-permute-start(f32[2,128]{1,0:T(2,128)S(1)} %add.42), channel_id=1, source_target_pairs={{0,2},{1,3},{2,0},{3,1},{4,6},{5,7},{6,4},{7,5},{8,10},{9,11},{10,... | collective-permute-start | bytes 3080 | tf_op jit(solution)/shard_map/ppermute | solution.py:216
  120.7 5.1 %collective-permute-start.18 = (f32[2,128]{1,0:T(2,128)S(1)}, f32[2,128]{1,0:T(2,128)S(1)}, u32[]{:S(2)}, u32[]{:S(2)}) collective-permute-start(f32[2,128]{1,0:T(2,128)S(1)} %add.43), channel_id=1, source_target_pairs={{0,4},{1,5},{2,6},{3,7},{4,0},{5,1},{6,2},{7,3},{8,12},{9,13},{10,... | collective-permute-start | bytes 3080 | tf_op jit(solution)/shard_map/ppermute | solution.py:216
  125.8 35.5 %collective-permute-start.13 = (bf16[4,2,384,128]{3,2,1,0:T(8,128)(2,1)S(1)}, bf16[4,2,384,128]{3,2,1,0:T(8,128)(2,1)S(1)}, u32[]{:S(2)}, u32[]{:S(2)}) collective-permute-start(bf16[4,2,384,128]{3,2,1,0:T(8,128)(2,1)S(1)} %add_convert_fusion), channel_id=1, source_target_pairs={{0,8},{8,0},{24,16},{32,40},{40,32},{56,48},{64,72},{72,64},{88,80... | collective-permute-start | bytes 2359304 | tf_op jit(solution)/shard_map/ppermute | solution.py:238
  144.0 13.1 %collective-permute-start.20 = (f32[2,128]{1,0:T(2,128)S(1)}, f32[2,128]{1,0:T(2,128)S(1)}, u32[]{:S(2)}, u32[]{:S(2)}) collective-permute-start(f32[2,128]{1,0:T(2,128)S(1)} %add.44), channel_id=1, source_target_pairs={{0,64},{8,72},{16,80},{24,88},{32,96},{40,104},{48,112},{56,120},{... | collective-permute-start | bytes 3080 | tf_op jit(solution)/shard_map/ppermute | solution.py:216
  147.3 9.8 %collective-permute-start.21 = (f32[2,128]{1,0:T(2,128)S(1)}, f32[2,128]{1,0:T(2,128)S(1)}, u32[]{:S(2)}, u32[]{:S(2)}) collective-permute-start(f32[2,128]{1,0:T(2,128)S(1)} %add.44), channel_id=1, source_target_pairs={{0,96},{8,104},{16,112},{24,120},{32,64},{40,72},{48,80},{56,88},{... | collective-permute-start | bytes 3080 | tf_op jit(solution)/shard_map/ppermute | solution.py:216
  149.8 7.2 %collective-permute-start.19 = (f32[2,128]{1,0:T(2,128)S(1)}, f32[2,128]{1,0:T(2,128)S(1)}, u32[]{:S(2)}, u32[]{:S(2)}) collective-permute-start(f32[2,128]{1,0:T(2,128)S(1)} %add.44), channel_id=1, source_target_pairs={{0,32},{8,40},{16,48},{24,56},{32,0},{40,8},{48,16},{56,24},{64,96... | collective-permute-start | bytes 3080 | tf_op jit(solution)/shard_map/ppermute | solution.py:216
  150.4 17.2 %collective-permute-start.10 = (bf16[4,2,384,128]{3,2,1,0:T(8,128)(2,1)S(1)}, bf16[4,2,384,128]{3,2,1,0:T(8,128)(2,1)S(1)}, u32[]{:S(2)}, u32[]{:S(2)}) collective-permute-start(bf16[4,2,384,128]{3,2,1,0:T(8,128)(2,1)S(1)} %add_convert_fusion.1), channel_id=1, source_target_pairs={{0,8},{8,0},{24,16},{32,40},{40,32},{56,48},{64,72},{72,64},{88,80... | collective-permute-start | bytes 2359304 | tf_op jit(solution)/shard_map/ppermute | solution.py:238
  157.1 9.2 %collective-permute-start.22 = (f32[2,128]{1,0:T(2,128)S(1)}, f32[2,128]{1,0:T(2,128)S(1)}, u32[]{:S(2)}, u32[]{:S(2)}) collective-permute-start(f32[2,128]{1,0:T(2,128)S(1)} %add_add_fusion.1), channel_id=1, source_target_pairs={{0,128},{8,136},{16,144},{24,152},{32,160},{40,168},{48,176},{56,1... | collective-permute-start | bytes 3080 | tf_op jit(solution)/shard_map/ppermute | solution.py:216
  167.7 7.6 %collective-permute-start.24 = (f32[2,128]{1,0:T(2,128)S(1)}, f32[2,128]{1,0:T(2,128)S(1)}, u32[]{:S(2)}, u32[]{:S(2)}) collective-permute-start(f32[2,128]{1,0:T(2,128)S(1)} %add.48), channel_id=1, source_target_pairs={{0,16},{8,24},{16,0},{24,8},{32,48},{40,56},{48,32},{56,40},{64,80... | collective-permute-start | bytes 3080 | tf_op jit(solution)/shard_map/ppermute | solution.py:216
  170.1 5.1 %collective-permute-start.25 = (f32[2,128]{1,0:T(2,128)S(1)}, f32[2,128]{1,0:T(2,128)S(1)}, u32[]{:S(2)}, u32[]{:S(2)}) collective-permute-start(f32[2,128]{1,0:T(2,128)S(1)} %add.48), channel_id=1, source_target_pairs={{0,24},{8,16},{16,8},{24,0},{32,56},{40,48},{48,40},{56,32},{64,88... | collective-permute-start | bytes 3080 | tf_op jit(solution)/shard_map/ppermute | solution.py:216
  170.6 4.7 %collective-permute-start.23 = (f32[2,128]{1,0:T(2,128)S(1)}, f32[2,128]{1,0:T(2,128)S(1)}, u32[]{:S(2)}, u32[]{:S(2)}) collective-permute-start(f32[2,128]{1,0:T(2,128)S(1)} %add.48), channel_id=1, source_target_pairs={{0,8},{8,0},{16,24},{24,16},{32,40},{40,32},{48,56},{56,48},{64,72... | collective-permute-start | bytes 3080 | tf_op jit(solution)/shard_map/ppermute | solution.py:216
  (5 other events, 19.3 us)

commit v4 on v3

--- a/solution.py
+++ b/solution.py
@@ -19,8 +19,8 @@
 CLOSE_BEFORE = {}
 CLOSE_AFTER = (0, 1)
 CLOSE_LAST = (2,)
-STAGES = (("dp", 1, 2), ("dp", 2, 2), ("dp", 4, 2), ("seq", 4, 4), ("seq", 16, 2), ("seq", 1, 4))
-TAIL = ((0, ("on",)), (3, ("z", "on2")), (5, ("y", "c")))
+STAGES = (("dp", 1, 2), ("dp", 2, 2), ("dp", 4, 2), ("seq", 1, 4), ("seq", 4, 4), ("seq", 16, 2))
+TAIL = ((0, ("on",)), (3, ("on2",)), (4, ("z",)), (5, ("y", "c")))
 ATTN_COST = 4_000_000_000
 CLOSE_COST = 1_000_000_000
 F32 = jnp.float32

time: 177 us -> 179 us (1.011); the launches traced: 176 us -> 175 us
  waiting for transfers between devices: 43.9 us -> 35.8 us
  starting transfers between devices: 63.6 us -> 71.1 us
    ppermute x4, waiting for transfers between devices: 14.9 us -> 0.01 us  [frames(): lax.ppermute(block, 'seq', [(t, t + step) for t in range(tiles) if 0 <= t...]
    ppermute x12, waiting for transfers between devices: 20.9 us -> 27.5 us  [in_row(): lax.ppermute(block, 'seq', [(s + a, s + b) for s in starts for a, b in ho...]
    ppermute x12, starting transfers between devices: 35.2 us -> 39.7 us  [in_row(): lax.ppermute(block, 'seq', [(s + a, s + b) for s in starts for a, b in ho...]
    ppermute x10, starting transfers between devices: 15.9 us -> 18.9 us  [spread(): lax.ppermute(x, axis, [(i, peer(i, d)) for i in range(size)])]
  transfers between devices with their start and end apart: 26 -> 26, of which waited for: 7 -> 9; matrix products, arithmetic and copies ran while one was open for 3% -> 3% of each run, Pallas kernels for 32% -> 32%
where the time goes in v4:
time: 179 us; the launch traced here: 175 us
  starting transfers between devices  71.1 us (40%)
  Pallas kernels  56.7 us (32%)
  waiting for transfers between devices  35.8 us (20%)
  local copies, waits for them, and re-layouts  5.94 us (3%)
  other arithmetic  4.51 us (3%)
    pallas_call x3, Pallas kernels, attn_part(): pl.pallas_call(functools.partial(attn_kernel, per_step, begun), grid=(hea...  44.3 us
    ppermute x12, starting transfers between devices, in_row(): lax.ppermute(block, 'seq', [(s + a, s + b) for s in starts for a, b in ho...  39.7 us
    ppermute x12, waiting for transfers between devices, in_row(): lax.ppermute(block, 'seq', [(s + a, s + b) for s in starts for a, b in ho...  27.5 us
    ppermute x10, starting transfers between devices, spread(): lax.ppermute(x, axis, [(i, peer(i, d)) for i in range(size)])  18.9 us
    ppermute x4, starting transfers between devices, frames(): lax.ppermute(block, 'seq', [(t, t + step) for t in range(tiles) if 0 <= t...  12.5 us
    pallas_call x3, Pallas kernels, close_part(): pl.pallas_call(functools.partial(close_kernel, count), grid=(heads,), in_...  12.4 us
    ppermute x10, waiting for transfers between devices, spread(): lax.ppermute(x, axis, [(i, peer(i, d)) for i in range(size)])  8.36 us
  transfers between devices with their start and end apart: 26, of which 9 were waited for; matrix products, arithmetic and copies ran while one was open for 3% of the time, Pallas kernels for 32%

profile of v4, /device:TPU:4, one launch (start us, length us, event | category | flops | bytes accessed | tf_op | source)
XLA Modules:
  0.0 175.2 jit_solution(14639547697940500476)
XLA Ops:
  0.6 1.8 %slice_bitcast_fusion.2 = (bf16[1,384,512]{2,1,0:T(8,128)(2,1)S(1)}, bf16[1,384,512]{2,1,0:T(8,128)(2,1)S(1)}, bf16[1,384,512]{2,1,0:T(8,128)(2,1)S(1)}, bf16[1,...) fusion(bf16[384,1536]{1,0:T(8,128)(2,1)} %bitcast.33, ...), kind=kLoop, calls=%fused_computation.9 | loop fusion | bytes 4718592 | tf_op jit(solution)/shard_map/stack | solution.py:260
  3.4 3.6 %collective-permute-start = (bf16[2,384,512]{2,1,0:T(8,128)(2,1)}, bf16[2,384,512]{2,1,0:T(8,128)(2,1)}, u32[]{:S(2)}, u32[]{:S(2)}) collective-permute-start(bf16[2,384,512]{2,1,0:T(8,128)(2,1)} %pad_maximum_fusion.2), channel_id=1, source_target_pairs={{0,8},{8,0},{16,24},{32,40},{40,32},{48,56},{64,72},{72,64},{80,88... | collective-permute-start | bytes 2359304 | tf_op jit(solution)/shard_map/ppermute | solution.py:238
  7.1 4.7 %collective-permute-start.3 = (bf16[2,384,512]{2,1,0:T(8,128)(2,1)}, bf16[2,384,512]{2,1,0:T(8,128)(2,1)}, u32[]{:S(2)}, u32[]{:S(2)}) collective-permute-start(bf16[2,384,512]{2,1,0:T(8,128)(2,1)} %pad_maximum_fusion.2), channel_id=1, source_target_pairs={{0,32},{8,40},{16,48},{24,56},{32,64},{40,72},{48,80},{56,88},{64,... | collective-permute-start | bytes 2359304 | tf_op jit(solution)/shard_map/ppermute | solution.py:241
  12.7 12.3 %collective-permute-done.kv1 = bf16[2,384,512]{2,1,0:T(8,128)(2,1)} collective-permute-done((bf16[2,384,512]{2,1,0:T(8,128)(2,1)}, bf16[2,384,512]{2,1,0:T(8,128)(2,1)}, u32[]{:S(2)}, u32[]{:S(2)}) %collective-permute-start) | collective-permute-done | bytes 786464 | tf_op jit(solution)/shard_map/ppermute | solution.py:238
  25.1 3.5 %collective-permute-start.1 = (bf16[2,384,512]{2,1,0:T(8,128)(2,1)}, bf16[2,384,512]{2,1,0:T(8,128)(2,1)}, u32[]{:S(2)}, u32[]{:S(2)}) collective-permute-start(bf16[2,384,512]{2,1,0:T(8,128)(2,1)} %pad_maximum_fusion.1), channel_id=1, source_target_pairs={{0,8},{8,0},{16,24},{32,40},{40,32},{48,56},{64,72},{72,64},{80,88... | collective-permute-start | bytes 2359304 | tf_op jit(solution)/shard_map/ppermute | solution.py:238
  28.5 3.7 %collective-permute-start.2 = (bf16[2,384,512]{2,1,0:T(8,128)(2,1)}, bf16[2,384,512]{2,1,0:T(8,128)(2,1)}, u32[]{:S(2)}, u32[]{:S(2)}) collective-permute-start(bf16[2,384,512]{2,1,0:T(8,128)(2,1)} %collective-permute-done.kv1), channel_id=1, source_target_pairs={{8,16},{0,24},{40,48},{32,56},{72,80},{64,88},{104,112},{96,120},{... | collective-permute-start | bytes 2359304 | tf_op jit(solution)/shard_map/ppermute | solution.py:238
  33.3 5.0 %collective-permute-start.7 = (bf16[2,384,1024]{2,1,0:T(8,128)(2,1)S(1)}, bf16[2,384,1024]{2,1,0:T(8,128)(2,1)}, u32[]{:S(2)}, u32[]{:S(2)}) collective-permute-start(bf16[2,384,1024]{2,1,0:T(8,128)(2,1)S(1)} %pad_maximum_fusion), channel_id=1, source_target_pairs={{0,32},{8,40},{16,48},{24,56},{32,64},{40,72},{48,80},{56,88},{64,... | collective-permute-start | bytes 4718600 | tf_op jit(solution)/shard_map/ppermute | solution.py:241
  38.4 7.3 %collective-permute-done.1.kv1 = bf16[2,384,512]{2,1,0:T(8,128)(2,1)} collective-permute-done((bf16[2,384,512]{2,1,0:T(8,128)(2,1)}, bf16[2,384,512]{2,1,0:T(8,128)(2,1)}, u32[]{:S(2)}, u32[]{:S(2)}) %collective-permute-start.1) | collective-permute-done | bytes 786464 | tf_op jit(solution)/shard_map/ppermute | solution.py:238
  45.7 3.5 %collective-permute-start.5 = (bf16[2,384,512]{2,1,0:T(8,128)(2,1)S(1)}, bf16[2,384,512]{2,1,0:T(8,128)(2,1)S(1)}, u32[]{:S(2)}, u32[]{:S(2)}) collective-permute-start(bf16[2,384,512]{2,1,0:T(8,128)(2,1)S(1)} %pad_maximum_fusion.3), channel_id=1, source_target_pairs={{0,8},{8,0},{16,24},{32,40},{40,32},{48,56},{64,72},{72,64},{80,88... | collective-permute-start | bytes 2359304 | tf_op jit(solution)/shard_map/ppermute | solution.py:238
  49.1 2.8 %collective-permute-start.6 = (bf16[2,384,512]{2,1,0:T(8,128)(2,1)}, bf16[2,384,512]{2,1,0:T(8,128)(2,1)S(1)}, u32[]{:S(2)}, u32[]{:S(2)}) collective-permute-start(bf16[2,384,512]{2,1,0:T(8,128)(2,1)} %collective-permute-done.1.kv1), channel_id=1, source_target_pairs={{8,16},{0,24},{40,48},{32,56},{72,80},{64,88},{104,112},{96,120},{... | collective-permute-start | bytes 2359304 | tf_op jit(solution)/shard_map/ppermute | solution.py:238
  51.9 14.7 %attention_part.3 = (bf16[384,1536]{1,0:T(8,128)(2,1)}, bf16[384,1536]{1,0:T(8,128)(2,1)}, bf16[4,2,384,128]{3,2,1,0:T(8,128)(2,1)}, bf16[4,2,384,128]{3,2,1,0:T...) custom-call(s32[3]{0:T(128)} %bitcast.55, ...), custom_call_target="tpu_custom_call" | custom-call | flops 16000000000 | bytes 16000000 | tf_op jit(solution)/shard_map/attention_part/pallas_call | solution.py:145
  66.6 1.3 collective-permute-start.4
  67.9 6.0 %collective-permute-start.8 = (bf16[2,384,512]{2,1,0:T(8,128)(2,1)S(1)}, bf16[2,384,512]{2,1,0:T(8,128)(2,1)S(1)}, u32[]{:S(2)}, u32[]{:S(2)}) collective-permute-start(bf16[2,384,512]{2,1,0:T(8,128)(2,1)S(1)} %collective-permute-done.5.kv1), channel_id=1, source_target_pairs={{8,16},{0,24},{40,48},{32,56},{72,80},{64,88},{104,112},{96,120},{... | collective-permute-start | bytes 2359304 | tf_op jit(solution)/shard_map/ppermute | solution.py:238
  74.9 14.8 %attention_part.4 = (bf16[384,1536]{1,0:T(8,128)(2,1)}, bf16[384,1536]{1,0:T(8,128)(2,1)}, bf16[4,2,384,128]{3,2,1,0:T(8,128)(2,1)}, bf16[4,2,384,128]{3,2,1,0:T...) custom-call(s32[3]{0:T(128)} %bitcast.56, ...), custom_call_target="tpu_custom_call", output_to_operand_aliasing={{6}: (10, {}), {7}: (11, {}), {0}: (12, {}), {1}: (13, {}),... | custom-call | flops 16000000000 | bytes 16000000 | tf_op jit(solution)/shard_map/attention_part/pallas_call | solution.py:145
  91.2 1.5 collective-permute-start.14
  93.7 14.9 %attention_part.5 = (bf16[384,1536]{1,0:T(8,128)(2,1)}, bf16[384,1536]{1,0:T(8,128)(2,1)}, bf16[4,2,384,128]{3,2,1,0:T(8,128)(2,1)}, bf16[4,2,384,128]{3,2,1,0:T...) custom-call(s32[3]{0:T(128)} %bitcast.57, ...), custom_call_target="tpu_custom_call", output_to_operand_aliasing={{6}: (10, {}), {7}: (11, {}), {0}: (12, {}), {1}: (13, {})} | custom-call | flops 16000000000 | bytes 16000000 | tf_op jit(solution)/shard_map/attention_part/pallas_call | solution.py:145
  109.8 2.8 %collective-permute-start.15 = (bf16[4,2,384,128]{3,2,1,0:T(8,128)(2,1)S(1)}, bf16[4,2,384,128]{3,2,1,0:T(8,128)(2,1)}, u32[]{:S(2)}, u32[]{:S(2)}) collective-permute-start(bf16[4,2,384,128]{3,2,1,0:T(8,128)(2,1)S(1)} %add_convert_fusion.2), channel_id=1, source_target_pairs={{0,8},{8,0},{24,16},{32,40},{40,32},{56,48},{64,72},{72,64},{88,80... | collective-permute-start | bytes 2359304 | tf_op jit(solution)/shard_map/ppermute | solution.py:238
  117.0 2.4 %collective-permute-done.17 = f32[2,128]{1,0:T(2,128)S(1)} collective-permute-done((f32[2,128]{1,0:T(2,128)S(1)}, f32[2,128]{1,0:T(2,128)S(1)}, u32[]{:S(2)}, u32[]{:S(2)}) %collective-permute-start.17) | collective-permute-done | bytes 1056 | tf_op jit(solution)/shard_map/ppermute | solution.py:216
  119.9 3.1 %collective-permute-start.13 = (bf16[4,2,384,128]{3,2,1,0:T(8,128)(2,1)S(1)}, bf16[4,2,384,128]{3,2,1,0:T(8,128)(2,1)S(1)}, u32[]{:S(2)}, u32[]{:S(2)}) collective-permute-start(bf16[4,2,384,128]{3,2,1,0:T(8,128)(2,1)S(1)} %add_convert_fusion), channel_id=1, source_target_pairs={{0,8},{8,0},{24,16},{32,40},{40,32},{56,48},{64,72},{72,64},{88,80... | collective-permute-start | bytes 2359304 | tf_op jit(solution)/shard_map/ppermute | solution.py:238
  123.0 1.5 collective-permute-done.18
  125.8 2.7 %collective-permute-done.9 = bf16[4,2,384,128]{3,2,1,0:T(8,128)(2,1)S(1)} collective-permute-done((bf16[4,2,384,128]{3,2,1,0:T(8,128)(2,1)}, bf16[4,2,384,128]{3,2,1,0:T(8,128)(2,1)S(1)}, u32[]{:S(2)}, u32[]{:S(2)}) %collective-permute-start.9) | collective-permute-done | bytes 786464 | tf_op jit(solution)/shard_map/ppermute | solution.py:238
  128.8 3.5 %collective-permute-done.15.refs_1_ = bf16[4,2,384,128]{3,2,1,0:T(8,128)(2,1)} collective-permute-done((bf16[4,2,384,128]{3,2,1,0:T(8,128)(2,1)S(1)}, bf16[4,2,384,128]{3,2,1,0:T(8,128)(2,1)}, u32[]{:S(2)}, u32[]{:S(2)}) %collective-permute-start.15) | collective-permute-done | bytes 786464 | tf_op jit(solution)/shard_map/ppermute | solution.py:238
  132.3 1.6 collective-permute-start.21
  133.9 2.0 %collective-permute-start.19 = (f32[2,128]{1,0:T(2,128)S(1)}, f32[2,128]{1,0:T(2,128)S(1)}, u32[]{:S(2)}, u32[]{:S(2)}) collective-permute-start(f32[2,128]{1,0:T(2,128)S(1)} %add.44), channel_id=1, source_target_pairs={{0,8},{8,0},{16,24},{24,16},{32,40},{40,32},{48,56},{56,48},{64,72... | collective-permute-start | bytes 3080 | tf_op jit(solution)/shard_map/ppermute | solution.py:216
  135.9 4.1 %close_part.3 = (bf16[384,1536]{1,0:T(8,128)(2,1)}, bf16[384,1536]{1,0:T(8,128)(2,1)}) custom-call(bf16[384,1536]{1,0:T(8,128)(2,1)} %bitcast.42, bf16[4,2,384,128]{3,2,1,0:T(8,128)(2,1)} %get-tuple-element.78.refs_0_, bf16[4,2,384,128]{3,2,1,0:T(8,128)(2,1)} %collective-permute-done.15.refs_1_, bf16[8,2,384,128]{3,2,1,0:T(8,128)(2,1)} %collective-permute-done.14.refs_2_, ...), custom_call_target="tpu_custom_call" | custom-call | flops 4000000000 | bytes 4000000 | tf_op jit(solution)/shard_map/close_part/pallas_call | solution.py:193
  140.0 3.3 %collective-permute-done.20 = f32[2,128]{1,0:T(2,128)S(1)} collective-permute-done((f32[2,128]{1,0:T(2,128)S(1)}, f32[2,128]{1,0:T(2,128)S(1)}, u32[]{:S(2)}, u32[]{:S(2)}) %collective-permute-start.20) | collective-permute-done | bytes 1056 | tf_op jit(solution)/shard_map/ppermute | solution.py:216
  143.4 7.0 %collective-permute-start.10 = (bf16[4,2,384,128]{3,2,1,0:T(8,128)(2,1)S(1)}, bf16[4,2,384,128]{3,2,1,0:T(8,128)(2,1)S(1)}, u32[]{:S(2)}, u32[]{:S(2)}) collective-permute-start(bf16[4,2,384,128]{3,2,1,0:T(8,128)(2,1)S(1)} %add_convert_fusion.1), channel_id=1, source_target_pairs={{0,8},{8,0},{24,16},{32,40},{40,32},{56,48},{64,72},{72,64},{88,80... | collective-permute-start | bytes 2359304 | tf_op jit(solution)/shard_map/ppermute | solution.py:238
  150.4 4.0 %collective-permute-start.23 = (f32[2,128]{1,0:T(2,128)S(1)}, f32[2,128]{1,0:T(2,128)S(1)}, u32[]{:S(2)}, u32[]{:S(2)}) collective-permute-start(f32[2,128]{1,0:T(2,128)S(1)} %add_add_fusion.1), channel_id=1, source_target_pairs={{0,64},{8,72},{16,80},{24,88},{32,96},{40,104},{48,112},{56,120},{... | collective-permute-start | bytes 3080 | tf_op jit(solution)/shard_map/ppermute | solution.py:216
  156.9 4.1 %close_part.4 = (bf16[384,1536]{1,0:T(8,128)(2,1)}, bf16[384,1536]{1,0:T(8,128)(2,1)}) custom-call(bf16[384,1536]{1,0:T(8,128)(2,1)} %bitcast.43, bf16[4,2,384,128]{3,2,1,0:T(8,128)(2,1)} %get-tuple-element.72.refs_0_, bf16[4,2,384,128]{3,2,1,0:T(8,128)(2,1)} %copy-done.7, ...), custom_call_target="tpu_custom_call", output_to_operand_aliasing={{0}: (5, {}), {1}: (6, {})} | custom-call | flops 4000000000 | bytes 4000000 | tf_op jit(solution)/shard_map/close_part/pallas_call | solution.py:193
  161.1 1.6 collective-permute-done.10.refs_1_
  162.7 7.8 %collective-permute-start.25 = (f32[2,128]{1,0:T(2,128)S(1)}, f32[2,128]{1,0:T(2,128)S(1)}, u32[]{:S(2)}, u32[]{:S(2)}) collective-permute-start(f32[2,128]{1,0:T(2,128)S(1)} %add_add_fusion), channel_id=1, source_target_pairs={{0,128},{8,136},{16,144},{24,152},{32,160},{40,168},{48,176},{56,1... | collective-permute-start | bytes 3080 | tf_op jit(solution)/shard_map/ppermute | solution.py:216
  170.5 4.1 %close_part.5 = (bf16[384,1536]{1,0:T(8,128)(2,1)}, bf16[384,1536]{1,0:T(8,128)(2,1)}) custom-call(bf16[384,1536]{1,0:T(8,128)(2,1)} %bitcast.44, bf16[4,2,384,128]{3,2,1,0:T(8,128)(2,1)} %get-tuple-element.68.refs_0_, bf16[4,2,384,128]{3,2,1,0:T(8,128)(2,1)} %copy-done.9, ...), custom_call_target="tpu_custom_call", output_to_operand_aliasing={{0}: (5, {}), {1}: (6, {})} | custom-call | flops 4000000000 | bytes 4000000 | tf_op jit(solution)/shard_map/close_part/pallas_call | solution.py:193
  (70 shorter events, 17.2 us)
Async XLA Ops:
  2.5 30.5 %copy-start.1 = (bf16[1,384,1536]{2,1,0:T(8,128)(2,1)S(1)}, bf16[1,384,1536]{2,1,0:T(8,128)(2,1)}, u32[]{:S(2)}) copy-start(bf16[1,384,1536]{2,1,0:T(8,128)(2,1)} %param.8) | copy-start | bytes 3538948
  3.4 28.8 %copy-start.5 = (f32[128]{0:T(128)S(1)}, f32[128]{0:T(128)}, u32[]{:S(2)}) copy-start(f32[128]{0:T(128)} %param.10) | copy-start | bytes 1540
  3.4 29.5 %copy-start = (bf16[1,384,1536]{2,1,0:T(8,128)(2,1)S(1)}, bf16[1,384,1536]{2,1,0:T(8,128)(2,1)}, u32[]{:S(2)}) copy-start(bf16[1,384,1536]{2,1,0:T(8,128)(2,1)} %param.9) | copy-start | bytes 3538948
  3.4 21.6 %collective-permute-start = (bf16[2,384,512]{2,1,0:T(8,128)(2,1)}, bf16[2,384,512]{2,1,0:T(8,128)(2,1)}, u32[]{:S(2)}, u32[]{:S(2)}) collective-permute-start(bf16[2,384,512]{2,1,0:T(8,128)(2,1)} %pad_maximum_fusion.2), channel_id=1, source_target_pairs={{0,8},{8,0},{16,24},{32,40},{40,32},{48,56},{64,72},{72,64},{80,88... | collective-permute-start | bytes 2359304 | tf_op jit(solution)/shard_map/ppermute | solution.py:238
  7.1 26.2 %collective-permute-start.3 = (bf16[2,384,512]{2,1,0:T(8,128)(2,1)}, bf16[2,384,512]{2,1,0:T(8,128)(2,1)}, u32[]{:S(2)}, u32[]{:S(2)}) collective-permute-start(bf16[2,384,512]{2,1,0:T(8,128)(2,1)} %pad_maximum_fusion.2), channel_id=1, source_target_pairs={{0,32},{8,40},{16,48},{24,56},{32,64},{40,72},{48,80},{56,88},{64,... | collective-permute-start | bytes 2359304 | tf_op jit(solution)/shard_map/ppermute | solution.py:241
  25.1 20.6 %collective-permute-start.1 = (bf16[2,384,512]{2,1,0:T(8,128)(2,1)}, bf16[2,384,512]{2,1,0:T(8,128)(2,1)}, u32[]{:S(2)}, u32[]{:S(2)}) collective-permute-start(bf16[2,384,512]{2,1,0:T(8,128)(2,1)} %pad_maximum_fusion.1), channel_id=1, source_target_pairs={{0,8},{8,0},{16,24},{32,40},{40,32},{48,56},{64,72},{72,64},{80,88... | collective-permute-start | bytes 2359304 | tf_op jit(solution)/shard_map/ppermute | solution.py:238
  28.5 23.4 %collective-permute-start.2 = (bf16[2,384,512]{2,1,0:T(8,128)(2,1)}, bf16[2,384,512]{2,1,0:T(8,128)(2,1)}, u32[]{:S(2)}, u32[]{:S(2)}) collective-permute-start(bf16[2,384,512]{2,1,0:T(8,128)(2,1)} %collective-permute-done.kv1), channel_id=1, source_target_pairs={{8,16},{0,24},{40,48},{32,56},{72,80},{64,88},{104,112},{96,120},{... | collective-permute-start | bytes 2359304 | tf_op jit(solution)/shard_map/ppermute | solution.py:238
  33.3 40.7 %collective-permute-start.7 = (bf16[2,384,1024]{2,1,0:T(8,128)(2,1)S(1)}, bf16[2,384,1024]{2,1,0:T(8,128)(2,1)}, u32[]{:S(2)}, u32[]{:S(2)}) collective-permute-start(bf16[2,384,1024]{2,1,0:T(8,128)(2,1)S(1)} %pad_maximum_fusion), channel_id=1, source_target_pairs={{0,32},{8,40},{16,48},{24,56},{32,64},{40,72},{48,80},{56,88},{64,... | collective-permute-start | bytes 4718600 | tf_op jit(solution)/shard_map/ppermute | solution.py:241
  45.7 22.2 %collective-permute-start.5 = (bf16[2,384,512]{2,1,0:T(8,128)(2,1)S(1)}, bf16[2,384,512]{2,1,0:T(8,128)(2,1)S(1)}, u32[]{:S(2)}, u32[]{:S(2)}) collective-permute-start(bf16[2,384,512]{2,1,0:T(8,128)(2,1)S(1)} %pad_maximum_fusion.3), channel_id=1, source_target_pairs={{0,8},{8,0},{16,24},{32,40},{40,32},{48,56},{64,72},{72,64},{80,88... | collective-permute-start | bytes 2359304 | tf_op jit(solution)/shard_map/ppermute | solution.py:238
  49.1 24.8 %collective-permute-start.6 = (bf16[2,384,512]{2,1,0:T(8,128)(2,1)}, bf16[2,384,512]{2,1,0:T(8,128)(2,1)S(1)}, u32[]{:S(2)}, u32[]{:S(2)}) collective-permute-start(bf16[2,384,512]{2,1,0:T(8,128)(2,1)} %collective-permute-done.1.kv1), channel_id=1, source_target_pairs={{8,16},{0,24},{40,48},{32,56},{72,80},{64,88},{104,112},{96,120},{... | collective-permute-start | bytes 2359304 | tf_op jit(solution)/shard_map/ppermute | solution.py:238
  66.6 23.1 %collective-permute-start.4 = (bf16[4,2,384,128]{3,2,1,0:T(8,128)(2,1)}, bf16[4,2,384,128]{3,2,1,0:T(8,128)(2,1)S(1)}, u32[]{:S(2)}, u32[]{:S(2)}) collective-permute-start(bf16[4,2,384,128]{3,2,1,0:T(8,128)(2,1)} %get-tuple-element.51), channel_id=1, source_target_pairs={{24,0},{16,8},{56,32},{48,40},{88,64},{80,72},{120,96},{112,104},{... | collective-permute-start | bytes 2359304 | tf_op jit(solution)/shard_map/ppermute | solution.py:238
  67.9 21.8 %copy-start.8 = (bf16[2,384,512]{2,1,0:T(8,128)(2,1)}, bf16[2,384,512]{2,1,0:T(8,128)(2,1)S(1)}, u32[]{:S(2)}) copy-start(bf16[2,384,512]{2,1,0:T(8,128)(2,1)S(1)} %collective-permute-done.5.kv1) | copy-start | bytes 2359300
  67.9 24.9 %collective-permute-start.8 = (bf16[2,384,512]{2,1,0:T(8,128)(2,1)S(1)}, bf16[2,384,512]{2,1,0:T(8,128)(2,1)S(1)}, u32[]{:S(2)}, u32[]{:S(2)}) collective-permute-start(bf16[2,384,512]{2,1,0:T(8,128)(2,1)S(1)} %collective-permute-done.5.kv1), channel_id=1, source_target_pairs={{8,16},{0,24},{40,48},{32,56},{72,80},{64,88},{104,112},{96,120},{... | collective-permute-start | bytes 2359304 | tf_op jit(solution)/shard_map/ppermute | solution.py:238
  74.9 14.9 %copy-start.4 = (bf16[4,2,384,128]{3,2,1,0:T(8,128)(2,1)S(1)}, bf16[4,2,384,128]{3,2,1,0:T(8,128)(2,1)}, u32[]{:S(2)}) copy-start(bf16[4,2,384,128]{3,2,1,0:T(8,128)(2,1)} %get-tuple-element.50) | copy-start | bytes 2359300
  89.9 24.4 %collective-permute-start.12 = (bf16[4,2,384,128]{3,2,1,0:T(8,128)(2,1)}, bf16[4,2,384,128]{3,2,1,0:T(8,128)(2,1)S(1)}, u32[]{:S(2)}, u32[]{:S(2)}) collective-permute-start(bf16[4,2,384,128]{3,2,1,0:T(8,128)(2,1)} %get-tuple-element.74), channel_id=1, source_target_pairs={{24,0},{16,8},{56,32},{48,40},{88,64},{80,72},{120,96},{112,104},{... | collective-permute-start | bytes 2359304 | tf_op jit(solution)/shard_map/ppermute | solution.py:238
  91.2 42.7 %collective-permute-start.14 = (bf16[8,2,384,128]{3,2,1,0:T(8,128)(2,1)}, bf16[8,2,384,128]{3,2,1,0:T(8,128)(2,1)}, u32[]{:S(2)}, u32[]{:S(2)}) collective-permute-start(bf16[8,2,384,128]{3,2,1,0:T(8,128)(2,1)} %get-tuple-element.77), channel_id=1, source_target_pairs={{32,0},{40,8},{48,16},{56,24},{64,32},{72,40},{80,48},{88,56},{96,... | collective-permute-start | bytes 4718600 | tf_op jit(solution)/shard_map/ppermute | solution.py:241
  93.7 20.7 %copy-start.3 = (bf16[4,2,384,128]{3,2,1,0:T(8,128)(2,1)S(1)}, bf16[4,2,384,128]{3,2,1,0:T(8,128)(2,1)}, u32[]{:S(2)}) copy-start(bf16[4,2,384,128]{3,2,1,0:T(8,128)(2,1)} %get-tuple-element.73) | copy-start | bytes 2359300
  108.5 20.0 %collective-permute-start.9 = (bf16[4,2,384,128]{3,2,1,0:T(8,128)(2,1)}, bf16[4,2,384,128]{3,2,1,0:T(8,128)(2,1)S(1)}, u32[]{:S(2)}, u32[]{:S(2)}) collective-permute-start(bf16[4,2,384,128]{3,2,1,0:T(8,128)(2,1)} %get-tuple-element.70), channel_id=1, source_target_pairs={{24,0},{16,8},{56,32},{48,40},{88,64},{80,72},{120,96},{112,104},{... | collective-permute-start | bytes 2359304 | tf_op jit(solution)/shard_map/ppermute | solution.py:238
  109.8 22.5 %collective-permute-start.15 = (bf16[4,2,384,128]{3,2,1,0:T(8,128)(2,1)S(1)}, bf16[4,2,384,128]{3,2,1,0:T(8,128)(2,1)}, u32[]{:S(2)}, u32[]{:S(2)}) collective-permute-start(bf16[4,2,384,128]{3,2,1,0:T(8,128)(2,1)S(1)} %add_convert_fusion.2), channel_id=1, source_target_pairs={{0,8},{8,0},{24,16},{32,40},{40,32},{56,48},{64,72},{72,64},{88,80... | collective-permute-start | bytes 2359304 | tf_op jit(solution)/shard_map/ppermute | solution.py:238
  114.6 1.2 collective-permute-start.16
  115.8 3.6 %collective-permute-start.17 = (f32[2,128]{1,0:T(2,128)S(1)}, f32[2,128]{1,0:T(2,128)S(1)}, u32[]{:S(2)}, u32[]{:S(2)}) collective-permute-start(f32[2,128]{1,0:T(2,128)S(1)} %add.42), channel_id=1, source_target_pairs={{0,2},{1,3},{2,0},{3,1},{4,6},{5,7},{6,4},{7,5},{8,10},{9,11},{10,... | collective-permute-start | bytes 3080 | tf_op jit(solution)/shard_map/ppermute | solution.py:216
  119.4 5.1 %collective-permute-start.18 = (f32[2,128]{1,0:T(2,128)S(1)}, f32[2,128]{1,0:T(2,128)S(1)}, u32[]{:S(2)}, u32[]{:S(2)}) collective-permute-start(f32[2,128]{1,0:T(2,128)S(1)} %add.43), channel_id=1, source_target_pairs={{0,4},{1,5},{2,6},{3,7},{4,0},{5,1},{6,2},{7,3},{8,12},{9,13},{10,... | collective-permute-start | bytes 3080 | tf_op jit(solution)/shard_map/ppermute | solution.py:216
  119.9 36.1 %collective-permute-start.13 = (bf16[4,2,384,128]{3,2,1,0:T(8,128)(2,1)S(1)}, bf16[4,2,384,128]{3,2,1,0:T(8,128)(2,1)S(1)}, u32[]{:S(2)}, u32[]{:S(2)}) collective-permute-start(bf16[4,2,384,128]{3,2,1,0:T(8,128)(2,1)S(1)} %add_convert_fusion), channel_id=1, source_target_pairs={{0,8},{8,0},{24,16},{32,40},{40,32},{56,48},{64,72},{72,64},{88,80... | collective-permute-start | bytes 2359304 | tf_op jit(solution)/shard_map/ppermute | solution.py:238
  124.5 25.9 %collective-permute-start.11 = (bf16[4,2,384,128]{3,2,1,0:T(8,128)(2,1)}, bf16[4,2,384,128]{3,2,1,0:T(8,128)(2,1)S(1)}, u32[]{:S(2)}, u32[]{:S(2)}) collective-permute-start(bf16[4,2,384,128]{3,2,1,0:T(8,128)(2,1)} %get-tuple-element.71), channel_id=1, source_target_pairs={{32,0},{40,8},{48,16},{56,24},{64,32},{72,40},{80,48},{88,56},{96,... | collective-permute-start | bytes 2359304 | tf_op jit(solution)/shard_map/ppermute | solution.py:241
  128.7 14.6 %collective-permute-start.20 = (f32[2,128]{1,0:T(2,128)S(1)}, f32[2,128]{1,0:T(2,128)S(1)}, u32[]{:S(2)}, u32[]{:S(2)}) collective-permute-start(f32[2,128]{1,0:T(2,128)S(1)} %add.44), channel_id=1, source_target_pairs={{0,16},{8,24},{16,0},{24,8},{32,48},{40,56},{48,32},{56,40},{64,80... | collective-permute-start | bytes 3080 | tf_op jit(solution)/shard_map/ppermute | solution.py:216
  132.3 18.1 %collective-permute-start.21 = (f32[2,128]{1,0:T(2,128)S(1)}, f32[2,128]{1,0:T(2,128)S(1)}, u32[]{:S(2)}, u32[]{:S(2)}) collective-permute-start(f32[2,128]{1,0:T(2,128)S(1)} %add.44), channel_id=1, source_target_pairs={{0,24},{8,16},{16,8},{24,0},{32,56},{40,48},{48,40},{56,32},{64,88... | collective-permute-start | bytes 3080 | tf_op jit(solution)/shard_map/ppermute | solution.py:216
  133.9 16.5 %collective-permute-start.19 = (f32[2,128]{1,0:T(2,128)S(1)}, f32[2,128]{1,0:T(2,128)S(1)}, u32[]{:S(2)}, u32[]{:S(2)}) collective-permute-start(f32[2,128]{1,0:T(2,128)S(1)} %add.44), channel_id=1, source_target_pairs={{0,8},{8,0},{16,24},{24,16},{32,40},{40,32},{48,56},{56,48},{64,72... | collective-permute-start | bytes 3080 | tf_op jit(solution)/shard_map/ppermute | solution.py:216
  143.4 19.4 %collective-permute-start.10 = (bf16[4,2,384,128]{3,2,1,0:T(8,128)(2,1)S(1)}, bf16[4,2,384,128]{3,2,1,0:T(8,128)(2,1)S(1)}, u32[]{:S(2)}, u32[]{:S(2)}) collective-permute-start(bf16[4,2,384,128]{3,2,1,0:T(8,128)(2,1)S(1)} %add_convert_fusion.1), channel_id=1, source_target_pairs={{0,8},{8,0},{24,16},{32,40},{40,32},{56,48},{64,72},{72,64},{88,80... | collective-permute-start | bytes 2359304 | tf_op jit(solution)/shard_map/ppermute | solution.py:238
  150.4 10.6 %collective-permute-start.23 = (f32[2,128]{1,0:T(2,128)S(1)}, f32[2,128]{1,0:T(2,128)S(1)}, u32[]{:S(2)}, u32[]{:S(2)}) collective-permute-start(f32[2,128]{1,0:T(2,128)S(1)} %add_add_fusion.1), channel_id=1, source_target_pairs={{0,64},{8,72},{16,80},{24,88},{32,96},{40,104},{48,112},{56,120},{... | collective-permute-start | bytes 3080 | tf_op jit(solution)/shard_map/ppermute | solution.py:216
  154.4 6.7 %collective-permute-start.24 = (f32[2,128]{1,0:T(2,128)S(1)}, f32[2,128]{1,0:T(2,128)S(1)}, u32[]{:S(2)}, u32[]{:S(2)}) collective-permute-start(f32[2,128]{1,0:T(2,128)S(1)} %add_add_fusion.1), channel_id=1, source_target_pairs={{0,96},{8,104},{16,112},{24,120},{32,64},{40,72},{48,80},{56,88},{... | collective-permute-start | bytes 3080 | tf_op jit(solution)/shard_map/ppermute | solution.py:216
  155.6 5.5 %collective-permute-start.22 = (f32[2,128]{1,0:T(2,128)S(1)}, f32[2,128]{1,0:T(2,128)S(1)}, u32[]{:S(2)}, u32[]{:S(2)}) collective-permute-start(f32[2,128]{1,0:T(2,128)S(1)} %add_add_fusion.1), channel_id=1, source_target_pairs={{0,32},{8,40},{16,48},{24,56},{32,0},{40,8},{48,16},{56,24},{64,96... | collective-permute-start | bytes 3080 | tf_op jit(solution)/shard_map/ppermute | solution.py:216
  162.7 11.9 %collective-permute-start.25 = (f32[2,128]{1,0:T(2,128)S(1)}, f32[2,128]{1,0:T(2,128)S(1)}, u32[]{:S(2)}, u32[]{:S(2)}) collective-permute-start(f32[2,128]{1,0:T(2,128)S(1)} %add_add_fusion), channel_id=1, source_target_pairs={{0,128},{8,136},{16,144},{24,152},{32,160},{40,168},{48,176},{56,1... | collective-permute-start | bytes 3080 | tf_op jit(solution)/shard_map/ppermute | solution.py:216
  (6 other events, 35.3 us)
